TPU v7x, 32 devices: a whole 2x2x4 slice. The times are simulated.
32 devices in a mesh: seq: 4 (over x, core), fsdp: 8 (over z, y).
Axes of the slice: x: 2, y: 2, z: 4, core: 2. Of those that a mesh axis runs over, the one named last changes fastest.
Arguments:
- tokens: bfloat16 [8, 1024, 1536], P('fsdp', 'seq'), may hold values from -6 to 6
- segment_ids: int32 [8, 1024], P('fsdp'), may hold values from 0 to 2, as said below
- attn_gain: bfloat16 [1536], P('fsdp'), may hold values from 0.5 to 1.5
- qkv_weight: bfloat16 [1536, 2048], P('fsdp'), may hold values from -0.15625 to 0.15625
- qkv_bias: bfloat16 [2048], P('fsdp'), may hold values from -3 to 3
- proj_weight: bfloat16 [1536, 1536], P('fsdp'), may hold values from -1.25 to 1.25
- mlp_gain: bfloat16 [1536], P('fsdp'), may hold values from 0.5 to 1.5
- gate_up_weight: bfloat16 [1536, 17920], P('fsdp'), may hold values from -0.15625 to 0.15625
- down_weight: bfloat16 [8960, 1536], P('fsdp'), may hold values from -0.0625 to 0.0625
- cotangent: bfloat16 [8, 1024, 1536], P('fsdp', 'seq'), may hold values from -6 to 6
Outputs:
- block_out: bfloat16 [8, 1024, 1536], P('fsdp', 'seq')
- tokens_grad: float32 [8, 1024, 1536], P('fsdp', 'seq')
- attn_gain_grad: float32 [1536], P('fsdp')
- qkv_weight_grad: float32 [1536, 2048], P('fsdp')
- qkv_bias_grad: float32 [2048], P('fsdp')
- proj_weight_grad: float32 [1536, 1536], P('fsdp')
- mlp_gain_grad: float32 [1536], P('fsdp')
- gate_up_weight_grad: float32 [1536, 17920], P('fsdp')
- down_weight_grad: float32 [8960, 1536], P('fsdp')
Inputs may be any that keep to these rules, and one draw needn't show every extreme that they name: `segment_ids`: each row is one sequence holding three documents in order: segment ids never fall along a row, each of 0, 1 and 2 occurs, and the first and the last document have at most 128 tokens each.
All inputs are finite; a program needn't handle non-finite values.
Results may differ from a plain program's by a relative error of at most 0.013.
Values may be sent and summed in bfloat16 or wider, within the bound.
A program may use at most 448 MiB of HBM per device.

v0:
```python
import jax
import jax.numpy as jnp
from jax import lax
from jax.sharding import PartitionSpec as P

H = 12
KV = 2
HD = 128
FF = 8960


EPSILON = 1e-06
THETA = 1000000.0
FLOOR = -1e30


def inverse_rms(value):
    return lax.rsqrt(jnp.mean(value * value, axis=-1, keepdims=True) + EPSILON)


def turned(value):
    halfway = value.shape[-1] // 2
    return jnp.concatenate([-value[..., halfway:], value[..., :halfway]], axis=-1)


def turned_back(value):
    halfway = value.shape[-1] // 2
    return jnp.concatenate([value[..., halfway:], -value[..., :halfway]], axis=-1)


def norm_back(value, factor, gain, upstream):
    weighted = upstream * gain
    gain_term = jnp.sum(upstream * value * factor, axis=0)
    through = factor * weighted - value * factor**3 * jnp.mean(
        weighted * value, axis=-1, keepdims=True
    )
    return (through, gain_term)


def column_product(left, right):
    return lax.dot_general(
        left, right, (((0,), (0,)), ((), ())), preferred_element_type=jnp.float32
    )


def times_transpose(left, right):
    return lax.dot_general(
        left, right, (((1,), (1,)), ((), ())), preferred_element_type=jnp.float32
    )


def fsdp_reduce(term_fn, owned_rows):
    return lax.psum_scatter(
        term_fn(jnp.int32(0), lax.axis_size("fsdp") * owned_rows),
        "fsdp",
        scatter_dimension=0,
        tiled=True,
    )


def local(
    tokens,
    segment_ids,
    attn_gain,
    qkv_weight,
    qkv_bias,
    proj_weight,
    mlp_gain,
    gate_up_weight,
    down_weight,
    cotangent,
):
    seq_count = lax.axis_size("seq")
    tok_rows = tokens.shape[1]
    seq_len = tok_rows * seq_count
    per_dev = H // seq_count
    copies = seq_count // KV
    head_cols = per_dev * HD
    score_scale = HD ** (-0.5)
    block_rows = min(512, seq_len)
    blocks = seq_len // block_rows
    segment_row = segment_ids[0]
    own_first = lax.axis_index("seq") * tok_rows
    own_index = own_first + jnp.arange(tok_rows, dtype=jnp.int32)
    own_segments = lax.dynamic_slice_in_dim(segment_row, own_first, tok_rows)
    doc_starts = jnp.sum((segment_row[None, :] < own_segments[:, None]).astype(jnp.int32), axis=1)
    places = own_index - doc_starts
    inverse = THETA ** (-2.0 * jnp.arange(HD // 2, dtype=jnp.float32) / HD)
    angles = places.astype(jnp.float32)[:, None] * inverse[None, :]
    angles = jnp.concatenate([angles, angles], axis=-1)
    cosines = jnp.cos(angles)[:, None, :]
    sines = jnp.sin(angles)[:, None, :]
    resid = tokens[0].astype(jnp.float32)
    attn_front = (
        lax.all_gather(attn_gain, "fsdp", axis=0, tiled=True),
        lax.all_gather(qkv_weight, "fsdp", axis=0, tiled=True),
        lax.all_gather(qkv_bias, "fsdp", axis=0, tiled=True),
        lax.all_gather(proj_weight, "fsdp", axis=0, tiled=True),
    )
    factor_one = inverse_rms(resid)
    normed_in = (resid * factor_one * attn_front[0].astype(jnp.float32)).astype(jnp.bfloat16)
    projected = jnp.dot(normed_in, attn_front[1], preferred_element_type=jnp.float32) + attn_front[
        2
    ].astype(jnp.float32)
    queries = projected[:, : H * HD].reshape(tok_rows, H, HD)
    key_heads = projected[:, H * HD : (H + KV) * HD].reshape(tok_rows, KV, HD)
    value_heads = projected[:, (H + KV) * HD :].reshape(tok_rows, KV, HD).astype(jnp.bfloat16)
    queries = (queries * cosines + turned(queries) * sines).astype(jnp.bfloat16)
    key_heads = (key_heads * cosines + turned(key_heads) * sines).astype(jnp.bfloat16)
    packed = jnp.concatenate(
        [
            queries.reshape(tok_rows, seq_count, head_cols),
            jnp.repeat(key_heads, copies, axis=1),
            jnp.repeat(value_heads, copies, axis=1),
        ],
        axis=-1,
    )
    arrived = lax.all_to_all(packed, "seq", split_axis=1, concat_axis=0, tiled=True)[:, 0, :]
    head_queries = arrived[:, :head_cols].reshape(blocks, block_rows, per_dev, HD)
    head_keys = arrived[:, head_cols : head_cols + HD]
    head_values = arrived[:, head_cols + HD :]
    key_index = jnp.arange(seq_len, dtype=jnp.int32)
    block_starts = jnp.arange(blocks, dtype=jnp.int32) * block_rows

    def scores_of(query_block, first_row):
        row_index = first_row + jnp.arange(block_rows, dtype=jnp.int32)
        row_segments = lax.dynamic_slice_in_dim(segment_row, first_row, block_rows)
        allowed = (key_index[None, :] <= row_index[:, None]) & (
            segment_row[None, :] == row_segments[:, None]
        )
        scores = (
            jnp.einsum("qhd,kd->hqk", query_block, head_keys, preferred_element_type=jnp.float32)
            * score_scale
        )
        return (jnp.where(allowed[None], scores, FLOOR), allowed)

    def attend(element):
        query_block, first_row = element
        scores, allowed = scores_of(query_block, first_row)
        highest = jnp.max(scores, axis=-1, keepdims=True)
        exponent = jnp.exp(scores - highest)
        row_total = jnp.sum(exponent, axis=-1, keepdims=True)
        weights = (exponent / row_total).astype(jnp.bfloat16)
        mixture = jnp.einsum(
            "hqk,kd->qhd", weights, head_values, preferred_element_type=jnp.float32
        )
        return (
            mixture.astype(jnp.bfloat16).reshape(block_rows, head_cols),
            (highest + jnp.log(row_total))[..., 0],
        )

    head_out, logsum = lax.map(attend, (head_queries, block_starts))
    merged = lax.all_to_all(
        head_out.reshape(seq_len, head_cols), "seq", split_axis=0, concat_axis=1, tiled=True
    )
    attended = jnp.dot(merged, attn_front[3], preferred_element_type=jnp.float32)
    hidden_in = resid + attended
    factor_two = inverse_rms(hidden_in)
    gain_two, gate_up_all, down_all = (
        lax.all_gather(mlp_gain, "fsdp", axis=0, tiled=True),
        lax.all_gather(gate_up_weight, "fsdp", axis=0, tiled=True),
        lax.all_gather(down_weight, "fsdp", axis=0, tiled=True),
    )
    normed_mid = (hidden_in * factor_two * gain_two.astype(jnp.float32)).astype(jnp.bfloat16)
    gate_up = jnp.dot(normed_mid, gate_up_all, preferred_element_type=jnp.float32)
    gain_two = gain_two.astype(jnp.float32)
    gate_part = gate_up[:, :FF]
    upward = gate_up[:, FF:]
    sigmoid_gate = jax.nn.sigmoid(gate_part)
    activated = (gate_part * sigmoid_gate * upward).astype(jnp.bfloat16)
    block_out = (
        hidden_in + jnp.dot(activated, down_all, preferred_element_type=jnp.float32)
    ).astype(jnp.bfloat16)
    upstream = cotangent[0].astype(jnp.float32)
    grad_branch = cotangent[0]
    grad_act = times_transpose(grad_branch, down_all)
    grad_gate = grad_act * upward * sigmoid_gate * (1.0 + gate_part * (1.0 - sigmoid_gate))
    grad_up = grad_act * gate_part * sigmoid_gate
    grad_gate_up = jnp.concatenate([grad_gate, grad_up], axis=-1).astype(jnp.bfloat16)
    grad_mid = times_transpose(grad_gate_up, gate_up_all)
    through_two, gain_two_term = norm_back(hidden_in, factor_two, gain_two, grad_mid)
    grad_hidden = upstream + through_two
    attn_back = (attn_front[0], attn_front[1], attn_front[3])
    grad_attended = grad_hidden.astype(jnp.bfloat16)
    grad_merged = times_transpose(grad_attended, attn_back[2]).astype(jnp.bfloat16)
    grad_heads = lax.all_to_all(
        grad_merged, "seq", split_axis=1, concat_axis=0, tiled=True
    ).reshape(blocks, block_rows, per_dev, HD)

    def attend_back(carry, element):
        query_block, grad_block, logsum_block, first_row = element
        scores, allowed = scores_of(query_block, first_row)
        probs = jnp.where(allowed[None], jnp.exp(scores - logsum_block[..., None]), 0.0)
        grad_probs = jnp.einsum(
            "qhd,kd->hqk", grad_block, head_values, preferred_element_type=jnp.float32
        )
        inner = jnp.sum(probs * grad_probs, axis=-1, keepdims=True)
        grad_scores = (probs * (grad_probs - inner)).astype(jnp.bfloat16)
        grad_query = (
            jnp.einsum("hqk,kd->qhd", grad_scores, head_keys, preferred_element_type=jnp.float32)
            * score_scale
        )
        grad_key = (
            carry[0]
            + jnp.einsum(
                "hqk,qhd->kd", grad_scores, query_block, preferred_element_type=jnp.float32
            )
            * score_scale
        )
        grad_value = carry[1] + jnp.einsum(
            "hqk,qhd->kd",
            probs.astype(jnp.bfloat16),
            grad_block,
            preferred_element_type=jnp.float32,
        )
        return (
            (grad_key, grad_value),
            grad_query.astype(jnp.bfloat16).reshape(block_rows, head_cols),
        )

    initial = (jnp.zeros((seq_len, HD), jnp.float32), jnp.zeros((seq_len, HD), jnp.float32))
    (grad_key, grad_value), grad_query = lax.scan(
        attend_back, initial, (head_queries, grad_heads, logsum, block_starts)
    )
    sent_back = jnp.concatenate(
        [
            grad_query.reshape(seq_len, head_cols),
            grad_key.astype(jnp.bfloat16),
            grad_value.astype(jnp.bfloat16),
        ],
        axis=-1,
    )[:, None, :]
    returned = lax.all_to_all(sent_back, "seq", split_axis=0, concat_axis=1, tiled=True)
    grad_q_rot = returned[:, :, :head_cols].reshape(tok_rows, H, HD).astype(jnp.float32)
    grad_k_rot = (
        returned[:, :, head_cols : head_cols + HD]
        .astype(jnp.float32)
        .reshape(tok_rows, KV, copies, HD)
        .sum(axis=2)
    )
    grad_v = (
        returned[:, :, head_cols + HD :]
        .astype(jnp.float32)
        .reshape(tok_rows, KV, copies, HD)
        .sum(axis=2)
    )
    grad_q = grad_q_rot * cosines + turned_back(grad_q_rot * sines)
    grad_k = grad_k_rot * cosines + turned_back(grad_k_rot * sines)
    grad_projected = jnp.concatenate(
        [
            grad_q.reshape(tok_rows, H * HD),
            grad_k.reshape(tok_rows, KV * HD),
            grad_v.reshape(tok_rows, KV * HD),
        ],
        axis=-1,
    ).astype(jnp.bfloat16)
    bias_term = jnp.sum(grad_projected.astype(jnp.float32), axis=0)
    grad_in = times_transpose(grad_projected, attn_back[1])
    through_one, gain_one_term = norm_back(
        resid, factor_one, attn_back[0].astype(jnp.float32), grad_in
    )
    tokens_grad = grad_hidden + through_one
    vectors = (
        lax.psum_scatter(gain_one_term, "fsdp", scatter_dimension=0, tiled=True),
        lax.psum_scatter(bias_term, "fsdp", scatter_dimension=0, tiled=True),
        lax.psum_scatter(gain_two_term, "fsdp", scatter_dimension=0, tiled=True),
    )
    owned_width = attn_gain.shape[0]
    owned_hidden = down_weight.shape[0]

    def attn_term(first_col, width):
        return jnp.concatenate(
            [column_product(normed_in, grad_projected), column_product(merged, grad_attended)],
            axis=1,
        )

    def gate_up_term(first_col, width):
        return column_product(normed_mid, grad_gate_up)

    def down_term(first_col, width):
        return column_product(activated, grad_branch)

    attn_grad = fsdp_reduce(attn_term, owned_width)
    gate_up_grad = fsdp_reduce(gate_up_term, owned_width)
    down_grad = fsdp_reduce(down_term, owned_hidden)
    summed = lax.psum(
        (vectors[0], attn_grad, vectors[1], vectors[2], gate_up_grad, down_grad), "seq"
    )
    qkv_cols = qkv_weight.shape[1]
    return (
        block_out[None],
        tokens_grad[None],
        summed[0],
        summed[1][:, :qkv_cols],
        summed[2],
        summed[1][:, qkv_cols:],
        summed[3],
        summed[4],
        summed[5],
    )


def solution(mesh):
    in_specs = (
        P("fsdp", "seq", None),
        P("fsdp", None),
        P("fsdp"),
        P("fsdp", None),
        P("fsdp"),
        P("fsdp", None),
        P("fsdp"),
        P("fsdp", None),
        P("fsdp", None),
        P("fsdp", "seq", None),
    )
    out_specs = (
        P("fsdp", "seq", None),
        P("fsdp", "seq", None),
        P("fsdp"),
        P("fsdp", None),
        P("fsdp"),
        P("fsdp", None),
        P("fsdp"),
        P("fsdp", None),
        P("fsdp", None),
    )
    return jax.shard_map(local, mesh=mesh, in_specs=in_specs, out_specs=out_specs, check_vma=False)
```

profile of v0, /device:TPU:0, one launch (start us, length us, event | category | flops | bytes accessed | tf_op | source)
XLA Modules:
  0.0 5267.0 jit_solution(17969465940307159752)
XLA Ops:
  10.1 22.5 all-gather
  34.4 18.2 all-reduce.8
  55.3 57.4 %all-gather.6.cloned.1.call-done = bf16[1536,2048]{1,0:T(8,128)(2,1)} async-done(((bf16[192,2048]{1,0:T(8,128)(2,1)}), bf16[1536,2048]{1,0:T(8,128)(2,1)}) %all-gather.6.cloned.1.call-update) | async-done | bytes 6291472 | tf_op jit(solution)/shard_map/all_gather | solution.py:96
  129.2 17.2 all-to-all-done
  154.0 23.2 while.28
  181.2 11.6 all-to-all-done.1
  197.2 1036.3 %all-gather.10.cloned.1.call-done = bf16[1536,17920]{1,0:T(8,128)(2,1)} async-done(((bf16[192,17920]{1,0:T(8,128)(2,1)}), bf16[1536,17920]{1,0:T(8,128)(2,1)}) %all-gather.10.cloned.1.call-update) | async-done | bytes 55050256 | tf_op jit(solution)/shard_map/all_gather | solution.py:161
  1233.5 29.4 fusion.83
  1262.9 496.7 %all-gather.12.cloned.1.call-done = bf16[8960,1536]{1,0:T(8,128)(2,1)} async-done(((bf16[1120,1536]{1,0:T(8,128)(2,1)}), bf16[8960,1536]{1,0:T(8,128)(2,1)}) %all-gather.12.cloned.1.call-update) | async-done | bytes 27525136 | tf_op jit(solution)/shard_map/all_gather | solution.py:162
  1759.5 21.5 multiply_convert_fusion.1
  1781.1 25.6 multiply_reduce_fusion
  1819.2 10.7 all-to-all-done.2
  1833.7 58.6 %while.29 = (s32[]{:T(128)}, f32[1024,128]{1,0:T(8,128)}, f32[1024,128]{1,0:T(8,128)}, bf16[2,512,384]{2,1,0:T(8,128)(2,1)}, s32[2]{0:T(128)S(1)}, /*index=5*/s3...) while((s32[]{:T(128)}, f32[1024,128]{1,0:T(8,128)}, ...), condition=%wide.region_10.11_spmd.clone, body=%wide.region_8.10_spmd.clone.sunk | while | flops 2031614976 | bytes 103463280 | solution.py:222
  1833.7 4.7 fusion.134
  1842.2 6.1 fusion.136
  1863.0 4.7 fusion.134
  1871.4 6.1 fusion.136
  1906.9 5.1 fusion.70
  1912.1 11.9 all-to-all-done.3
  1933.2 7.9 pad_maximum_fusion
  1942.2 22.7 fusion.66
  1966.3 41.8 fusion.50
  2008.4 289.8 %reduce-scatter.4.cloned.1.call-done = f32[192,3584]{1,0:T(8,128)} async-done(((f32[1536,3584]{1,0:T(8,128)}), f32[192,3584]{1,0:T(8,128)}) %reduce-scatter.4.cloned.1.call-update) | async-done | bytes 2752528 | tf_op jit(solution)/shard_map/reduce_scatter | solution.py:53
  2298.2 862.0 %reduce-scatter.8.cloned.1.call-done = f32[1120,1536]{1,0:T(8,128)} async-done(((f32[8960,1536]{1,0:T(8,128)}), f32[1120,1536]{1,0:T(8,128)}) %reduce-scatter.8.cloned.1.call-update) | async-done | bytes 6881296 | tf_op jit(solution)/shard_map/reduce_scatter | solution.py:53
  3160.2 1678.9 %reduce-scatter.6.cloned.1.call-done = f32[192,17920]{1,0:T(8,128)} async-done(((f32[1536,17920]{1,0:T(8,128)}), f32[192,17920]{1,0:T(8,128)}) %reduce-scatter.6.cloned.1.call-update) | async-done | bytes 13762576 | tf_op jit(solution)/shard_map/reduce_scatter | solution.py:53
  4840.4 16.2 fusion.53
  4857.0 6.0 fusion.63
  4863.0 35.2 all-reduce.5
  4898.5 7.1 all-reduce.6
  4908.6 328.7 %all-reduce.11.cloned.1.call-done = (f32[192,3584]{1,0:T(8,128)}, f32[192,17920]{1,0:T(8,128)}, f32[1120,1536]{1,0:T(8,128)}) async-done(((f32[192,3584]{1,0:T(8,128)}, f32[192,17920]{1,0:T(8,128)}, f32[1120,1536]{1,0:T(8,128)}), (f32[192,3584]{1,0:T(8,128)}, f32[192,17920]{1,0:T(8,128)}, f32[1120,1536]{1,0:T(8,128)})) %all-reduce.11.cloned.1.call-update) | async-done | bytes 23396368 | tf_op jit(solution)/shard_map/psum | solution.py:286
  5242.4 11.0 copy.214
  5253.3 6.4 copy.215
  (258 shorter events, 142.3 us)
Async XLA Ops:
  7.2 105.5 %all-gather.6.cloned.1.call-start = ((), (), s32[]{:S(2)}) async-start(), calls=%async_computation.7 | async-start | bytes 7077888 | tf_op jit(solution)/shard_map/all_gather | solution.py:96
  7.9 185.2 %all-gather.8.cloned.1.call-start = ((), (), s32[]{:S(2)}) async-start(), calls=%async_computation.8 | async-start | bytes 5308416 | tf_op jit(solution)/shard_map/all_gather | solution.py:98
  8.7 1224.8 %all-gather.10.cloned.1.call-start = ((), (), s32[]{:S(2)}) async-start(), calls=%async_computation.9 | async-start | bytes 61931520 | tf_op jit(solution)/shard_map/all_gather | solution.py:161
  9.4 23.2 copy-start.38
  9.4 24.4 copy-start.40
  9.4 24.7 copy-start.41
  9.4 43.2 copy-start.25
  9.4 45.0 copy-start.12
  9.5 1750.1 %all-gather.12.cloned.1.call-start = ((), (), s32[]{:S(2)}) async-start(), calls=%async_computation.10 | async-start | bytes 30965760 | tf_op jit(solution)/shard_map/all_gather | solution.py:162
  52.6 60.1 %copy-start.32 = (f32[1536]{0:T(1024)}, f32[1536]{0:T(1024)S(1)}, u32[]{:S(2)}) copy-start(f32[1536]{0:T(1024)S(1)} %convert_element_type.107) | copy-start | bytes 18436
  53.6 66.0 %copy-start.17 = (f32[256,128]{1,0:T(8,128)}, f32[256,128]{1,0:T(8,128)S(1)}, u32[]{:S(2)}) copy-start(f32[256,128]{1,0:T(8,128)S(1)} %get-tuple-element.398) | copy-start | bytes 393220
  53.6 66.0 %copy-start.19 = (f32[256,128]{1,0:T(8,128)}, f32[256,128]{1,0:T(8,128)S(1)}, u32[]{:S(2)}) copy-start(f32[256,128]{1,0:T(8,128)S(1)} %get-tuple-element.397) | copy-start | bytes 393220
  53.7 68.9 %copy-start.21 = (f32[256,128]{0,1:T(8,128)}, f32[256,128]{0,1:T(8,128)S(1)}, u32[]{:S(2)}) copy-start(f32[256,128]{0,1:T(8,128)S(1)} %copy.136) | copy-start | bytes 393220
  55.3 57.4 %copy-start.34 = (f32[256]{0:T(256)}, f32[256]{0:T(256)S(1)}, u32[]{:S(2)}) copy-start(f32[256]{0:T(256)S(1)} %get-tuple-element.400) | copy-start | bytes 3076
  125.7 20.8 all-to-all-start
  177.2 15.6 all-to-all-start.1
  181.2 1625.5 %copy-start.26 = (f32[1536]{0:T(1024)}, f32[1536]{0:T(1024)S(1)}, u32[]{:S(2)}) copy-start(f32[1536]{0:T(1024)S(1)} %convert_element_type.115) | copy-start | bytes 18436
  197.2 1609.5 %copy-start.3 = (f32[256,1536]{1,0:T(8,128)}, f32[256,1536]{1,0:T(8,128)S(1)}, u32[]{:S(2)}) copy-start(f32[256,1536]{1,0:T(8,128)S(1)} %get-tuple-element.406) | copy-start | bytes 4718596
  197.2 1609.5 %copy-start.30 = (f32[256]{0:T(256)}, f32[256]{0:T(256)S(1)}, u32[]{:S(2)}) copy-start(f32[256]{0:T(256)S(1)} %get-tuple-element.402) | copy-start | bytes 3076
  1233.5 526.1 %copy-start.15 = (bf16[1,256,1536]{2,1,0:T(8,128)(2,1)S(1)}, bf16[1,256,1536]{2,1,0:T(8,128)(2,1)}, u32[]{:S(2)}) copy-start(bf16[1,256,1536]{2,1,0:T(8,128)(2,1)} %param.23) | copy-start | bytes 2359300
  1814.6 15.3 all-to-all-start.2
  1841.7 6.7 slice-start
  1870.9 6.7 slice-start
  1898.6 8.3 copy-start.6
  1898.6 8.3 copy-start.9
  1902.3 21.6 all-to-all-start.3
  1906.6 391.6 %reduce-scatter.4.cloned.1.call-start = ((), (), s32[]{:S(2)}) async-start(), calls=%async_computation.11 | async-start | bytes 24772608 | tf_op jit(solution)/shard_map/reduce_scatter | solution.py:53
  1941.1 1219.1 %reduce-scatter.8.cloned.1.call-start = ((), (), s32[]{:S(2)}) async-start(), calls=%async_computation.13 | async-start | bytes 61931520 | tf_op jit(solution)/shard_map/reduce_scatter | solution.py:53
  1965.0 2874.2 %reduce-scatter.6.cloned.1.call-start = ((), (), s32[]{:S(2)}) async-start(), calls=%async_computation.12 | async-start | bytes 123863040 | tf_op jit(solution)/shard_map/reduce_scatter | solution.py:53
  2008.1 3229.2 %all-reduce.11.cloned.1.call-start = ((), (), s32[]{:S(2)}) async-start(), calls=%async_computation.14 | async-start | bytes 46792704 | tf_op jit(solution)/shard_map/psum | solution.py:286
  4857.0 48.6 copy-start.7
  4857.0 48.6 copy-start.37
  (32 other events, 75.2 us)
Sparse Core Ops, SparseCore 0:
  10.2 102.4 all-gather.5
  114.9 78.0 all-gather.7
  194.5 1038.9 all-gather.9
  1234.9 524.6 all-gather.11
  1941.3 356.9 reduce-scatter.3
  2302.5 857.7 reduce-scatter.7
  3164.1 1674.9 reduce-scatter.5
  4842.1 395.1 all-reduce.10
where the time goes:
time: 5280 us; the launch traced here: 5270 us
  waiting for transfers between devices  4800 us (91%)
  matrix products  234 us (4%)
  blocking collectives  83 us (2%)
  local copies, waits for them, and re-layouts  70.9 us (1%)
    reduce_scatter x3, waiting for transfers between devices, fsdp_reduce(): lax.psum_scatter(term_fn(jnp.int32(0), lax.axis_size('fsdp') * owned_rows...  2830 us
    all_gather x1, waiting for transfers between devices, local(): lax.all_gather(gate_up_weight, 'fsdp', axis=0, tiled=True)  1040 us
    all_gather x1, waiting for transfers between devices, local(): lax.all_gather(down_weight, 'fsdp', axis=0, tiled=True)  497 us
    psum x1, waiting for transfers between devices, local(): lax.psum((vectors[0], attn_grad, vectors[1], vectors[2], gate_up_grad, do...  329 us
  transfers between devices with their start and end apart: 12, of which 11 were waited for; matrix products, arithmetic and copies ran while one was open for 3% of the time, Pallas kernels for 0%

commit v1 on v0

v1 whole, which is shorter than its diff:
```python
import jax
import jax.numpy as jnp
from jax import lax
from jax.sharding import PartitionSpec as P

H = 12
KV = 2
HD = 128
EPSILON = 1e-06
THETA = 1000000.0
FLOOR = -1e30
LOW = jnp.bfloat16
F32 = jnp.float32


def inverse_rms(value):
    return lax.rsqrt(jnp.mean(value * value, axis=-1, keepdims=True) + EPSILON)


def turned(value):
    halfway = value.shape[-1] // 2
    return jnp.concatenate([-value[..., halfway:], value[..., :halfway]], axis=-1)


def turned_back(value):
    halfway = value.shape[-1] // 2
    return jnp.concatenate([value[..., halfway:], -value[..., :halfway]], axis=-1)


def norm_back(value, factor, gain, upstream):
    weighted = upstream * gain
    gain_term = jnp.sum(upstream * value * factor, axis=0)
    through = factor * weighted - value * factor**3 * jnp.mean(
        weighted * value, axis=-1, keepdims=True
    )
    return (through, gain_term)


def dot(left, right):
    return jnp.dot(left, right, preferred_element_type=F32)


def column_product(left, right):
    return lax.dot_general(left, right, (((0,), (0,)), ((), ())), preferred_element_type=F32)


def times_transpose(left, right):
    return lax.dot_general(left, right, (((1,), (1,)), ((), ())), preferred_element_type=F32)


def swap(value, axis, distance):
    return lax.ppermute(value, axis, [(i, i ^ distance) for i in range(lax.axis_size(axis))])


def lines():
    size = lax.axis_size("fsdp")
    return [list(range(first, size, 2)) for first in range(2)]


def line_gather(value):
    return lax.all_gather(value, "fsdp", axis=0, axis_index_groups=lines(), tiled=False)


def line_reduce(value):
    return lax.psum_scatter(
        value, "fsdp", scatter_dimension=0, axis_index_groups=lines(), tiled=False
    )


def seq_gather(value):
    return lax.all_gather(value, "seq", axis=0, tiled=True)


def seq_reduce(value):
    return lax.psum_scatter(value, "seq", scatter_dimension=0, tiled=True)


def seq_exchange(pieces):
    size = pieces.shape[0]
    me = lax.axis_index("seq")
    taken = [lax.dynamic_index_in_dim(pieces, me ^ k, 0, keepdims=False) for k in range(size)]
    arrived = [taken[0]] + [swap(taken[k], "seq", k) for k in range(1, size)]
    bits = 1
    while bits < size:
        flip = (me & bits) != 0
        arrived = [jnp.where(flip, arrived[k ^ bits], arrived[k]) for k in range(size)]
        bits *= 2
    return arrived


def by_pair(own, other):
    second = lax.axis_index("fsdp") % 2 == 1
    return (jnp.where(second, other, own), jnp.where(second, own, other))


def pick(flag, first, second):
    return (jnp.where(flag, second, first), jnp.where(flag, first, second))


def local(
    tokens,
    segment_ids,
    attn_gain,
    qkv_weight,
    qkv_bias,
    proj_weight,
    mlp_gain,
    gate_up_weight,
    down_weight,
    cotangent,
):
    seq_count = lax.axis_size("seq")
    fsdp_count = lax.axis_size("fsdp")
    line = fsdp_count // 2
    place = lax.axis_index("seq")
    odd = lax.axis_index("fsdp") % 2 == 1
    tok_rows, width = tokens.shape[1:]
    seq_len = tok_rows * seq_count
    owned = qkv_weight.shape[0]
    owned_hidden = down_weight.shape[0]
    hidden = owned_hidden * fsdp_count
    quarter = width // seq_count
    per_dev = H // seq_count
    head_cols = per_dev * HD
    score_scale = HD ** (-0.5)
    group = line // seq_count
    mine_ff = group * owned_hidden

    holds_values = place % 2 == 1
    pair_head = place // 2
    kv_first = (H + KV * (place % 2) + pair_head) * HD
    qkv_own = jnp.concatenate(
        [
            lax.dynamic_slice_in_dim(qkv_weight, place * head_cols, head_cols, 1),
            lax.dynamic_slice_in_dim(qkv_weight, kv_first, HD, 1),
        ],
        axis=1,
    )
    cols = head_cols + HD
    vector = jnp.concatenate([attn_gain, mlp_gain, qkv_bias])
    vector_size = vector.shape[0]
    vector_rows = -(-vector_size // (16 * cols)) * 16
    vector = jnp.pad(vector, (0, vector_rows * cols - vector_size)).reshape(vector_rows, cols)
    qkv_line = line_gather(jnp.concatenate([qkv_own, vector], axis=0))
    tokens_all = seq_gather(tokens[0])
    qkv_both = jnp.stack(by_pair(qkv_line, swap(qkv_line, "fsdp", 1)), axis=1)
    qkv_mine = qkv_both[:, :, :owned].reshape(width, cols)
    vectors = qkv_both[:, :, owned:].reshape(fsdp_count, vector_rows * cols)[:, :vector_size]
    gain_one = vectors[:, :owned].reshape(width).astype(F32)
    gain_two = vectors[:, owned : 2 * owned].reshape(width).astype(F32)
    bias = vectors[:, 2 * owned :].reshape(-1).astype(F32)
    bias_mine = jnp.concatenate(
        [
            lax.dynamic_slice_in_dim(bias, place * head_cols, head_cols),
            lax.dynamic_slice_in_dim(bias, kv_first, HD),
        ]
    )

    proj_cols = lax.dynamic_slice_in_dim(proj_weight, place * quarter, quarter, 1)
    proj_line = line_gather(proj_cols).reshape(seq_count, group * owned, quarter)
    proj_half = jnp.concatenate(seq_exchange(proj_line), axis=1).reshape(group, owned, width)
    proj_mine = jnp.stack(by_pair(proj_half, swap(proj_half, "fsdp", 1)), axis=1).reshape(
        head_cols, width
    )

    down_cols = lax.dynamic_slice_in_dim(down_weight, place * quarter, quarter, 1)
    down_line = line_gather(down_cols).reshape(seq_count, mine_ff, quarter)
    down_mine = jnp.concatenate(seq_exchange(down_line), axis=1)

    def ff_slice(first):
        both = lax.dynamic_slice_in_dim(
            gate_up_weight, first + place * 2 * mine_ff, 2 * mine_ff, 1
        ).reshape(owned, group, 2, owned_hidden)
        return (
            both[:, :, 0].reshape(owned, mine_ff),
            both[:, :, 1].reshape(owned, mine_ff),
        )

    gate_pair, up_pair = ff_slice(0), ff_slice(hidden)
    for_even = jnp.concatenate([gate_pair[0], up_pair[0]], axis=1)
    for_odd = jnp.concatenate([gate_pair[1], up_pair[1]], axis=1)
    kept, given = pick(odd, for_even, for_odd)
    gate_up_pair = jnp.stack(by_pair(kept, swap(given, "fsdp", 1)), axis=0)
    gate_up_mine = line_gather(gate_up_pair).reshape(width, 2 * mine_ff)

    segment_row = segment_ids[0]
    doc_starts = jnp.sum((segment_row[None, :] < segment_row[:, None]).astype(jnp.int32), axis=1)
    places = jnp.arange(seq_len, dtype=jnp.int32) - doc_starts
    inverse = THETA ** (-2.0 * jnp.arange(HD // 2, dtype=F32) / HD)
    angles = places.astype(F32)[:, None] * inverse[None, :]
    angles = jnp.concatenate([angles, angles], axis=-1)
    cosines = jnp.cos(angles)
    sines = jnp.sin(angles)

    resid_all = tokens_all.astype(F32)
    normed_in = (resid_all * inverse_rms(resid_all) * gain_one).astype(LOW)
    projected = dot(normed_in, qkv_mine) + bias_mine
    heads = projected.reshape(seq_len, per_dev + 1, HD)
    rotated = (heads * cosines[:, None] + turned(heads) * sines[:, None]).astype(LOW)
    queries = rotated[:, :per_dev]
    kv_own = jnp.where(holds_values, heads[:, per_dev].astype(LOW), rotated[:, per_dev])
    kv_other = swap(kv_own, "seq", 1)
    head_keys, head_values = pick(holds_values, kv_own, kv_other)

    block_rows = min(512, seq_len)
    blocks = seq_len // block_rows

    def scores_of(index):
        first, last = index * block_rows, (index + 1) * block_rows
        row_index = first + jnp.arange(block_rows, dtype=jnp.int32)
        key_index = jnp.arange(last, dtype=jnp.int32)
        allowed = (key_index[None, :] <= row_index[:, None]) & (
            segment_row[None, :last] == segment_row[first:last, None]
        )
        scores = (
            jnp.einsum(
                "qhd,kd->hqk", queries[first:last], head_keys[:last], preferred_element_type=F32
            )
            * score_scale
        )
        return (jnp.where(allowed[None], scores, FLOOR), allowed)

    head_parts, logsums = [], []
    for index in range(blocks):
        last = (index + 1) * block_rows
        scores, allowed = scores_of(index)
        highest = jnp.max(scores, axis=-1, keepdims=True)
        exponent = jnp.exp(scores - highest)
        row_total = jnp.sum(exponent, axis=-1, keepdims=True)
        weights = (exponent / row_total).astype(LOW)
        mixture = jnp.einsum("hqk,kd->qhd", weights, head_values[:last], preferred_element_type=F32)
        head_parts.append(mixture.astype(LOW).reshape(block_rows, head_cols))
        logsums.append((highest + jnp.log(row_total))[..., 0])
    merged = jnp.concatenate(head_parts, axis=0)

    resid = tokens[0].astype(F32)
    attended = seq_reduce(dot(merged, proj_mine).astype(LOW))
    hidden_in = resid + attended.astype(F32)
    factor_two = inverse_rms(hidden_in)
    normed_own = (hidden_in * factor_two * gain_two).astype(LOW)

    mids = (seq_gather(normed_own), seq_gather(swap(normed_own, "fsdp", 1)))
    cots = (seq_gather(cotangent[0]), seq_gather(swap(cotangent[0], "fsdp", 1)))
    acts, grads, blocks_out, grad_mids = [], [], [], []
    for mid, cot in zip(mids, cots):
        gate_up = dot(mid, gate_up_mine)
        gate, upward = gate_up[:, :mine_ff], gate_up[:, mine_ff:]
        sigmoid_gate = jax.nn.sigmoid(gate)
        act = (gate * sigmoid_gate * upward).astype(LOW)
        grad_act = times_transpose(cot, down_mine)
        grad_gate = grad_act * upward * sigmoid_gate * (1.0 + gate * (1.0 - sigmoid_gate))
        grad_up = grad_act * gate * sigmoid_gate
        grad = jnp.concatenate([grad_gate, grad_up], axis=-1).astype(LOW)
        acts.append(act)
        grads.append(grad)
        blocks_out.append(dot(act, down_mine).astype(LOW))
        grad_mids.append(times_transpose(grad, gate_up_mine).astype(LOW))

    def to_tokens(parts):
        return seq_reduce(parts[0]).astype(F32) + swap(seq_reduce(parts[1]), "fsdp", 1).astype(F32)

    grad_mid = to_tokens(grad_mids)
    block_out = (hidden_in + to_tokens(blocks_out)).astype(LOW)
    down_term = sum(column_product(a, c) for a, c in zip(acts, cots)).astype(LOW)
    gate_up_term = sum(column_product(m, g) for m, g in zip(mids, grads)).astype(LOW)

    through_two, gain_two_term = norm_back(hidden_in, factor_two, gain_two, grad_mid)
    grad_hidden = cotangent[0].astype(F32) + through_two

    grad_attended = seq_gather(grad_hidden.astype(LOW))
    proj_term = column_product(merged, grad_attended).astype(LOW)
    grad_merged = times_transpose(grad_attended, proj_mine).astype(LOW)
    grad_heads = grad_merged.reshape(seq_len, per_dev, HD)
    grad_key = jnp.zeros((seq_len, HD), F32)
    grad_value = jnp.zeros((seq_len, HD), F32)
    grad_queries = []
    for index in range(blocks):
        first, last = index * block_rows, (index + 1) * block_rows
        scores, allowed = scores_of(index)
        probs = jnp.where(allowed[None], jnp.exp(scores - logsums[index][..., None]), 0.0)
        grad_block = grad_heads[first:last]
        grad_probs = jnp.einsum(
            "qhd,kd->hqk", grad_block, head_values[:last], preferred_element_type=F32
        )
        inner = jnp.sum(probs * grad_probs, axis=-1, keepdims=True)
        grad_scores = (probs * (grad_probs - inner)).astype(LOW)
        grad_queries.append(
            (
                jnp.einsum(
                    "hqk,kd->qhd", grad_scores, head_keys[:last], preferred_element_type=F32
                )
                * score_scale
            ).astype(LOW)
        )
        key_term = (
            jnp.einsum(
                "hqk,qhd->kd", grad_scores, queries[first:last], preferred_element_type=F32
            )
            * score_scale
        )
        value_term = jnp.einsum(
            "hqk,qhd->kd", probs.astype(LOW), grad_block, preferred_element_type=F32
        )
        grad_key = grad_key + jnp.pad(key_term, ((0, seq_len - last), (0, 0)))
        grad_value = grad_value + jnp.pad(value_term, ((0, seq_len - last), (0, 0)))
    kept_kv, given_kv = pick(holds_values, grad_key.astype(LOW), grad_value.astype(LOW))
    grad_kv = kept_kv.astype(F32) + swap(given_kv, "seq", 1).astype(F32)
    grad_q = jnp.concatenate(grad_queries, axis=0).astype(F32)
    grad_rot = jnp.concatenate([grad_q, grad_kv[:, None]], axis=1)
    unturned = grad_rot * cosines[:, None] + turned_back(grad_rot * sines[:, None])
    grad_projected = jnp.concatenate(
        [unturned[:, :per_dev], jnp.where(holds_values, grad_kv[:, None], unturned[:, per_dev:])],
        axis=1,
    ).reshape(seq_len, cols).astype(LOW)
    bias_part = jnp.sum(grad_projected.astype(F32), axis=0)
    grad_in = seq_reduce(times_transpose(grad_projected, qkv_mine).astype(LOW)).astype(F32)
    qkv_term = column_product(normed_in, grad_projected).astype(LOW)
    through_one, gain_one_term = norm_back(resid, inverse_rms(resid), gain_one, grad_in)
    tokens_grad = grad_hidden + through_one

    def pair_sum(value):
        kept_rows, given_rows = pick(odd, value[:, 0], value[:, 1])
        arrived = swap(given_rows, "fsdp", 1)
        return (kept_rows.astype(F32) + arrived.astype(F32)).astype(LOW)

    def col_exchange(value):
        rows = value.shape[0]
        cut = jnp.stack([value[:, k * quarter : (k + 1) * quarter] for k in range(seq_count)])
        return jnp.stack(seq_exchange(cut)).reshape(line, rows // group, quarter)

    def from_quarters(value):
        wide = lax.all_gather(value, "seq", axis=0, tiled=False)
        return jnp.concatenate([wide[k] for k in range(seq_count)], axis=-1).astype(F32)

    down_grad = from_quarters(line_reduce(col_exchange(down_term)))
    gate_up_line = line_reduce(gate_up_term.reshape(line, 2, owned, 2 * mine_ff))
    kept, given = pick(odd, gate_up_line[0], gate_up_line[1])
    gate_up_pair = by_pair(kept, swap(given, "fsdp", 1))
    wide = lax.all_gather(jnp.stack(gate_up_pair), "seq", axis=0, tiled=False)
    wide = wide.reshape(seq_count, 2, owned, 2, group, owned_hidden)
    gate_up_grad = jnp.concatenate(
        [
            wide[k, pair, :, part, member]
            for part in range(2)
            for k in range(seq_count)
            for member in range(group)
            for pair in range(2)
        ],
        axis=-1,
    ).astype(F32)
    proj_sum = pair_sum(proj_term.reshape(group, 2, owned, width)).reshape(group * owned, width)
    proj_grad = from_quarters(line_reduce(col_exchange(proj_sum)))
    qkv_sum = line_reduce(pair_sum(qkv_term.reshape(line, 2, owned, cols)))
    wide = lax.all_gather(qkv_sum, "seq", axis=0, tiled=False)
    qkv_grad = jnp.concatenate(
        [wide[k, :, :head_cols] for k in range(seq_count)]
        + [wide[k, :, head_cols:] for k in range(0, seq_count, 2)]
        + [wide[k, :, head_cols:] for k in range(1, seq_count, 2)],
        axis=-1,
    ).astype(F32)

    bias_term = jnp.zeros(qkv_weight.shape[1], F32)
    bias_term = lax.dynamic_update_slice_in_dim(
        bias_term, bias_part[:head_cols], place * head_cols, 0
    )
    bias_term = lax.dynamic_update_slice_in_dim(bias_term, bias_part[head_cols:], kv_first, 0)
    vector_sum = lax.psum(
        jnp.concatenate([gain_one_term, gain_two_term, bias_term]), ("seq", "fsdp")
    )
    at = lax.axis_index("fsdp")
    attn_gain_grad = lax.dynamic_slice_in_dim(vector_sum, at * owned, owned)
    mlp_gain_grad = lax.dynamic_slice_in_dim(vector_sum, width + at * owned, owned)
    owned_bias = qkv_bias.shape[0]
    bias_grad = lax.dynamic_slice_in_dim(vector_sum, 2 * width + at * owned_bias, owned_bias)
    return (
        block_out[None],
        tokens_grad[None],
        attn_gain_grad,
        qkv_grad,
        bias_grad,
        proj_grad,
        mlp_gain_grad,
        gate_up_grad,
        down_grad,
    )


def solution(mesh):
    in_specs = (
        P("fsdp", "seq", None),
        P("fsdp", None),
        P("fsdp"),
        P("fsdp", None),
        P("fsdp"),
        P("fsdp", None),
        P("fsdp"),
        P("fsdp", None),
        P("fsdp", None),
        P("fsdp", "seq", None),
    )
    out_specs = (
        P("fsdp", "seq", None),
        P("fsdp", "seq", None),
        P("fsdp"),
        P("fsdp", None),
        P("fsdp"),
        P("fsdp", None),
        P("fsdp"),
        P("fsdp", None),
        P("fsdp", None),
    )
    return jax.shard_map(local, mesh=mesh, in_specs=in_specs, out_specs=out_specs, check_vma=False)
```

time: 5280 us -> 1120 us (0.21)
  waiting for transfers between devices: 4800 us -> 620 us
  matrix products: 234 us -> 159 us
    reduce_scatter x3 -> x10, waiting for transfers between devices: 2830 us -> 123 us  [the longest x4 72 us: line_reduce(): lax.psum_scatter(value, 'fsdp', scatter_dimension=0, axis_index_groups=li...]
    all_gather x4 -> x10, waiting for transfers between devices: 1590 us -> 258 us  [the longest x6 109 us: seq_gather(): return lax.all_gather(value, 'seq', axis=0, tiled=True)]
    psum x1 -> x0, waiting for transfers between devices: 329 us -> none  [local(): lax.psum((vectors[0], attn_grad, vectors[1], vectors[2], gate_up_grad, do...]
    ppermute x0 -> x24, waiting for transfers between devices: none -> 237 us  [swap(): lax.ppermute(value, axis, [(i, i ^ distance) for i in range(lax.axis_size...]
    unnamed x2 -> x0, blocking collectives: 53.5 us -> none
  transfers between devices with their start and end apart: 12 -> 44, of which waited for: 11 -> 29; matrix products, arithmetic and copies ran while one was open for 3% -> 22% of each run, Pallas kernels for 0% -> 0%
where the time goes in v1:
time: 1120 us; the launch traced here: 1110 us
  waiting for transfers between devices  620 us (55%)
  matrix products  159 us (14%)
  local copies, waits for them, and re-layouts  113 us (10%)
  blocking collectives  96.3 us (9%)
  other arithmetic  78.5 us (7%)
  starting transfers between devices  24.8 us (2%)
  between operations  17.3 us (2%)
    ppermute x24, waiting for transfers between devices, swap(): lax.ppermute(value, axis, [(i, i ^ distance) for i in range(lax.axis_size...  237 us
    all_gather x6, waiting for transfers between devices, seq_gather(): return lax.all_gather(value, 'seq', axis=0, tiled=True)  109 us
    reduce_scatter x4, waiting for transfers between devices, line_reduce(): lax.psum_scatter(value, 'fsdp', scatter_dimension=0, axis_index_groups=li...  72 us
    all_gather x2, waiting for transfers between devices, line_gather(): lax.all_gather(value, 'fsdp', axis=0, axis_index_groups=lines(), tiled=Fa...  71.4 us
    dot_general x6, matrix products, dot(): return jnp.dot(left, right, preferred_element_type=F32)  51.1 us
    reduce_scatter x6, waiting for transfers between devices, seq_reduce(): return lax.psum_scatter(value, 'seq', scatter_dimension=0, tiled=True)  51 us
    dot_general x6, matrix products, times_transpose(): lax.dot_general(left, right, (((1,), (1,)), ((), ())), preferred_element_...  48.7 us
    all_gather x1, waiting for transfers between devices, local(): wide = lax.all_gather(jnp.stack(gate_up_pair), 'seq', axis=0, tiled=False)  47.1 us
  transfers between devices with their start and end apart: 44, of which 29 were waited for; matrix products, arithmetic and copies ran while one was open for 22% of the time, Pallas kernels for 0%

profile of v1, /device:TPU:0, one launch (start us, length us, event | category | flops | bytes accessed | tf_op | source)
XLA Modules:
  0.0 1108.6 jit_solution(10834919232353681802)
XLA Ops:
  9.9 18.4 %all-gather.2 = bf16[768,384]{1,0:T(8,128)(2,1)} all-gather(bf16[192,384]{1,0:T(8,128)(2,1)S(1)} %constant_dynamic-slice_fusion.3), channel_id=4, replica_groups={{0,2,4,6},{1,3,5,7},{8,10,12,14},{9,11,13,15},{16,18,20,22},{17,19,21,2..., dimensions={0}, use_global_device_ids=true | all-gather | bytes 737280 | tf_op jit(solution)/shard_map/all_gather | solution.py:61
  34.6 21.5 %all-gather.1 = bf16[832,512]{1,0:T(8,128)(2,1)} all-gather(bf16[208,512]{1,0:T(8,128)(2,1)S(1)} %pad_maximum_fusion.22), channel_id=3, replica_groups={{0,2,4,6},{1,3,5,7},{8,10,12,14},{9,11,13,15},{16,18,20,22},{17,19,21,2..., dimensions={0}, use_global_device_ids=true | all-gather | bytes 1064960 | tf_op jit(solution)/shard_map/all_gather | solution.py:61
  66.8 21.1 %collective-permute-done.5 = bf16[1,192,1536]{2,1,0:T(8,128)(2,1)} collective-permute-done((bf16[1,192,1536]{2,1,0:T(8,128)(2,1)}, bf16[1,192,1536]{2,1,0:T(8,128)(2,1)}, u32[]{:S(2)}, u32[]{:S(2)}) %collective-permute-start.5) | collective-permute-done | bytes 589856 | tf_op jit(solution)/shard_map/ppermute | solution.py:52
  133.3 20.2 %collective-permute-done.6 = bf16[192,2240]{1,0:T(8,128)(2,1)S(1)} collective-permute-done((bf16[192,2240]{1,0:T(8,128)(2,1)S(1)}, bf16[192,2240]{1,0:T(8,128)(2,1)S(1)}, u32[]{:S(2)}, u32[]{:S(2)}) %collective-permute-start.6) | collective-permute-done | bytes 860192 | tf_op jit(solution)/shard_map/ppermute | solution.py:52
  165.7 17.8 %collective-permute-done.10 = bf16[256,1536]{1,0:T(8,128)(2,1)S(1)} collective-permute-done((bf16[256,1536]{1,0:T(8,128)(2,1)S(1)}, bf16[256,1536]{1,0:T(8,128)(2,1)S(1)}, u32[]{:S(2)}, u32[]{:S(2)}) %collective-permute-start.10) | collective-permute-done | bytes 786464 | tf_op jit(solution)/shard_map/ppermute | solution.py:52
  186.1 17.0 %collective-permute-done.12 = bf16[256,1536]{1,0:T(8,128)(2,1)S(1)} collective-permute-done((bf16[256,1536]{1,0:T(8,128)(2,1)S(1)}, bf16[256,1536]{1,0:T(8,128)(2,1)S(1)}, u32[]{:S(2)}, u32[]{:S(2)}) %collective-permute-start.12) | collective-permute-done | bytes 786464 | tf_op jit(solution)/shard_map/ppermute | solution.py:52
  210.6 19.2 %collective-permute-done.7 = bf16[1120,384]{1,0:T(8,128)(2,1)S(1)} collective-permute-done((bf16[1120,384]{1,0:T(8,128)(2,1)}, bf16[1120,384]{1,0:T(8,128)(2,1)S(1)}, u32[]{:S(2)}, u32[]{:S(2)}) %collective-permute-start.7) | collective-permute-done | bytes 860192 | tf_op jit(solution)/shard_map/ppermute | solution.py:52
  229.8 16.7 %collective-permute-done.8 = bf16[1120,384]{1,0:T(8,128)(2,1)S(1)} collective-permute-done((bf16[1120,384]{1,0:T(8,128)(2,1)}, bf16[1120,384]{1,0:T(8,128)(2,1)S(1)}, u32[]{:S(2)}, u32[]{:S(2)}) %collective-permute-start.8) | collective-permute-done | bytes 860192 | tf_op jit(solution)/shard_map/ppermute | solution.py:52
  250.9 71.4 %all-gather.30.cloned.1.call-done = bf16[8,192,2240]{2,1,0:T(8,128)(2,1)} async-done(((bf16[2,192,2240]{2,1,0:T(8,128)(2,1)}), bf16[8,192,2240]{2,1,0:T(8,128)(2,1)}) %all-gather.30.cloned.1.call-update) | async-done | bytes 6881296 | tf_op jit(solution)/shard_map/all_gather | solution.py:61
  322.3 28.7 %all-gather.20.cloned.1.call-done = bf16[1024,1536]{1,0:T(8,128)(2,1)} async-done(((bf16[256,1536]{1,0:T(8,128)(2,1)}), bf16[1024,1536]{1,0:T(8,128)(2,1)}) %all-gather.20.cloned.1.call-update) | async-done | bytes 3145744 | tf_op jit(solution)/shard_map/all_gather | solution.py:71
  364.2 16.8 %all-gather.22.cloned.1.call-done = bf16[1024,1536]{1,0:T(8,128)(2,1)} async-done(((bf16[256,1536]{1,0:T(8,128)(2,1)}), bf16[1024,1536]{1,0:T(8,128)(2,1)}) %all-gather.22.cloned.1.call-update) | async-done | bytes 3145744 | tf_op jit(solution)/shard_map/all_gather | solution.py:71
  411.2 13.4 %fusion.132 = f32[1024,2240]{0,1:T(8,128)} fusion(bf16[1024,1536]{1,0:T(8,128)(2,1)} %all-gather.18.cloned.1.call-done, bf16[1536,2240]{1,0:T(8,128)(2,1)} %bitcast.517), kind=kOutput, calls=%fused_computation.343 | convolution fusion | flops 7046430720 | bytes 19202048 | tf_op jit(solution)/shard_map/dot_general | solution.py:40
  424.6 32.9 %all-gather.34.cloned.1.call-done = bf16[1,1024,1536]{2,1,0:T(8,128)(2,1)} async-done(((bf16[1,256,1536]{2,1,0:T(8,128)(2,1)}), bf16[1,1024,1536]{2,1,0:T(8,128)(2,1)}) %all-gather.34.cloned.1.call-update) | async-done | bytes 3145744 | tf_op jit(solution)/shard_map/all_gather | solution.py:71
  494.8 32.3 %collective-permute-done.21 = bf16[1120,384]{1,0:T(8,128)(2,1)S(1)} collective-permute-done((bf16[1120,384]{1,0:T(8,128)(2,1)S(1)}, bf16[1120,384]{1,0:T(8,128)(2,1)S(1)}, u32[]{:S(2)}, u32[]{:S(2)}) %collective-permute-start.21) | collective-permute-done | bytes 860192 | tf_op jit(solution)/shard_map/ppermute | solution.py:52
  527.1 22.5 %collective-permute-done.22 = bf16[1120,384]{1,0:T(8,128)(2,1)S(1)} collective-permute-done((bf16[1120,384]{1,0:T(8,128)(2,1)S(1)}, bf16[1120,384]{1,0:T(8,128)(2,1)S(1)}, u32[]{:S(2)}, u32[]{:S(2)}) %collective-permute-start.22) | collective-permute-done | bytes 860192 | tf_op jit(solution)/shard_map/ppermute | solution.py:52
  553.8 18.0 %collective-permute-done.13 = bf16[256,1536]{1,0:T(8,128)(2,1)} collective-permute-done((bf16[256,1536]{1,0:T(8,128)(2,1)}, bf16[256,1536]{1,0:T(8,128)(2,1)}, u32[]{:S(2)}, u32[]{:S(2)}) %collective-permute-start.13) | collective-permute-done | bytes 786464 | tf_op jit(solution)/shard_map/ppermute | solution.py:52
  577.3 13.4 %fusion.32 = f32[1536,2240]{0,1:T(8,128)} fusion(bf16[1024,1536]{1,0:T(8,128)(2,1)} %all-gather.18.cloned.1.call-done, bf16[1024,1120]{0,1:T(8,128)(2,1)} %copy-done.79, bf16[1024,1120]{0,1:T(8,128)(2,1)} %copy-done.78), kind=kOutput, calls=%fused_computation.74 | convolution fusion | flops 7055605760 | bytes 21495808 | tf_op jit(solution)/shard_map/dot_general | solution.py:44
  590.7 14.4 %add_convert_fusion = bf16[1536,2240]{0,1:T(8,128)(2,1)} fusion(f32[1536,2240]{0,1:T(8,128)} %fusion.32, bf16[1024,1536]{1,0:T(8,128)(2,1)S(1)} %copy-done.70, bf16[1024,1120]{0,1:T(8,128)(2,1)S(1)} %copy-done.83, bf16[1024,1120]{0,1:T(8,128)(2,1)S(1)} %copy-done.81), kind=kOutput, calls=%fused_computation | convolution fusion | flops 7062487040 | bytes 28377088 | tf_op jit(solution)/shard_map/dot_general | solution.py:44
  625.9 22.1 %all-gather.24.cloned.1.call-done = bf16[1024,1536]{1,0:T(8,128)(2,1)} async-done(((bf16[256,1536]{1,0:T(8,128)(2,1)}), bf16[1024,1536]{1,0:T(8,128)(2,1)}) %all-gather.24.cloned.1.call-update) | async-done | bytes 3145744 | tf_op jit(solution)/shard_map/all_gather | solution.py:71
  702.7 18.5 %collective-permute-done.15 = bf16[4,192,512]{2,1,0:T(8,128)(2,1)S(1)} collective-permute-done((bf16[4,192,512]{2,1,0:T(8,128)(2,1)S(1)}, bf16[4,192,512]{2,1,0:T(8,128)(2,1)S(1)}, u32[]{:S(2)}, u32[]{:S(2)}) %collective-permute-start.15) | collective-permute-done | bytes 786464 | tf_op jit(solution)/shard_map/ppermute | solution.py:52
  737.3 37.3 %reduce-scatter.27.cloned.1.call-done = bf16[1,2,192,2240]{3,2,1,0:T(8,128)(2,1)} async-done(((bf16[4,2,192,2240]{3,2,1,0:T(8,128)(2,1)}), bf16[1,2,192,2240]{3,2,1,0:T(8,128)(2,1)}) %reduce-scatter.27.cloned.1.call-update) | async-done | bytes 1720336 | tf_op jit(solution)/shard_map/reduce_scatter | solution.py:65
  777.7 20.0 %collective-permute-done.20 = bf16[192,2240]{1,0:T(8,128)(2,1)S(1)} collective-permute-done((bf16[192,2240]{1,0:T(8,128)(2,1)S(1)}, bf16[192,2240]{1,0:T(8,128)(2,1)S(1)}, u32[]{:S(2)}, u32[]{:S(2)}) %collective-permute-start.20) | collective-permute-done | bytes 860192 | tf_op jit(solution)/shard_map/ppermute | solution.py:52
  799.3 16.5 %reduce-scatter.15.cloned.1.call-done = bf16[256,1536]{1,0:T(8,128)(2,1)} async-done(((bf16[1024,1536]{1,0:T(8,128)(2,1)}), bf16[256,1536]{1,0:T(8,128)(2,1)}) %reduce-scatter.15.cloned.1.call-update) | async-done | bytes 786448 | tf_op jit(solution)/shard_map/reduce_scatter | solution.py:75
  817.4 30.1 %all-gather.26.cloned.1.call-done = bf16[4,1120,384]{2,1,0:T(8,128)(2,1)} async-done(((bf16[1,1120,384]{2,1,0:T(8,128)(2,1)}), bf16[4,1120,384]{2,1,0:T(8,128)(2,1)}) %all-gather.26.cloned.1.call-update) | async-done | bytes 3440656 | tf_op jit(solution)/shard_map/all_gather | solution.py:332
  853.2 19.1 %reduce-scatter.25.cloned.1.call-done = bf16[1,192,384]{2,1,0:T(8,128)(2,1)} async-done(((bf16[4,192,384]{2,1,0:T(8,128)(2,1)}), bf16[1,192,384]{2,1,0:T(8,128)(2,1)}) %reduce-scatter.25.cloned.1.call-update) | async-done | bytes 147472 | tf_op jit(solution)/shard_map/reduce_scatter | solution.py:65
  881.2 15.6 %reduce-scatter.23.cloned.1.call-done = bf16[1,192,512]{2,1,0:T(8,128)(2,1)} async-done(((bf16[4,192,512]{2,1,0:T(8,128)(2,1)}), bf16[1,192,512]{2,1,0:T(8,128)(2,1)}) %reduce-scatter.23.cloned.1.call-update) | async-done | bytes 196624 | tf_op jit(solution)/shard_map/reduce_scatter | solution.py:65
  907.4 29.1 %reduce-scatter.21.cloned.1.call-done = bf16[256,1536]{1,0:T(8,128)(2,1)} async-done(((bf16[1024,1536]{1,0:T(8,128)(2,1)}), bf16[256,1536]{1,0:T(8,128)(2,1)}) %reduce-scatter.21.cloned.1.call-update) | async-done | bytes 786448 | tf_op jit(solution)/shard_map/reduce_scatter | solution.py:75
  938.1 39.7 %psum.7 = f32[5120]{0:T(1024)S(1)} all-reduce(f32[5120]{0:T(1024)S(1)} %pad_maximum_fusion.24), channel_id=1, replica_groups=mesh['seq'=4,'fsdp'=8] {'seq','fsdp'}, use_global_device_ids=true, to_apply=%region_21.22 | all-reduce | flops 5120 | bytes 40960 | tf_op jit(solution)/shard_map/psum | solution.py:367
  983.7 47.1 %all-gather.36.cloned.1.call-done = bf16[8,192,2240]{2,1,0:T(8,128)(2,1)} async-done(((bf16[2,192,2240]{2,1,0:T(8,128)(2,1)}), bf16[8,192,2240]{2,1,0:T(8,128)(2,1)}) %all-gather.36.cloned.1.call-update) | async-done | bytes 6881296 | tf_op jit(solution)/shard_map/all_gather | solution.py:339
  1030.7 16.1 %reshape.414 = bf16[4,2,192,2,1,1120]{5,3,2,1,0,4:T(2,128)(2,1)} reshape(bf16[8,192,2240]{2,1,0:T(8,128)(2,1)} %all-gather.36.cloned.1.call-done) | data formatting | bytes 13762560 | tf_op jit(solution)/shard_map/reshape | solution.py:340
  1046.8 17.9 %fusion.123 = (bf16[1,1,192,1,1,1120]{5,3,2,1,0,4:T(2,128)(2,1)S(1)}, bf16[1,1,192,1,1,1120]{5,3,2,1,0,4:T(2,128)(2,1)S(1)}, bf16[1,1,192,1,1,1120]{5,3,2,1,0,4:...) fusion(bf16[4,2,192,2,1,1120]{5,3,2,1,0,4:T(2,128)(2,1)} %resha, ...), kind=kLoop, calls=%fused_computation.334 | loop fusion | bytes 13762560 | tf_op jit(solution)/shard_map/slice | solution.py:343
  1075.7 15.6 %concatenate.96 = bf16[192,17920]{1,0:T(8,128)(2,1)} concatenate(bf16[192,1120]{1,0:T(8,128)(2,1)S(1)} %bitcast.481, bf16[192,1120]{1,0:T(8,128)(2,1)} %bitcast.482, bf16[192,1120]{1,0:T(8,128)(2,1)} %bitcast.483, bf16[192,1120]{1,0:T(8,128)(2,1)} %bitcast.484, bf16[192,1120]{1,0:T(8,128)(2,1)} %bitcast.485, bf16[192,1120]{1,0:T(8,128)(2,1)} %bitcast.486, ...), dimensions={1} | concatenate | bytes 13762560 | tf_op jit(solution)/shard_map/concatenate | solution.py:341
  (419 shorter events, 330.8 us)
Async XLA Ops:
  8.0 88.1 %all-gather.28.cloned.1.call-start = ((), (), s32[]{:S(2)}) async-start(), calls=%async_computation.25 | async-start | bytes 3932160 | tf_op jit(solution)/shard_map/all_gather | solution.py:71
  8.8 152.5 %reduce-scatter.11.cloned.1.call-start = ((), (), s32[]{:S(2)}) async-start(), calls=%async_computation.10 | async-start | bytes 3932160 | tf_op jit(solution)/shard_map/reduce_scatter | solution.py:75
  30.2 28.2 %collective-permute-start.2 = (bf16[192,384]{1,0:T(8,128)(2,1)}, bf16[192,384]{1,0:T(8,128)(2,1)}, u32[]{:S(2)}, u32[]{:S(2)}) collective-permute-start(bf16[192,384]{1,0:T(8,128)(2,1)} %get-tuple-element.103), channel_id=1, source_target_pairs={{0,24},{8,16},{16,8},{24,0},{1,25},{9,17},{17,9},{25,1},{2,26},{10... | collective-permute-start | bytes 442376 | tf_op jit(solution)/shard_map/ppermute | solution.py:52
  30.2 28.2 %collective-permute-start.3 = (bf16[192,384]{1,0:T(8,128)(2,1)}, bf16[192,384]{1,0:T(8,128)(2,1)}, u32[]{:S(2)}, u32[]{:S(2)}) collective-permute-start(bf16[192,384]{1,0:T(8,128)(2,1)} %get-tuple-element.102), channel_id=1, source_target_pairs={{0,16},{8,24},{16,0},{24,8},{1,17},{9,25},{17,1},{25,9},{2,18},{10... | collective-permute-start | bytes 442376 | tf_op jit(solution)/shard_map/ppermute | solution.py:52
  31.7 26.7 %collective-permute-start.4 = (bf16[192,384]{1,0:T(8,128)(2,1)}, bf16[192,384]{1,0:T(8,128)(2,1)}, u32[]{:S(2)}, u32[]{:S(2)}) collective-permute-start(bf16[192,384]{1,0:T(8,128)(2,1)} %get-tuple-element.101), channel_id=1, source_target_pairs={{0,8},{8,0},{16,24},{24,16},{1,9},{9,1},{17,25},{25,17},{2,10},{10... | collective-permute-start | bytes 442376 | tf_op jit(solution)/shard_map/ppermute | solution.py:52
  56.1 34.3 %collective-permute-start = (bf16[4,208,512]{2,1,0:T(8,128)(2,1)}, bf16[4,208,512]{2,1,0:T(8,128)(2,1)}, u32[]{:S(2)}, u32[]{:S(2)}) collective-permute-start(bf16[4,208,512]{2,1,0:T(8,128)(2,1)} %bitcast.3), channel_id=1, source_target_pairs={{0,1},{1,0},{2,3},{3,2},{4,5},{5,4},{6,7},{7,6},{8,9},{9,8},{10,11... | collective-permute-start | bytes 2555912 | tf_op jit(solution)/shard_map/ppermute | solution.py:52
  61.2 26.7 %collective-permute-start.5 = (bf16[1,192,1536]{2,1,0:T(8,128)(2,1)}, bf16[1,192,1536]{2,1,0:T(8,128)(2,1)}, u32[]{:S(2)}, u32[]{:S(2)}) collective-permute-start(bf16[1,192,1536]{2,1,0:T(8,128)(2,1)} %maximum_bitcast_fusion), channel_id=1, source_target_pairs={{0,1},{1,0},{2,3},{3,2},{4,5},{5,4},{6,7},{7,6},{8,9},{9,8},{10,11... | collective-permute-start | bytes 1769480 | tf_op jit(solution)/shard_map/ppermute | solution.py:52
  123.1 81.7 %all-gather.32.cloned.1.call-start = ((), (), s32[]{:S(2)}) async-start(), calls=%async_computation.27 | async-start | bytes 4300800 | tf_op jit(solution)/shard_map/all_gather | solution.py:61
  124.3 198.0 %all-gather.30.cloned.1.call-start = ((), (), s32[]{:S(2)}) async-start(), calls=%async_computation.26 | async-start | bytes 8847360 | tf_op jit(solution)/shard_map/all_gather | solution.py:61
  131.7 21.8 %collective-permute-start.6 = (bf16[192,2240]{1,0:T(8,128)(2,1)S(1)}, bf16[192,2240]{1,0:T(8,128)(2,1)S(1)}, u32[]{:S(2)}, u32[]{:S(2)}) collective-permute-start(bf16[192,2240]{1,0:T(8,128)(2,1)S(1)} %broadcast_select_fusion.2), channel_id=1, source_target_pairs={{0,1},{1,0},{2,3},{3,2},{4,5},{5,4},{6,7},{7,6},{8,9},{9,8},{10,11... | collective-permute-start | bytes 2580488 | tf_op jit(solution)/shard_map/ppermute | solution.py:52
  155.7 195.3 %all-gather.20.cloned.1.call-start = ((), (), s32[]{:S(2)}) async-start(), calls=%async_computation.13 | async-start | bytes 3932160 | tf_op jit(solution)/shard_map/all_gather | solution.py:71
  184.5 196.6 %all-gather.22.cloned.1.call-start = ((), (), s32[]{:S(2)}) async-start(), calls=%async_computation.16 | async-start | bytes 3932160 | tf_op jit(solution)/shard_map/all_gather | solution.py:71
  204.0 207.2 %all-gather.18.cloned.1.call-start = ((), (), s32[]{:S(2)}) async-start(), calls=%async_computation.11 | async-start | bytes 3932160 | tf_op jit(solution)/shard_map/all_gather | solution.py:71
  204.8 252.8 %all-gather.34.cloned.1.call-start = ((), (), s32[]{:S(2)}) async-start(), calls=%async_computation.28 | async-start | bytes 3932160 | tf_op jit(solution)/shard_map/all_gather | solution.py:71
  208.2 38.3 %collective-permute-start.8 = (bf16[1120,384]{1,0:T(8,128)(2,1)}, bf16[1120,384]{1,0:T(8,128)(2,1)S(1)}, u32[]{:S(2)}, u32[]{:S(2)}) collective-permute-start(bf16[1120,384]{1,0:T(8,128)(2,1)} %get-tuple-element.60), channel_id=1, source_target_pairs={{0,16},{8,24},{16,0},{24,8},{1,17},{9,25},{17,1},{25,9},{2,18},{10... | collective-permute-start | bytes 2580488 | tf_op jit(solution)/shard_map/ppermute | solution.py:52
  208.8 38.6 %collective-permute-start.9 = (bf16[1120,384]{1,0:T(8,128)(2,1)S(1)}, bf16[1120,384]{1,0:T(8,128)(2,1)}, u32[]{:S(2)}, u32[]{:S(2)}) collective-permute-start(bf16[1120,384]{1,0:T(8,128)(2,1)S(1)} %get-tuple-element.59), channel_id=1, source_target_pairs={{0,8},{8,0},{16,24},{24,16},{1,9},{9,1},{17,25},{25,17},{2,10},{10... | collective-permute-start | bytes 2580488 | tf_op jit(solution)/shard_map/ppermute | solution.py:52
  210.1 342.1 %reduce-scatter.19.cloned.1.call-start = ((), (), s32[]{:S(2)}) async-start(), calls=%async_computation.17 | async-start | bytes 3932160 | tf_op jit(solution)/shard_map/reduce_scatter | solution.py:75
  402.3 151.5 %reduce-scatter.17.cloned.1.call-start = ((), (), s32[]{:S(2)}) async-start(), calls=%async_computation.15 | async-start | bytes 3932160 | tf_op jit(solution)/shard_map/reduce_scatter | solution.py:75
  480.7 144.9 %reduce-scatter.29.cloned.1.call-start = ((), (), s32[]{:S(2)}) async-start(), calls=%async_computation.23 | async-start | bytes 4300800 | tf_op jit(solution)/shard_map/reduce_scatter | solution.py:65
  492.8 34.2 %collective-permute-start.21 = (bf16[1120,384]{1,0:T(8,128)(2,1)S(1)}, bf16[1120,384]{1,0:T(8,128)(2,1)S(1)}, u32[]{:S(2)}, u32[]{:S(2)}) collective-permute-start(bf16[1120,384]{1,0:T(8,128)(2,1)S(1)} %get-tuple-element.54), channel_id=1, source_target_pairs={{0,24},{8,16},{16,8},{24,0},{1,25},{9,17},{17,9},{25,1},{2,26},{10... | collective-permute-start | bytes 2580488 | tf_op jit(solution)/shard_map/ppermute | solution.py:52
  493.1 56.5 %collective-permute-start.22 = (bf16[1120,384]{1,0:T(8,128)(2,1)S(1)}, bf16[1120,384]{1,0:T(8,128)(2,1)S(1)}, u32[]{:S(2)}, u32[]{:S(2)}) collective-permute-start(bf16[1120,384]{1,0:T(8,128)(2,1)S(1)} %get-tuple-element.53), channel_id=1, source_target_pairs={{0,16},{8,24},{16,0},{24,8},{1,17},{9,25},{17,1},{25,9},{2,18},{10... | collective-permute-start | bytes 2580488 | tf_op jit(solution)/shard_map/ppermute | solution.py:52
  494.8 54.8 %collective-permute-start.23 = (bf16[1120,384]{1,0:T(8,128)(2,1)S(1)}, bf16[1120,384]{1,0:T(8,128)(2,1)S(1)}, u32[]{:S(2)}, u32[]{:S(2)}) collective-permute-start(bf16[1120,384]{1,0:T(8,128)(2,1)S(1)} %get-tuple-element.52), channel_id=1, source_target_pairs={{0,8},{8,0},{16,24},{24,16},{1,9},{9,1},{17,25},{25,17},{2,10},{10... | collective-permute-start | bytes 2580488 | tf_op jit(solution)/shard_map/ppermute | solution.py:52
  552.2 95.9 %all-gather.24.cloned.1.call-start = ((), (), s32[]{:S(2)}) async-start(), calls=%async_computation.18 | async-start | bytes 3932160 | tf_op jit(solution)/shard_map/all_gather | solution.py:71
  576.8 197.7 %reduce-scatter.27.cloned.1.call-start = ((), (), s32[]{:S(2)}) async-start(), calls=%async_computation.22 | async-start | bytes 8847360 | tf_op jit(solution)/shard_map/reduce_scatter | solution.py:65
  615.3 200.5 %reduce-scatter.15.cloned.1.call-start = ((), (), s32[]{:S(2)}) async-start(), calls=%async_computation.14 | async-start | bytes 3932160 | tf_op jit(solution)/shard_map/reduce_scatter | solution.py:75
  624.9 222.7 %all-gather.26.cloned.1.call-start = ((), (), s32[]{:S(2)}) async-start(), calls=%async_computation.24 | async-start | bytes 4300800 | tf_op jit(solution)/shard_map/all_gather | solution.py:332
  625.7 246.7 %reduce-scatter.25.cloned.1.call-start = ((), (), s32[]{:S(2)}) async-start(), calls=%async_computation.21 | async-start | bytes 737280 | tf_op jit(solution)/shard_map/reduce_scatter | solution.py:65
  701.0 195.9 %reduce-scatter.23.cloned.1.call-start = ((), (), s32[]{:S(2)}) async-start(), calls=%async_computation.20 | async-start | bytes 983040 | tf_op jit(solution)/shard_map/reduce_scatter | solution.py:65
  722.4 214.0 %reduce-scatter.21.cloned.1.call-start = ((), (), s32[]{:S(2)}) async-start(), calls=%async_computation.19 | async-start | bytes 3932160 | tf_op jit(solution)/shard_map/reduce_scatter | solution.py:75
  727.7 251.4 %reduce-scatter.13.cloned.1.call-start = ((), (), s32[]{:S(2)}) async-start(), calls=%async_computation.12 | async-start | bytes 3932160 | tf_op jit(solution)/shard_map/reduce_scatter | solution.py:75
  737.2 293.5 %all-gather.36.cloned.1.call-start = ((), (), s32[]{:S(2)}) async-start(), calls=%async_computation.29 | async-start | bytes 8847360 | tf_op jit(solution)/shard_map/all_gather | solution.py:339
  815.8 163.3 %collective-permute-start.11 = (bf16[256,1536]{1,0:T(8,128)(2,1)}, bf16[256,1536]{1,0:T(8,128)(2,1)}, u32[]{:S(2)}, u32[]{:S(2)}) collective-permute-start(bf16[256,1536]{1,0:T(8,128)(2,1)} %reduce-scatter.15.cloned.1.call-done), channel_id=1, source_target_pairs={{0,1},{1,0},{2,3},{3,2},{4,5},{5,4},{6,7},{7,6},{8,9},{9,8},{10,11... | collective-permute-start | bytes 2359304 | tf_op jit(solution)/shard_map/ppermute | solution.py:52
  (98 other events, 1637.9 us)
Sparse Core Ops, SparseCore 0:
  10.4 37.5 all-gather.27
  123.3 37.9 reduce-scatter.10
  402.4 38.1 reduce-scatter.18
  480.8 54.9 reduce-scatter.16
  552.3 64.8 reduce-scatter.28
  619.2 28.7 all-gather.23
  651.0 123.4 reduce-scatter.26
  777.2 38.4 reduce-scatter.14
  817.3 30.1 all-gather.25
  850.3 22.0 reduce-scatter.24
  875.2 21.5 reduce-scatter.22
  899.2 37.1 reduce-scatter.20
  939.2 38.4 reduce-scatter.12
  979.7 51.0 all-gather.35
Sparse Core Ops, SparseCore 1:
  125.3 68.1 all-gather.31
  195.6 126.7 all-gather.29
  324.4 26.6 all-gather.19
  352.6 28.3 all-gather.21
  382.6 28.5 all-gather.17
  412.8 44.7 all-gather.33

commit v2 on v1

v2 whole, which is shorter than its diff:
```python
import functools

import jax
import jax.numpy as jnp
from jax import lax
from jax.experimental import pallas as pl
from jax.experimental.pallas import tpu as pltpu
from jax.sharding import PartitionSpec as P

H = 12
KV = 2
HD = 128
EPSILON = 1e-06
THETA = 1000000.0
FLOOR = -1e30
LOW = jnp.bfloat16
F32 = jnp.float32


def inverse_rms(value):
    return lax.rsqrt(jnp.mean(value * value, axis=-1, keepdims=True) + EPSILON)


def turned(value):
    halfway = value.shape[-1] // 2
    return jnp.concatenate([-value[..., halfway:], value[..., :halfway]], axis=-1)


def turned_back(value):
    halfway = value.shape[-1] // 2
    return jnp.concatenate([value[..., halfway:], -value[..., :halfway]], axis=-1)


def norm_back(value, factor, gain, upstream):
    weighted = upstream * gain
    gain_term = jnp.sum(upstream * value * factor, axis=0)
    through = factor * weighted - value * factor**3 * jnp.mean(
        weighted * value, axis=-1, keepdims=True
    )
    return (through, gain_term)


def dot(left, right):
    return jnp.dot(left, right, preferred_element_type=F32)


def column_product(left, right):
    return lax.dot_general(left, right, (((0,), (0,)), ((), ())), preferred_element_type=F32)


def times_transpose(left, right):
    return lax.dot_general(left, right, (((1,), (1,)), ((), ())), preferred_element_type=F32)


def swap(value, axis, distance):
    return lax.ppermute(value, axis, [(i, i ^ distance) for i in range(lax.axis_size(axis))])


def lines():
    size = lax.axis_size("fsdp")
    return [list(range(first, size, 2)) for first in range(2)]


def line_reduce(value):
    return lax.psum_scatter(
        value, "fsdp", scatter_dimension=0, axis_index_groups=lines(), tiled=False
    )


def by_pair(own, other):
    second = lax.axis_index("fsdp") % 2 == 1
    return (jnp.where(second, other, own), jnp.where(second, own, other))


def pick(flag, first, second):
    return (jnp.where(flag, second, first), jnp.where(flag, first, second))


def after(value, *earlier):
    return lax.optimization_barrier((value, *earlier))[0]


def seq_blocks(value):
    across = swap(value, "seq", 2)
    return [value, swap(value, "seq", 1), across, swap(across, "seq", 1)]


def seq_reduce(parts):
    arrived = swap(jnp.stack([parts[1], parts[3]]), "seq", 1)
    across = (parts[2].astype(F32) + arrived[1].astype(F32)).astype(LOW)
    here = parts[0].astype(F32) + arrived[0].astype(F32)
    return here + swap(across, "seq", 2).astype(F32)


def in_order(blocks):
    me = lax.axis_index("seq")
    bits = 1
    while bits < len(blocks):
        flip = (me & bits) != 0
        blocks = [jnp.where(flip, blocks[k ^ bits], blocks[k]) for k in range(len(blocks))]
        bits *= 2
    return blocks


def relative(value):
    size = lax.axis_size("seq")
    me = lax.axis_index("seq")
    cut = value.reshape(size, value.shape[0] // size, *value.shape[1:])
    return [lax.dynamic_index_in_dim(cut, me ^ k, 0, keepdims=False) for k in range(size)]


def seq_exchange(pieces):
    taken = [part[0] for part in relative(pieces)]
    return in_order([taken[0]] + [swap(taken[k], "seq", k) for k in range(1, len(taken))])


MESH = pl.DeviceIdType.MESH


def neighbours():
    me, owner = lax.axis_index("seq"), lax.axis_index("fsdp")
    sibling = me + 1 - 2 * (me % 2)
    across = me + 2 - 4 * (me // 2 % 2)
    partner = owner + 1 - 2 * (owner % 2)
    return (me, sibling, across), ({"seq": sibling}, {"seq": across}, {"fsdp": partner})


def greet(devices):
    barrier = pltpu.get_barrier_semaphore()
    for device in devices:
        pl.semaphore_signal(barrier, inc=1, device_id=device, device_id_type=MESH)
    pl.semaphore_wait(barrier, len(devices))


class Sender:
    def __init__(self, send_sems, recv_sems):
        self.sems = (send_sems, recv_sems)
        self.copies = []

    def send(self, source, target, device):
        number = len(self.copies)
        copy = pltpu.make_async_remote_copy(
            src_ref=source,
            dst_ref=target,
            send_sem=self.sems[0].at[number],
            recv_sem=self.sems[1].at[number],
            device_id=device,
            device_id_type=MESH,
        )
        copy.start()
        self.copies.append(copy)
        return copy

    def finish(self):
        for copy in self.copies:
            copy.wait_send()


def whole_call(kernel, out_shapes, scratch, copies, number, args):
    sems = [pltpu.SemaphoreType.DMA((copies,))] * 2
    return pl.pallas_call(
        kernel,
        out_shape=out_shapes,
        in_specs=[pl.BlockSpec(memory_space=pltpu.VMEM)] * len(args),
        out_specs=[pl.BlockSpec(memory_space=pltpu.VMEM)] * len(out_shapes),
        scratch_shapes=[*scratch, *sems],
        compiler_params=pltpu.CompilerParams(
            collective_id=number, has_side_effects=True, vmem_limit_bytes=40 << 20
        ),
    )(*args)


def plane_gather(link, blocks, ids):
    core, over_x, over_y = ids
    rows = blocks.shape[1]
    halves = (pl.ds(0, rows // 2), pl.ds(rows // 2, rows // 2))
    to_x = [link.send(blocks.at[0, half], blocks.at[2, half], over_x) for half in halves]
    to_y = [link.send(blocks.at[0, half], blocks.at[4, half], over_y) for half in halves[::-1]]
    last = [link.send(blocks.at[0], blocks.at[1], core)]
    yield
    to_x[0].wait_recv()
    diagonal = [link.send(blocks.at[2, halves[0]], blocks.at[6, halves[0]], over_y)]
    last.append(link.send(blocks.at[2, halves[0]], blocks.at[3, halves[0]], core))
    to_y[0].wait_recv()
    diagonal.append(link.send(blocks.at[4, halves[1]], blocks.at[6, halves[1]], over_x))
    last.append(link.send(blocks.at[4, halves[1]], blocks.at[5, halves[1]], core))
    to_x[1].wait_recv()
    last.append(link.send(blocks.at[2, halves[1]], blocks.at[3, halves[1]], core))
    to_y[1].wait_recv()
    last.append(link.send(blocks.at[4, halves[0]], blocks.at[5, halves[0]], core))
    for copy, half in zip(diagonal, halves):
        copy.wait_recv()
        last.append(link.send(blocks.at[6, half], blocks.at[7, half], core))
    for copy in last:
        copy.wait_recv()
    yield


def opening_kernel(
    shape,
    tokens,
    cotangent,
    qkv,
    proj,
    ff_first,
    ff_second,
    cosines,
    sines,
    seg_col,
    seg_row,
    tokens_all,
    qkv_all,
    proj_mine,
    first_all,
    second_all,
    first_rows,
    second_rows,
    normed,
    queries,
    keys,
    values,
    merged,
    logsum,
    hidden,
    mids,
    cots,
    proj_all,
    weight,
    vectors,
    kv,
    part,
    arrived,
    summed,
    across_in,
    send_sems,
    recv_sems,
    local_sems,
):
    owned, vector_size, per_dev, group = shape
    (me, sibling, across), ids = neighbours()
    core, over_x, over_y = ids
    far = across + 1 - 2 * (across % 2)
    line = qkv_all.shape[0]
    size = 2 * line
    owner = lax.axis_index("fsdp")
    at, pair = owner // 2, owner % 2
    below, above = ({"fsdp": (owner + size - 2) % size}, {"fsdp": (owner + 2) % size})
    rows, width = tokens.shape
    seq_count = tokens_all.shape[0]
    seq_len = seq_count * rows
    halves = (pl.ds(0, rows // 2), pl.ds(rows // 2, rows // 2))
    others = (sibling, across, far)
    greet((*ids, {"seq": far}, below, above))
    link = Sender(send_sems, recv_sems)

    own_copies = []
    for number, (own, whole) in enumerate(((ff_first, first_all), (ff_second, second_all))):
        for place, source in enumerate((pair, 2)):
            copy = pltpu.make_async_copy(
                own.at[source], whole.at[at, source], local_sems.at[2 * number + place]
            )
            copy.start()
            own_copies.append(copy)
    tokens_all[me] = tokens[...]
    qkv_all[at, pair] = qkv[...]
    proj_all[at, pair] = proj[...]

    last = []

    def step(array, k):
        here = array.at[(at + k) % line, pair]
        onward = link.send(here, here, below) if k < line - 1 else None
        last.append(link.send(here, here, over_y))
        return onward

    onward = [step(array, 0) for array in (qkv_all, proj_all)]
    to_x = [link.send(tokens_all.at[me, half], tokens_all.at[me, half], over_x) for half in halves]
    last.append(link.send(tokens_all.at[me], tokens_all.at[me], core))
    for k in range(1, line):
        for number, array in enumerate((qkv_all, proj_all)):
            onward[number].wait_recv()
            onward[number] = step(array, k)

    turned_over = [
        link.send(own.at[1 - pair], whole.at[at, pair], over_y)
        for own, whole in ((ff_first, first_all), (ff_second, second_all))
    ]
    arrivals = []

    def ring_steps():
        for number, (own, whole) in enumerate(((ff_first, first_all), (ff_second, second_all))):
            before = None
            for k in range(line - 1):
                block, now = whole.at[(at + k) % line], []
                for place, part_of in enumerate((pair, 2, 1 - pair)):
                    if k > 0:
                        before[place].wait_recv()
                    elif place == 2:
                        turned_over[number].wait_recv()
                    source = own if k == 0 and place < 2 else block
                    now.append(link.send(source.at[part_of], block.at[part_of], below))
                before = now
                yield
            arrivals.append(before)

    ring = ring_steps()

    def pump(count=1):
        for _ in range(count):
            next(ring, None)

    def exchange_rows(number, whole, rows_mine):
        while len(arrivals) <= number:
            next(ring, None)
        for copy in arrivals[number]:
            copy.wait_recv()
        for copy in own_copies[2 * number : 2 * number + 2]:
            copy.wait()
        mine = whole.at[pl.ds(me * group, group), 2]
        copy = pltpu.make_async_copy(mine, rows_mine.at[me], local_sems.at[4 + number])
        copy.start()
        sent = [copy]
        for target in others:
            source = whole.at[pl.ds(target * group, group), 2]
            sent.append(link.send(source, rows_mine.at[me], {"seq": target}))
        return sent

    pump()
    for copy, half in zip(to_x, halves):
        copy.wait_recv()
        last.append(link.send(tokens_all.at[across, half], tokens_all.at[across, half], core))
    for copy in last:
        copy.wait_recv()
    cots[0] = cotangent[...]
    gather_cots = plane_gather(link, cots, ids)
    next(gather_cots)

    for z in range(line):
        for y in range(2):
            owner_row = 2 * z + y
            weight[pl.ds(owner_row * owned, owned), :] = qkv_all[z, y, :owned, :]
            done = 0
            cols = qkv_all.shape[3]
            for start, count, target in (
                (0, owned, 0),
                (owned, owned, 1),
                (2 * owned, vector_size - 2 * owned, 2),
            ):
                while count > 0:
                    row, col = start // cols, start % cols
                    span = min(count, cols - col)
                    length = (owned, owned, vector_size - 2 * owned)[target]
                    to = owner_row * length + (length - count)
                    vectors[target : target + 1, to : to + span] = qkv_all[
                        z, y, owned + row : owned + row + 1, col : col + span
                    ].astype(F32)
                    start, count = start + span, count - span
    exchange = [
        link.send(proj_all.at[pl.ds(target * group, group)], proj_mine.at[me], {"seq": target})
        for target in others
    ]
    proj_mine[me] = proj_all[pl.ds(me * group, group)]

    head_cols = per_dev * HD
    holds_values = me % 2 == 1
    kv_first = (H + KV * (me % 2) + me // 2) * HD
    bias = jnp.concatenate(
        [
            vectors[2:3, pl.ds(pl.multiple_of(me * head_cols, HD), head_cols)],
            vectors[2:3, pl.ds(pl.multiple_of(kv_first, HD), HD)],
        ],
        axis=1,
    )
    for block in range(seq_count):
        here = pl.ds(block * rows, rows)
        value = tokens_all[block].astype(F32)
        normal = (value * inverse_rms(value) * vectors[0:1, :width]).astype(LOW)
        normed[block] = normal
        projected = dot(normal, weight[...]) + bias
        cosine, sine = cosines[here, :], sines[here, :]

        def rotate(head):
            return head * cosine + pltpu.roll(head, HD // 2, 1) * sine

        for head in range(per_dev):
            queries[head, here, :] = rotate(projected[:, head * HD : (head + 1) * HD]).astype(LOW)
        plain = projected[:, head_cols:]
        kv[0, here, :] = jnp.where(holds_values, plain, rotate(plain)).astype(LOW)
    swapped = link.send(kv.at[0], kv.at[1], core)
    pump()
    swapped.wait_recv()
    keys[...] = jnp.where(holds_values, kv[1], kv[0])
    values[...] = jnp.where(holds_values, kv[0], kv[1])

    for block in range(seq_count):
        here, last_key = pl.ds(block * rows, rows), (block + 1) * rows
        row_index = block * rows + lax.broadcasted_iota(jnp.int32, (rows, last_key), 0)
        key_index = lax.broadcasted_iota(jnp.int32, (rows, last_key), 1)
        allowed = (key_index <= row_index) & (seg_col[here, :] == seg_row[:, :last_key])
        for head in range(per_dev):
            scores = times_transpose(queries[head, here, :], keys[:last_key, :]) * HD ** (-0.5)
            scores = jnp.where(allowed, scores, FLOOR)
            highest = jnp.max(scores, axis=-1, keepdims=True)
            exponent = jnp.exp(scores - highest)
            total = jnp.sum(exponent, axis=-1, keepdims=True)
            mixture = dot((exponent / total).astype(LOW), values[:last_key, :])
            merged[here, head * HD : (head + 1) * HD] = mixture.astype(LOW)
            logsum[head, here, :] = highest + jnp.log(total)
    for copy in exchange:
        copy.wait_recv()
    quarter = proj.shape[1]
    for block in range(seq_count):
        for k in range(seq_count):
            columns = proj_mine[k].reshape(-1, quarter)
            part[block, :, k * quarter : (k + 1) * quarter] = dot(
                merged[block * rows : (block + 1) * rows, :], columns
            ).astype(LOW)

    first = link.send(part.at[far], arrived.at[0], core)
    second = link.send(part.at[sibling], arrived.at[1], core)
    first.wait_recv()
    summed[...] = (part[across].astype(F32) + arrived[0].astype(F32)).astype(LOW)
    third = link.send(summed, across_in, over_x)
    second.wait_recv()
    hidden[...] = tokens[...].astype(F32) + (part[me].astype(F32) + arrived[1].astype(F32))
    pump(2)
    third.wait_recv()
    total = hidden[...] + across_in[...].astype(F32)
    hidden[...] = total
    mids[0] = (total * inverse_rms(total) * vectors[1:2, :width]).astype(LOW)
    for _ in plane_gather(link, mids, ids):
        pass
    exchanged = [exchange_rows(0, first_all, first_rows)]
    pump()
    next(gather_cots)
    exchanged.append(exchange_rows(1, second_all, second_rows))
    for kept, *sent in exchanged:
        kept.wait()
        for copy in sent:
            copy.wait_recv()
    link.finish()


def opening(tokens, cotangent, qkv, proj, ff_first, ff_second, tables, segments, sizes):
    owned, vector_size, per_dev, group, line = sizes
    rows, width = tokens.shape
    block = (rows, width)
    seq_len = 4 * rows
    cols = qkv.shape[1]
    heads = (seq_len, HD)
    vmem, hbm = (pl.BlockSpec(memory_space=pltpu.VMEM), pl.BlockSpec(memory_space=pl.ANY))

    def like(*shape, dtype=LOW):
        return jax.ShapeDtypeStruct(shape, dtype)

    outs = [
        (like(4, *block), vmem),
        (like(line, 2, *qkv.shape), vmem),
        (like(4, group, 2, *proj.shape), vmem),
        (like(line, *ff_first.shape), hbm),
        (like(line, *ff_second.shape), hbm),
        (like(4, group, *ff_first.shape[1:]), vmem),
        (like(4, group, *ff_second.shape[1:]), vmem),
        (like(4, *block), vmem),
        (like(per_dev, *heads), vmem),
        (like(*heads), vmem),
        (like(*heads), vmem),
        (like(seq_len, per_dev * HD), vmem),
        (like(per_dev, seq_len, 1, dtype=F32), vmem),
        (like(*block, dtype=F32), vmem),
        (like(8, *block), vmem),
        (like(8, *block), vmem),
    ]
    copies = 10 * line + 40
    return pl.pallas_call(
        functools.partial(opening_kernel, (owned, vector_size, per_dev, group)),
        out_shape=[shape for shape, _ in outs],
        in_specs=[vmem] * 10,
        out_specs=[place for _, place in outs],
        scratch_shapes=[
            pltpu.VMEM((line, 2, *proj.shape), LOW),
            pltpu.VMEM((width, cols), LOW),
            pltpu.VMEM((3, max(width, 2048)), F32),
            pltpu.VMEM((2, *heads), LOW),
            pltpu.VMEM((4, *block), LOW),
            pltpu.VMEM((2, *block), LOW),
            pltpu.VMEM(block, LOW),
            pltpu.VMEM(block, LOW),
            pltpu.SemaphoreType.DMA((copies,)),
            pltpu.SemaphoreType.DMA((copies,)),
            pltpu.SemaphoreType.DMA((6,)),
        ],
        compiler_params=pltpu.CompilerParams(
            collective_id=0, has_side_effects=True, vmem_limit_bytes=56 << 20
        ),
    )(tokens, cotangent, qkv, proj, ff_first, ff_second, *tables, *segments)


def return_kernel(
    part,
    hidden,
    upstream,
    gain,
    grad_hidden,
    gain_term,
    gathered,
    arrived,
    held,
    from_x,
    from_y,
    corner,
    send_sems,
    recv_sems,
):
    (me, _, across), (core, over_x, over_y) = neighbours()
    rows = hidden.shape[0]
    low, high = (pl.ds(0, rows // 2), pl.ds(rows // 2, rows // 2))
    greet((core, over_x, over_y))
    link = Sender(send_sems, recv_sems)
    halved = {k: link.send(part.at[k + 1], arrived.at[k // 2], core) for k in (6, 2, 4, 0)}

    def chip_sum(k):
        halved[k].wait_recv()
        return part[k].astype(F32) + arrived[k // 2].astype(F32)

    held[2] = chip_sum(6).astype(LOW)
    turn_y = link.send(held.at[2, low], corner.at[0], over_x)
    turn_x = link.send(held.at[2, high], corner.at[1], over_y)
    held[0] = chip_sum(2).astype(LOW)
    direct_x = link.send(held.at[0, low], from_x.at[low], over_x)
    held[1] = chip_sum(4).astype(LOW)
    direct_y = link.send(held.at[1, high], from_y.at[high], over_y)
    grad_hidden[...] = chip_sum(0)
    turn_x.wait_recv()
    held[0, high] = (held[0, high].astype(F32) + corner[1].astype(F32)).astype(LOW)
    late_x = link.send(held.at[0, high], from_x.at[high], over_x)
    turn_y.wait_recv()
    held[1, low] = (held[1, low].astype(F32) + corner[0].astype(F32)).astype(LOW)
    late_y = link.send(held.at[1, low], from_y.at[low], over_y)
    for copy in (direct_x, direct_y, late_x, late_y):
        copy.wait_recv()
    grad_mid = grad_hidden[...] + from_x[...].astype(F32) + from_y[...].astype(F32)
    through, term = norm_back(hidden[...], inverse_rms(hidden[...]), gain[...], grad_mid)
    gain_term[...] = term[None]
    total = upstream[...].astype(F32) + through
    grad_hidden[...] = total
    gathered[me] = total.astype(LOW)
    to_core = link.send(gathered.at[me], gathered.at[me], core)
    to_x = [link.send(gathered.at[me, half], gathered.at[me, half], over_x) for half in (low, high)]
    last = [to_core]
    for copy, half in zip(to_x, (low, high)):
        copy.wait_recv()
        last.append(link.send(gathered.at[across, half], gathered.at[across, half], core))
    for copy in last:
        copy.wait_recv()
    link.finish()


def return_call(part, hidden, upstream, gain):
    _, rows, width = part.shape
    block = (rows, width)
    return whole_call(
        return_kernel,
        [
            jax.ShapeDtypeStruct(block, F32),
            jax.ShapeDtypeStruct((1, width), F32),
            jax.ShapeDtypeStruct((4, *block), LOW),
        ],
        [
            pltpu.VMEM((4, *block), LOW),
            pltpu.VMEM((3, *block), LOW),
            pltpu.VMEM(block, LOW),
            pltpu.VMEM(block, LOW),
            pltpu.VMEM((2, rows // 2, width), LOW),
        ],
        15,
        2,
        (part, hidden, upstream, gain),
    )


def columns_kernel(place, *refs):
    *pieces, out = refs
    row = 0
    for piece in pieces:
        count, rows, quarter = piece.shape
        for k in range(count):
            here = place[0] + k - 2 * ((place[0] % 2) * (k % 2)) - 4 * (
                (place[0] // 2 % 2) * (k // 2 % 2)
            )
            out[pl.ds(row, rows), pl.ds(k * quarter, quarter)] = piece[here].astype(F32)
        row += rows


def columns_call(place, pieces):
    rows = sum(piece.shape[1] for piece in pieces)
    width = pieces[0].shape[0] * pieces[0].shape[2]
    return pl.pallas_call(
        columns_kernel,
        out_shape=jax.ShapeDtypeStruct((rows, width), F32),
        in_specs=[pl.BlockSpec(memory_space=pltpu.SMEM)]
        + [pl.BlockSpec(memory_space=pltpu.VMEM)] * len(pieces),
        out_specs=pl.BlockSpec(memory_space=pltpu.VMEM),
        compiler_params=pltpu.CompilerParams(vmem_limit_bytes=40 << 20),
    )(place, *pieces)


def down_kernel(fold, place, *refs):
    *pieces, out = refs
    row = 0
    for piece in pieces:
        count, owned, width = piece.shape
        span = width // fold
        for k in range(count):
            here = place[0] + k - 2 * ((place[0] % 2) * (k % 2)) - 4 * (
                (place[0] // 2 % 2) * (k // 2 % 2)
            )
            whole = piece[here].astype(F32)
            for j in range(fold):
                whole_part = whole[:, j * span : (j + 1) * span]
                out[pl.ds(row, span), pl.ds((k * fold + j) * owned, owned)] = whole_part.T
        row += span


def down_call(place, pieces, fold):
    rows = sum(piece.shape[2] // fold for piece in pieces)
    width = pieces[0].shape[0] * pieces[0].shape[1] * fold
    return pl.pallas_call(
        functools.partial(down_kernel, fold),
        out_shape=jax.ShapeDtypeStruct((rows, width), F32),
        in_specs=[pl.BlockSpec(memory_space=pltpu.SMEM)]
        + [pl.BlockSpec(memory_space=pltpu.VMEM)] * len(pieces),
        out_specs=pl.BlockSpec(memory_space=pltpu.VMEM),
        compiler_params=pltpu.CompilerParams(vmem_limit_bytes=40 << 20),
    )(place, *pieces)


def hidden_kernel(cuts, group, place, *refs):
    *pieces, out = refs
    units = cuts[-1][1]
    count = pieces[0].shape[0] // 2
    for k in range(count):
        here = place[0] + k - 2 * ((place[0] % 2) * (k % 2)) - 4 * (
            (place[0] // 2 % 2) * (k // 2 % 2)
        )
        for pair in range(2):
            entry = (pair + place[1] - 2 * pair * place[1]) * count + here
            for part in range(2):
                for member in range(group):
                    first = (((part * count + k) * group + member) * 2 + pair) * units
                    for piece, (low, high) in zip(pieces, cuts):
                        span = high - low
                        at = (part * group + member) * span
                        out[:, first + low : first + high] = piece[entry][
                            :, at : at + span
                        ].astype(F32)


def hidden_call(place, pieces, cuts, group):
    rows = pieces[0].shape[1]
    units = cuts[-1][1]
    width = 2 * 8 * group * units
    step = 16
    return pl.pallas_call(
        functools.partial(hidden_kernel, cuts, group),
        grid=(rows // step,),
        out_shape=jax.ShapeDtypeStruct((rows, width), F32),
        in_specs=[pl.BlockSpec(memory_space=pltpu.SMEM)]
        + [pl.BlockSpec((8, step, piece.shape[2]), lambda i: (0, i, 0)) for piece in pieces],
        out_specs=pl.BlockSpec((step, width), lambda i: (i, 0)),
        compiler_params=pltpu.CompilerParams(vmem_limit_bytes=40 << 20),
    )(place, *pieces)


def local(
    tokens,
    segment_ids,
    attn_gain,
    qkv_weight,
    qkv_bias,
    proj_weight,
    mlp_gain,
    gate_up_weight,
    down_weight,
    cotangent,
):
    seq_count = lax.axis_size("seq")
    fsdp_count = lax.axis_size("fsdp")
    line = fsdp_count // 2
    place = lax.axis_index("seq")
    odd = lax.axis_index("fsdp") % 2 == 1
    tok_rows, width = tokens.shape[1:]
    seq_len = tok_rows * seq_count
    owned = qkv_weight.shape[0]
    owned_hidden = down_weight.shape[0]
    hidden = owned_hidden * fsdp_count
    quarter = width // seq_count
    per_dev = H // seq_count
    head_cols = per_dev * HD
    score_scale = HD ** (-0.5)
    group = line // seq_count
    cut_at = owned_hidden // 2 // 128 * 128
    cuts = [(0, cut_at), (cut_at, owned_hidden)]

    holds_values = place % 2 == 1
    kv_first = (H + KV * (place % 2) + place // 2) * HD
    qkv_own = jnp.concatenate(
        [
            lax.dynamic_slice_in_dim(qkv_weight, place * head_cols, head_cols, 1),
            lax.dynamic_slice_in_dim(qkv_weight, kv_first, HD, 1),
        ],
        axis=1,
    )
    cols = head_cols + HD
    vector = jnp.concatenate([attn_gain, mlp_gain, qkv_bias])
    vector_size = vector.shape[0]
    vector_rows = -(-vector_size // (16 * cols)) * 16
    vector = jnp.pad(vector, (0, vector_rows * cols - vector_size)).reshape(vector_rows, cols)
    proj_cols = lax.dynamic_slice_in_dim(proj_weight, place * quarter, quarter, 1)
    down_cols = lax.dynamic_slice_in_dim(down_weight, place * quarter, quarter, 1)
    ff_all = jnp.stack(
        [
            lax.dynamic_slice_in_dim(
                gate_up_weight,
                first + place * group * 2 * owned_hidden,
                group * 2 * owned_hidden,
                1,
            ).reshape(owned, group, 2, owned_hidden)
            for first in (0, hidden)
        ]
    )
    fold = quarter // owned

    def folded(value):
        return jnp.concatenate(
            [value[..., j * owned : (j + 1) * owned, :] for j in range(fold)], axis=-1
        )

    def unfolded(value):
        span = value.shape[-1] // fold
        return jnp.concatenate(
            [value[..., j * span : (j + 1) * span] for j in range(fold)], axis=-2
        )

    ff_sent = []
    for low, high in cuts:
        ff_part = ff_all[:, :, :, :, low:high]
        by_owner = [
            jnp.concatenate(
                [ff_part[part, :, m, pair] for part in range(2) for m in range(group)], axis=1
            )
            for pair in range(2)
        ]
        ff_sent.append(jnp.stack([*by_owner, folded(jnp.transpose(down_cols[low:high]))]))

    segment_row = segment_ids[0]
    doc_starts = jnp.sum((segment_row[None, :] < segment_row[:, None]).astype(jnp.int32), axis=1)
    places = jnp.arange(seq_len, dtype=jnp.int32) - doc_starts
    inverse = THETA ** (-2.0 * jnp.arange(HD // 2, dtype=F32) / HD)
    angles = places.astype(F32)[:, None] * inverse[None, :]
    angles = jnp.concatenate([angles, angles], axis=-1)
    cosines = jnp.cos(angles)
    sines = jnp.sin(angles)

    signs = jnp.where(jnp.arange(HD) < HD // 2, -1.0, 1.0).astype(F32)
    (
        tokens_all,
        qkv_both,
        proj_mine,
        first_all,
        second_all,
        first_rows,
        second_rows,
        normed_in,
        queries,
        head_keys,
        head_values,
        merged,
        logsum,
        hidden_in,
        mids,
        cots,
    ) = opening(
        tokens[0],
        cotangent[0],
        jnp.concatenate([qkv_own, vector], axis=0),
        lax.dynamic_slice_in_dim(proj_weight, place * quarter, quarter, 1),
        *ff_sent,
        (cosines, sines * signs),
        (segment_row[:, None], segment_row[None]),
        (owned, vector_size, per_dev, group, line),
    )
    qkv_mine = qkv_both[:, :, :owned].reshape(width, cols)
    vectors = qkv_both[:, :, owned:].reshape(fsdp_count, vector_rows * cols)[:, :vector_size]
    gain_one = vectors[:, :owned].reshape(width).astype(F32)
    gain_two = vectors[:, owned : 2 * owned].reshape(width).astype(F32)
    proj_mine = jnp.moveaxis(proj_mine.reshape(seq_count, head_cols, quarter), 0, 1)
    proj_mine = proj_mine.reshape(head_cols, width)
    normed_in = normed_in.reshape(seq_len, width)
    resid = tokens[0].astype(F32)
    resid_all = tokens_all.reshape(seq_len, width).astype(F32)
    factor_all = inverse_rms(resid_all)
    mids = mids.reshape(2 * seq_len, width)
    cots = cots.reshape(2 * seq_len, width)
    gate_up_mine = [whole[:, :2].reshape(width, -1) for whole in (first_all, second_all)]
    down_mine = [
        jnp.moveaxis(unfolded(whole), 1, 2).reshape(width, -1)
        for whole in (first_rows, second_rows)
    ]
    block_rows = min(512, seq_len)
    blocks = seq_len // block_rows

    def scores_of(index):
        first, last = index * block_rows, (index + 1) * block_rows
        row_index = first + jnp.arange(block_rows, dtype=jnp.int32)
        key_index = jnp.arange(last, dtype=jnp.int32)
        allowed = (key_index[None, :] <= row_index[:, None]) & (
            segment_row[None, :last] == segment_row[first:last, None]
        )
        scores = (
            jnp.einsum(
                "hqd,kd->hqk", queries[:, first:last], head_keys[:last], preferred_element_type=F32
            )
            * score_scale
        )
        return (jnp.where(allowed[None], scores, FLOOR), allowed)

    def plane_reduce(total):
        parts = [total[k * tok_rows : (k + 1) * tok_rows] for k in range(2 * seq_count)]
        away = seq_reduce(parts[seq_count:]).astype(LOW)
        return seq_reduce(parts[:seq_count]) + swap(away, "fsdp", 1).astype(F32)

    outs, grad_mids, terms = [], [], []
    for gate_up_part, down_part in zip(gate_up_mine, down_mine):
        units = down_part.shape[1]
        gate_up = dot(after(mids, *terms[-1:]), gate_up_part)
        gate, upward = gate_up[:, :units], gate_up[:, units:]
        sigmoid_gate = jax.nn.sigmoid(gate)
        act = (gate * sigmoid_gate * upward).astype(LOW)
        grad_act = dot(cots, down_part)
        grad_gate = grad_act * upward * sigmoid_gate * (1.0 + gate * (1.0 - sigmoid_gate))
        grad_up = grad_act * gate * sigmoid_gate
        grad = jnp.concatenate([grad_gate, grad_up], axis=-1).astype(LOW)
        gate_up_term = column_product(mids, grad).astype(LOW).reshape(line, 2, owned, -1)
        down_term = column_product(cots, act).astype(LOW)
        down_term = jnp.moveaxis(down_term.reshape(seq_count, quarter, group, -1), 2, 1)
        down_term = jnp.stack(seq_exchange(down_term)).reshape(line, 1, quarter, -1)
        terms.append(jnp.concatenate([gate_up_term, folded(down_term)], axis=1))
        outs.append(times_transpose(act, down_part))
        grad_mids.append(times_transpose(grad, gate_up_part))
    grad_mid = after(sum(grad_mids).astype(LOW), *terms[-1:])
    grad_mid = grad_mid.reshape(2 * seq_count, tok_rows, width)
    grad_hidden, gain_two_term, grad_attended = return_call(
        grad_mid, hidden_in, cotangent[0], gain_two[None]
    )
    grad_attended = grad_attended.reshape(seq_len, width)
    block_out = (hidden_in + plane_reduce(sum(outs).astype(LOW))).astype(LOW)

    places_here = jnp.stack([place, lax.axis_index("fsdp") % 2]).astype(jnp.int32)
    down_pieces, hidden_pieces, sums = [], [], []
    for term in terms:
        summed = line_reduce(term)
        sums.append(summed)
        kept, given = pick(odd, summed[0], summed[1])
        here = seq_blocks(jnp.stack([kept, summed[2]]))
        hidden_pieces.append(
            jnp.stack([pair[0] for pair in here] + seq_blocks(swap(given, "fsdp", 1)))
        )
        down_pieces.append(jnp.stack([pair[1] for pair in here]))

    proj_term = column_product(merged, grad_attended).astype(LOW)
    grad_merged = times_transpose(grad_attended, proj_mine).astype(LOW)
    grad_heads = grad_merged.reshape(seq_len, per_dev, HD)
    grad_key = jnp.zeros((seq_len, HD), F32)
    grad_value = jnp.zeros((seq_len, HD), F32)
    grad_queries = []
    for index in range(blocks):
        first, last = index * block_rows, (index + 1) * block_rows
        scores, allowed = scores_of(index)
        probs = jnp.where(allowed[None], jnp.exp(scores - logsum[:, first:last]), 0.0)
        grad_block = grad_heads[first:last]
        grad_probs = jnp.einsum(
            "qhd,kd->hqk", grad_block, head_values[:last], preferred_element_type=F32
        )
        inner = jnp.sum(probs * grad_probs, axis=-1, keepdims=True)
        grad_scores = (probs * (grad_probs - inner)).astype(LOW)
        grad_queries.append(
            (
                jnp.einsum(
                    "hqk,kd->qhd", grad_scores, head_keys[:last], preferred_element_type=F32
                )
                * score_scale
            ).astype(LOW)
        )
        key_term = (
            jnp.einsum(
                "hqk,hqd->kd", grad_scores, queries[:, first:last], preferred_element_type=F32
            )
            * score_scale
        )
        value_term = jnp.einsum(
            "hqk,qhd->kd", probs.astype(LOW), grad_block, preferred_element_type=F32
        )
        grad_key = grad_key + jnp.pad(key_term, ((0, seq_len - last), (0, 0)))
        grad_value = grad_value + jnp.pad(value_term, ((0, seq_len - last), (0, 0)))
    kept_kv, given_kv = pick(holds_values, grad_key.astype(LOW), grad_value.astype(LOW))
    grad_kv = kept_kv.astype(F32) + swap(given_kv, "seq", 1).astype(F32)
    grad_q = jnp.concatenate(grad_queries, axis=0).astype(F32)
    grad_rot = jnp.concatenate([grad_q, grad_kv[:, None]], axis=1)
    unturned = grad_rot * cosines[:, None] + turned_back(grad_rot * sines[:, None])
    grad_projected = (
        jnp.concatenate(
            [
                unturned[:, :per_dev],
                jnp.where(holds_values, grad_kv[:, None], unturned[:, per_dev:]),
            ],
            axis=1,
        )
        .reshape(seq_len, cols)
        .astype(LOW)
    )
    grad_projected = after(grad_projected, sums[-1], hidden_pieces[0], down_pieces[0])
    bias_part = jnp.sum(grad_projected.astype(F32), axis=0)
    grad_in_part = times_transpose(grad_projected, qkv_mine)
    gain_one_part = jnp.sum(grad_in_part * resid_all * factor_all, axis=0)
    grad_in = seq_reduce(relative(grad_in_part.astype(LOW)))
    qkv_term = column_product(normed_in, grad_projected).astype(LOW)
    through_one, _ = norm_back(resid, inverse_rms(resid), gain_one, grad_in)
    tokens_grad = grad_hidden + through_one

    def pair_sum(value):
        kept_rows, given_rows = pick(odd, value[:, 0], value[:, 1])
        arrived = swap(given_rows, "fsdp", 1)
        return (kept_rows.astype(F32) + arrived.astype(F32)).astype(LOW)

    def col_exchange(value):
        rows = value.shape[0]
        cut = jnp.stack([value[:, k * quarter : (k + 1) * quarter] for k in range(seq_count)])
        return jnp.stack(seq_exchange(cut)).reshape(line, rows // group, quarter)

    down_grad = down_call(places_here, down_pieces, fold)
    gate_up_grad = hidden_call(places_here, hidden_pieces, cuts, group)
    proj_sum = pair_sum(proj_term.reshape(group, 2, owned, width)).reshape(group * owned, width)
    proj_sum = col_exchange(proj_sum)

    bias_term = jnp.zeros(qkv_weight.shape[1], F32)
    bias_term = lax.dynamic_update_slice_in_dim(
        bias_term, bias_part[:head_cols], place * head_cols, 0
    )
    bias_term = lax.dynamic_update_slice_in_dim(bias_term, bias_part[head_cols:], kv_first, 0)
    vector_terms = jnp.concatenate(
        [term.reshape(fsdp_count, -1) for term in (gain_one_part, gain_two_term, bias_term)],
        axis=1,
    )
    vector_terms = jnp.pad(vector_terms, ((0, 0), (0, vector_rows * cols - vector_size)))
    qkv_packed = jnp.concatenate(
        [
            qkv_term.reshape(line, 2, owned, cols),
            vector_terms.astype(LOW).reshape(line, 2, vector_rows, cols),
        ],
        axis=2,
    )
    qkv_packed = pair_sum(qkv_packed)
    proj_sum = jnp.pad(proj_sum, ((0, 0), (0, vector_rows), (0, 0)))
    attn_sums = seq_blocks(line_reduce(jnp.concatenate([qkv_packed, proj_sum], axis=-1)))
    proj_grad = columns_call(
        places_here, [jnp.stack([part[:owned, cols:] for part in attn_sums])]
    )
    qkv_sums = in_order([part[:, :cols] for part in attn_sums])
    qkv_grad = jnp.concatenate(
        [part[:owned, :head_cols] for part in qkv_sums]
        + [part[:owned, head_cols:] for part in qkv_sums[0::2]]
        + [part[:owned, head_cols:] for part in qkv_sums[1::2]],
        axis=-1,
    ).astype(F32)
    vector_sum = sum(part[owned:].astype(F32) for part in qkv_sums).reshape(-1)
    return (
        block_out[None],
        tokens_grad[None],
        vector_sum[:owned],
        qkv_grad,
        vector_sum[2 * owned : vector_size],
        proj_grad,
        vector_sum[owned : 2 * owned],
        gate_up_grad,
        down_grad,
    )


def solution(mesh):
    in_specs = (
        P("fsdp", "seq", None),
        P("fsdp", None),
        P("fsdp"),
        P("fsdp", None),
        P("fsdp"),
        P("fsdp", None),
        P("fsdp"),
        P("fsdp", None),
        P("fsdp", None),
        P("fsdp", "seq", None),
    )
    out_specs = (
        P("fsdp", "seq", None),
        P("fsdp", "seq", None),
        P("fsdp"),
        P("fsdp", None),
        P("fsdp"),
        P("fsdp", None),
        P("fsdp"),
        P("fsdp", None),
        P("fsdp", None),
    )
    return jax.shard_map(local, mesh=mesh, in_specs=in_specs, out_specs=out_specs, check_vma=False)
```

time: 1120 us -> 758 us (0.68)
  waiting for transfers between devices: 620 us -> 105 us
  Pallas kernels: 0 us -> 311 us
  blocking collectives: 96.3 us -> 0 us
  local copies, waits for them, and re-layouts: 113 us -> 79.4 us
    pallas_call x0 -> x5, Pallas kernels: none -> 311 us  [the longest x1 243 us: opening(): pl.pallas_call(functools.partial(opening_kernel, (owned, vector_size, per...]
    all_gather x10 -> x0, waiting for transfers between devices: 258 us -> none  [the longest x6 109 us: seq_gather(): return lax.all_gather(value, 'seq', axis=0, tiled=True)]
    ppermute x24 -> x36, waiting for transfers between devices: 237 us -> 105 us  [swap(): lax.ppermute(value, axis, [(i, i ^ distance) for i in range(lax.axis_size...]
    reduce_scatter x4 -> x3, waiting for transfers between devices: 72 us -> 0.01 us  [line_reduce(): lax.psum_scatter(value, 'fsdp', scatter_dimension=0, axis_index_groups=li...]
    all_gather x4 -> x0, blocking collectives: 56.6 us -> none  [the longest x2 39.9 us: line_gather(): lax.all_gather(value, 'fsdp', axis=0, axis_index_groups=lines(), tiled=Fa...]
    reduce_scatter x6 -> x0, waiting for transfers between devices: 51 us -> none  [seq_reduce(): return lax.psum_scatter(value, 'seq', scatter_dimension=0, tiled=True)]
    psum x1 -> x0, blocking collectives: 39.7 us -> none  [local(): lax.psum(jnp.concatenate([gain_one_term, gain_two_term, bias_term]), ('se...]
    reshape x4, local copies, waits for them, and re-layouts: 20.8 us -> 2.55 us  [the longest x1 2.37 us: local(): proj_mine.reshape(seq_count, head_cols, quarter)]
  transfers between devices with their start and end apart: 44 -> 39, of which waited for: 29 -> 12; matrix products, arithmetic and copies ran while one was open for 22% -> 29% of each run, Pallas kernels for 0% -> 9%
where the time goes in v2:
time: 758 us; the launch traced here: 751 us
  Pallas kernels  311 us (41%)
  matrix products  149 us (20%)
  waiting for transfers between devices  105 us (14%)
  local copies, waits for them, and re-layouts  79.4 us (10%)
  other arithmetic  67.7 us (9%)
  starting transfers between devices  22.5 us (3%)
  between operations  15.4 us (2%)
    pallas_call x1, Pallas kernels, opening(): pl.pallas_call(functools.partial(opening_kernel, (owned, vector_size, per...  243 us
    ppermute x36, waiting for transfers between devices, swap(): lax.ppermute(value, axis, [(i, i ^ distance) for i in range(lax.axis_size...  105 us
    dot_general x6, matrix products, times_transpose(): lax.dot_general(left, right, (((1,), (1,)), ((), ())), preferred_element_...  55.7 us
    pallas_call x1, Pallas kernels, whole_call(): pl.pallas_call(kernel, out_shape=out_shapes, in_specs=[pl.BlockSpec(memor...  52.2 us
    dot_general x4, matrix products, dot(): return jnp.dot(left, right, preferred_element_type=F32)  43.9 us
    dot_general x6, matrix products, column_product(): lax.dot_general(left, right, (((0,), (0,)), ((), ())), preferred_element_...  38 us
    unnamed x163, local copies, waits for them, and re-layouts  23.4 us
    ppermute x36, starting transfers between devices, swap(): lax.ppermute(value, axis, [(i, i ^ distance) for i in range(lax.axis_size...  22.2 us
  transfers between devices with their start and end apart: 39, of which 12 were waited for; matrix products, arithmetic and copies ran while one was open for 29% of the time, Pallas kernels for 9%

profile of v2, /device:TPU:0, one launch (start us, length us, event | category | flops | bytes accessed | tf_op | source)
XLA Modules:
  0.0 750.7 jit_solution(3553514134284304266)
XLA Ops:
  22.5 3.3 fusion.68
  31.2 242.6 %shard_map.169 = (bf16[4,256,1536]{2,1,0:T(8,128)(2,1)}, bf16[4,2,208,512]{3,2,1,0:T(8,128)(2,1)}, bf16[4,1,2,192,384]{4,3,2,1,0:T(8,128)(2,1)}, bf16[4,3,192,10...) custom-call(bf16[256,1536]{1,0:T(8,128)(2,1)} %bitcast.386, ...), custom_call_target="tpu_custom_call" | custom-call | tf_op jit(solution)/shard_map/pallas_call | solution.py:475
  278.3 9.1 %fusion.119 = f32[2048,1024]{0,1:T(8,128)} fusion(bf16[2048,1536]{1,0:T(8,128)(2,1)S(1)} %bitcast.439, bf16[1536,1024]{1,0:T(8,128)(2,1)S(1)} %bitcast.404), kind=kOutput, calls=%fused_computation.322 | convolution fusion | flops 6442450944 | bytes 17825792 | tf_op jit(solution)/shard_map/dot_general | solution.py:44
  287.4 9.1 %multiply_convert_fusion.4 = (bf16[2048,512]{0,1:T(8,128)(2,1)}, bf16[2048,512]{0,1:T(8,128)(2,1)}, bf16[2048,512]{0,1:T(8,128)(2,1)S(1)}) fusion(f32[2048,1024]{0,1:T(8,128)} %fusion.119, bf16[2048,1536]{1,0:T(8,128)(2,1)S(1)} %bitcast.446, bf16[1536,512]{1,0:T(8,128)(2,1)S(1)} %bitcast.413), kind=kOutput, calls=%fused_computation.23 | convolution fusion | flops 3238002688 | bytes 22544384 | tf_op jit(solution)/shard_map/dot_general | solution.py:44
  297.9 3.6 convolution_convert_fusion.4
  304.6 10.5 %fusion.120 = f32[2048,1536]{1,0:T(8,128)} fusion(bf16[2048,512]{0,1:T(8,128)(2,1)} %copy-done.62, bf16[1536,512]{1,0:T(8,128)(2,1)} %bitcast.414), kind=kOutput, calls=%fused_computation.323 | convolution fusion | flops 3221225472 | bytes 16252928 | tf_op jit(solution)/shard_map/dot_general | solution.py:52
  320.6 11.7 %convolution_convert_fusion.1 = bf16[1536,1024]{1,0:T(8,128)(2,1)} fusion(bf16[2048,1536]{1,0:T(8,128)(2,1)} %bitcast.435, bf16[2048,512]{0,1:T(8,128)(2,1)} %get-tuple-element.64, bf16[2048,512]{0,1:T(8,128)(2,1)S(1)} %copy-done.63), kind=kOutput, calls=%fused_computation.27 | convolution fusion | flops 6452412416 | bytes 13631488 | tf_op jit(solution)/shard_map/dot_general | solution.py:48
  340.8 4.4 slice.400
  354.1 14.2 %fusion.121 = f32[2048,1216]{0,1:T(8,128)} fusion(bf16[2048,1536]{1,0:T(8,128)(2,1)} %bitcast.436, bf16[1536,1216]{1,0:T(8,128)(2,1)} %bitcast.398), kind=kOutput, calls=%fused_computation.324 | convolution fusion | flops 7650410496 | bytes 19988480 | tf_op jit(solution)/shard_map/dot_general | solution.py:44
  368.3 11.5 %multiply_convert_fusion.1 = (bf16[2048,608]{0,1:T(8,128)(2,1)}, bf16[2048,608]{0,1:T(8,128)(2,1)}, bf16[2048,608]{0,1:T(8,128)(2,1)S(1)}) fusion(f32[2048,1216]{0,1:T(8,128)} %fusion.121, bf16[2048,1536]{1,0:T(8,128)(2,1)} %bitcast.443, bf16[1536,608]{1,0:T(8,128)(2,1)S(1)} %bitcast.407), kind=kOutput, calls=%fused_computation.17 | convolution fusion | flops 3845128192 | bytes 25591808 | tf_op jit(solution)/shard_map/dot_general | solution.py:44
  379.8 10.0 %add_convert_fusion.1 = bf16[2048,1536]{1,0:T(8,128)(2,1)} fusion(f32[2048,1536]{1,0:T(8,128)} %fusion.120, bf16[2048,608]{0,1:T(8,128)(2,1)S(1)} %get-tuple-element.65, bf16[1536,608]{1,0:T(8,128)(2,1)S(1)} %bitcast.408), kind=kOutput, calls=%fused_computation.1 | convolution fusion | flops 3831496704 | bytes 23232512 | tf_op jit(solution)/shard_map/dot_general | solution.py:52
  389.8 5.2 convolution_convert_fusion.2
  406.1 13.6 %fusion.6 = f32[2048,1536]{1,0:T(8,128)} fusion(bf16[1536,1216]{1,0:T(8,128)(2,1)S(1)} %bitcast.399, bf16[2048,608]{0,1:T(8,128)(2,1)} %get-tuple-element.62, bf16[2048,608]{0,1:T(8,128)(2,1)} %get-tuple-element.61), kind=kOutput, calls=%fused_computation.28 | convolution fusion | flops 7660371968 | bytes 21299200 | tf_op jit(solution)/shard_map/dot_general | solution.py:52
  419.8 13.2 %add_convert_fusion = bf16[2048,1536]{1,0:T(8,128)(2,1)} fusion(f32[2048,1536]{1,0:T(8,128)} %fusion.6, bf16[1536,1024]{1,0:T(8,128)(2,1)S(1)} %bitcast.405, bf16[2048,512]{0,1:T(8,128)(2,1)} %get-tuple-element.64, bf16[2048,512]{0,1:T(8,128)(2,1)} %get-tuple-element.63), kind=kOutput, calls=%fused_computation | convolution fusion | flops 6457131008 | bytes 26214400 | tf_op jit(solution)/shard_map/dot_general | solution.py:52
  433.0 12.0 %convolution_convert_fusion = bf16[1536,1216]{0,1:T(8,128)(2,1)} fusion(bf16[2048,1536]{1,0:T(8,128)(2,1)S(1)} %bitcast.442, bf16[2048,608]{0,1:T(8,128)(2,1)} %get-tuple-element.62, bf16[2048,608]{0,1:T(8,128)(2,1)} %get-tuple-element.61), kind=kOutput, calls=%fused_computation.2 | convolution fusion | flops 7662239744 | bytes 15007744 | tf_op jit(solution)/shard_map/dot_general | solution.py:48
  444.9 6.1 copy.89
  454.6 4.2 fusion.5
  463.2 52.2 %shard_map.170 = (f32[256,1536]{1,0:T(8,128)S(1)}, f32[1,1536]{1,0:T(1,128)S(1)}, bf16[4,256,1536]{2,1,0:T(8,128)(2,1)S(1)}) custom-call(bf16[8,256,1536]{2,1,0:T(8,128)(2,1)S(1)} %bitcast.378, f32[256,1536]{1,0:T(8,128)S(1)} %copy-done.3, bf16[256,1536]{1,0:T(8,128)(2,1)S(1)} %bitcast.380, f32[1,1536]{1,0:T(1,128)S(1)} %reshape.497.gain), custom_call_target="tpu_custom_call" | custom-call | tf_op jit(solution)/shard_map/pallas_call | solution.py:161
  522.8 3.8 fusion.2
  530.0 3.8 fusion.4
  545.1 11.1 %collective-permute-done.22 = bf16[1,192,1536]{2,1,0:T(8,128)(2,1)S(1)} collective-permute-done((bf16[1,192,1536]{2,1,0:T(8,128)(2,1)}, bf16[1,192,1536]{2,1,0:T(8,128)(2,1)S(1)}, u32[]{:S(2)}, u32[]{:S(2)}) %collective-permute-start.22) | collective-permute-done | bytes 589856 | tf_op jit(solution)/shard_map/ppermute | solution.py:56
  557.5 3.4 fusion.24
  569.3 32.2 %collective-permute-done.24 = bf16[192,384]{1,0:T(8,128)(2,1)S(1)} collective-permute-done((bf16[192,384]{1,0:T(8,128)(2,1)S(1)}, bf16[192,384]{1,0:T(8,128)(2,1)S(1)}, u32[]{:S(2)}, u32[]{:S(2)}) %collective-permute-start.24) | collective-permute-done | bytes 147488 | tf_op jit(solution)/shard_map/ppermute | solution.py:56
  609.5 22.5 %collective-permute-done.17 = bf16[192,1024]{1,0:T(8,128)(2,1)S(1)} collective-permute-done((bf16[192,1024]{1,0:T(8,128)(2,1)S(1)}, bf16[192,1024]{1,0:T(8,128)(2,1)S(1)}, u32[]{:S(2)}, u32[]{:S(2)}) %collective-permute-start.17) | collective-permute-done | bytes 393248 | tf_op jit(solution)/shard_map/ppermute | solution.py:56
  636.6 7.0 fusion.1
  643.8 4.2 convolution_convert_fusion.3
  663.0 8.6 %collective-permute-done.21 = bf16[4,208,512]{2,1,0:T(8,128)(2,1)} collective-permute-done((bf16[4,208,512]{2,1,0:T(8,128)(2,1)}, bf16[4,208,512]{2,1,0:T(8,128)(2,1)}, u32[]{:S(2)}, u32[]{:S(2)}) %collective-permute-start.21) | collective-permute-done | bytes 852000 | tf_op jit(solution)/shard_map/ppermute | solution.py:56
  674.3 6.9 collective-permute-done.32
  684.9 10.7 %collective-permute-done.34 = bf16[192,1216]{1,0:T(8,128)(2,1)S(1)} collective-permute-done((bf16[192,1216]{1,0:T(8,128)(2,1)}, bf16[192,1216]{1,0:T(8,128)(2,1)S(1)}, u32[]{:S(2)}, u32[]{:S(2)}) %collective-permute-start.34) | collective-permute-done | bytes 466976 | tf_op jit(solution)/shard_map/ppermute | solution.py:56
  700.7 10.1 %collective-permute-done.20 = bf16[256,1536]{1,0:T(8,128)(2,1)S(1)} collective-permute-done((bf16[256,1536]{1,0:T(8,128)(2,1)S(1)}, bf16[256,1536]{1,0:T(8,128)(2,1)S(1)}, u32[]{:S(2)}, u32[]{:S(2)}) %collective-permute-start.20) | collective-permute-done | bytes 786464 | tf_op jit(solution)/shard_map/ppermute | solution.py:56
  722.8 5.9 shard_map.173
  728.7 8.4 %shard_map.172 = f32[192,17920]{1,0:T(8,128)} custom-call(s32[2]{0:T(128)S(1)} %pad_add_fusion.place, bf16[8,192,1024]{2,1,0:T(8,128)(2,1)S(1)} %copy-done.6, bf16[8,192,1216]{2,1,0:T(8,128)(2,1)S(1)} %copy-done.4), custom_call_target="tpu_custom_call" | custom-call | tf_op jit(solution)/shard_map/pallas_call | solution.py:664
  (389 shorter events, 160.1 us)
Async XLA Ops:
  7.2 554.9 %reduce-scatter.4.cloned.1.call-start = ((), (), s32[]{:S(2)}) async-start(), calls=%async_computation.3 | async-start | bytes 5898240 | tf_op jit(solution)/shard_map/reduce_scatter | solution.py:65
  302.7 44.8 %collective-permute-start.2 = (bf16[1,384,512]{2,1,0:T(8,128)(2,1)}, bf16[1,384,512]{2,1,0:T(8,128)(2,1)S(1)}, u32[]{:S(2)}, u32[]{:S(2)}) collective-permute-start(bf16[1,384,512]{2,1,0:T(8,128)(2,1)} %get-tuple-element.98), channel_id=1, source_target_pairs={{0,8},{8,0},{16,24},{24,16},{1,9},{9,1},{17,25},{25,17},{2,10},{10... | collective-permute-start | bytes 1179656 | tf_op jit(solution)/shard_map/ppermute | solution.py:56
  302.7 44.8 %collective-permute-start.1 = (bf16[1,384,512]{2,1,0:T(8,128)(2,1)}, bf16[1,384,512]{2,1,0:T(8,128)(2,1)S(1)}, u32[]{:S(2)}, u32[]{:S(2)}) collective-permute-start(bf16[1,384,512]{2,1,0:T(8,128)(2,1)} %get-tuple-element.99), channel_id=1, source_target_pairs={{0,16},{8,24},{16,0},{24,8},{1,17},{9,25},{17,1},{25,9},{2,18},{10... | collective-permute-start | bytes 1179656 | tf_op jit(solution)/shard_map/ppermute | solution.py:56
  303.5 44.8 %collective-permute-start = (bf16[1,384,512]{2,1,0:T(8,128)(2,1)}, bf16[1,384,512]{2,1,0:T(8,128)(2,1)}, u32[]{:S(2)}, u32[]{:S(2)}) collective-permute-start(bf16[1,384,512]{2,1,0:T(8,128)(2,1)} %get-tuple-element.100), channel_id=1, source_target_pairs={{0,24},{8,16},{16,8},{24,0},{1,25},{9,17},{17,9},{25,1},{2,26},{10... | collective-permute-start | bytes 1179656 | tf_op jit(solution)/shard_map/ppermute | solution.py:56
  354.0 297.4 %reduce-scatter.8.cloned.1.call-start = ((), (), s32[]{:S(2)}) async-start(), calls=%async_computation.5 | async-start | bytes 7372800 | tf_op jit(solution)/shard_map/reduce_scatter | solution.py:65
  399.1 52.0 %collective-permute-start.10 = (bf16[1,384,608]{2,1,0:T(8,128)(2,1)}, bf16[1,384,608]{2,1,0:T(8,128)(2,1)S(1)}, u32[]{:S(2)}, u32[]{:S(2)}) collective-permute-start(bf16[1,384,608]{2,1,0:T(8,128)(2,1)} %get-tuple-element.91), channel_id=1, source_target_pairs={{0,8},{8,0},{16,24},{24,16},{1,9},{9,1},{17,25},{25,17},{2,10},{10... | collective-permute-start | bytes 1400840 | tf_op jit(solution)/shard_map/ppermute | solution.py:56
  399.4 51.7 %collective-permute-start.9 = (bf16[1,384,608]{2,1,0:T(8,128)(2,1)}, bf16[1,384,608]{2,1,0:T(8,128)(2,1)}, u32[]{:S(2)}, u32[]{:S(2)}) collective-permute-start(bf16[1,384,608]{2,1,0:T(8,128)(2,1)} %get-tuple-element.92), channel_id=1, source_target_pairs={{0,16},{8,24},{16,0},{24,8},{1,17},{9,25},{17,1},{25,9},{2,18},{10... | collective-permute-start | bytes 1400840 | tf_op jit(solution)/shard_map/ppermute | solution.py:56
  400.1 50.9 %collective-permute-start.8 = (bf16[1,384,608]{2,1,0:T(8,128)(2,1)}, bf16[1,384,608]{2,1,0:T(8,128)(2,1)}, u32[]{:S(2)}, u32[]{:S(2)}) collective-permute-start(bf16[1,384,608]{2,1,0:T(8,128)(2,1)} %get-tuple-element.93), channel_id=1, source_target_pairs={{0,24},{8,16},{16,8},{24,0},{1,25},{9,17},{17,9},{25,1},{2,26},{10... | collective-permute-start | bytes 1400840 | tf_op jit(solution)/shard_map/ppermute | solution.py:56
  404.3 153.2 %collective-permute-start.5 = (bf16[2,256,1536]{2,1,0:T(8,128)(2,1)}, bf16[2,256,1536]{2,1,0:T(8,128)(2,1)}, u32[]{:S(2)}, u32[]{:S(2)}) collective-permute-start(bf16[2,256,1536]{2,1,0:T(8,128)(2,1)} %pad_maximum_fusion.14), channel_id=1, source_target_pairs={{0,8},{8,0},{16,24},{24,16},{1,9},{9,1},{17,25},{25,17},{2,10},{10... | collective-permute-start | bytes 4718600 | tf_op jit(solution)/shard_map/ppermute | solution.py:56
  406.1 151.4 %collective-permute-start.3 = (bf16[2,256,1536]{2,1,0:T(8,128)(2,1)}, bf16[2,256,1536]{2,1,0:T(8,128)(2,1)}, u32[]{:S(2)}, u32[]{:S(2)}) collective-permute-start(bf16[2,256,1536]{2,1,0:T(8,128)(2,1)} %pad_maximum_fusion.13), channel_id=1, source_target_pairs={{0,8},{8,0},{16,24},{24,16},{1,9},{9,1},{17,25},{25,17},{2,10},{10... | collective-permute-start | bytes 4718600 | tf_op jit(solution)/shard_map/ppermute | solution.py:56
  458.8 262.0 %reduce-scatter.6.cloned.1.call-start = ((), (), s32[]{:S(2)}) async-start(), calls=%async_computation.4 | async-start | bytes 1863680 | tf_op jit(solution)/shard_map/reduce_scatter | solution.py:65
  540.7 15.6 %collective-permute-start.22 = (bf16[1,192,1536]{2,1,0:T(8,128)(2,1)}, bf16[1,192,1536]{2,1,0:T(8,128)(2,1)S(1)}, u32[]{:S(2)}, u32[]{:S(2)}) collective-permute-start(bf16[1,192,1536]{2,1,0:T(8,128)(2,1)} %select_bitcast_fusion.1), channel_id=1, source_target_pairs={{0,1},{1,0},{2,3},{3,2},{4,5},{5,4},{6,7},{7,6},{8,9},{9,8},{10,11... | collective-permute-start | bytes 1769480 | tf_op jit(solution)/shard_map/ppermute | solution.py:56
  560.9 44.5 %collective-permute-start.6 = (bf16[256,1536]{1,0:T(8,128)(2,1)}, bf16[256,1536]{1,0:T(8,128)(2,1)}, u32[]{:S(2)}, u32[]{:S(2)}) collective-permute-start(bf16[256,1536]{1,0:T(8,128)(2,1)} %get-tuple-element.72), channel_id=1, source_target_pairs={{0,16},{8,24},{16,0},{24,8},{1,17},{9,25},{17,1},{25,9},{2,18},{10... | collective-permute-start | bytes 2359304 | tf_op jit(solution)/shard_map/ppermute | solution.py:56
  564.9 40.1 %collective-permute-start.13 = (bf16[2,192,1024]{2,1,0:T(8,128)(2,1)S(1)}, bf16[2,192,1024]{2,1,0:T(8,128)(2,1)S(1)}, u32[]{:S(2)}, u32[]{:S(2)}) collective-permute-start(bf16[2,192,1024]{2,1,0:T(8,128)(2,1)S(1)} %pad_maximum_fusion.23), channel_id=1, source_target_pairs={{0,16},{8,24},{16,0},{24,8},{1,17},{9,25},{17,1},{25,9},{2,18},{10... | collective-permute-start | bytes 2359304 | tf_op jit(solution)/shard_map/ppermute | solution.py:56
  565.9 35.6 %collective-permute-start.24 = (bf16[192,384]{1,0:T(8,128)(2,1)S(1)}, bf16[192,384]{1,0:T(8,128)(2,1)S(1)}, u32[]{:S(2)}, u32[]{:S(2)}) collective-permute-start(bf16[192,384]{1,0:T(8,128)(2,1)S(1)} %get-tuple-element.138), channel_id=1, source_target_pairs={{0,16},{8,24},{16,0},{24,8},{1,17},{9,25},{17,1},{25,9},{2,18},{10... | collective-permute-start | bytes 442376 | tf_op jit(solution)/shard_map/ppermute | solution.py:56
  567.2 34.8 %collective-permute-start.23 = (bf16[192,384]{1,0:T(8,128)(2,1)S(1)}, bf16[192,384]{1,0:T(8,128)(2,1)S(1)}, u32[]{:S(2)}, u32[]{:S(2)}) collective-permute-start(bf16[192,384]{1,0:T(8,128)(2,1)S(1)} %get-tuple-element.139), channel_id=1, source_target_pairs={{0,24},{8,16},{16,8},{24,0},{1,25},{9,17},{17,9},{25,1},{2,26},{10... | collective-permute-start | bytes 442376 | tf_op jit(solution)/shard_map/ppermute | solution.py:56
  567.9 36.0 %collective-permute-start.15 = (bf16[192,1024]{1,0:T(8,128)(2,1)S(1)}, bf16[192,1024]{1,0:T(8,128)(2,1)S(1)}, u32[]{:S(2)}, u32[]{:S(2)}) collective-permute-start(bf16[192,1024]{1,0:T(8,128)(2,1)S(1)} %get-tuple-element.109), channel_id=1, source_target_pairs={{0,1},{1,0},{2,3},{3,2},{4,5},{5,4},{6,7},{7,6},{8,9},{9,8},{10,11... | collective-permute-start | bytes 1179656 | tf_op jit(solution)/shard_map/ppermute | solution.py:56
  601.5 30.6 %collective-permute-start.12 = (bf16[2,192,1024]{2,1,0:T(8,128)(2,1)S(1)}, bf16[2,192,1024]{2,1,0:T(8,128)(2,1)S(1)}, u32[]{:S(2)}, u32[]{:S(2)}) collective-permute-start(bf16[2,192,1024]{2,1,0:T(8,128)(2,1)S(1)} %pad_maximum_fusion.23), channel_id=1, source_target_pairs={{0,8},{8,0},{16,24},{24,16},{1,9},{9,1},{17,25},{25,17},{2,10},{10... | collective-permute-start | bytes 2359304 | tf_op jit(solution)/shard_map/ppermute | solution.py:56
  602.9 55.8 %collective-permute-start.4 = (bf16[256,1536]{1,0:T(8,128)(2,1)}, bf16[256,1536]{1,0:T(8,128)(2,1)}, u32[]{:S(2)}, u32[]{:S(2)}) collective-permute-start(bf16[256,1536]{1,0:T(8,128)(2,1)} %get-tuple-element.71), channel_id=1, source_target_pairs={{0,16},{8,24},{16,0},{24,8},{1,17},{9,25},{17,1},{25,9},{2,18},{10... | collective-permute-start | bytes 2359304 | tf_op jit(solution)/shard_map/ppermute | solution.py:56
  603.9 28.1 %collective-permute-start.17 = (bf16[192,1024]{1,0:T(8,128)(2,1)S(1)}, bf16[192,1024]{1,0:T(8,128)(2,1)S(1)}, u32[]{:S(2)}, u32[]{:S(2)}) collective-permute-start(bf16[192,1024]{1,0:T(8,128)(2,1)S(1)} %collective-permute-done.15), channel_id=1, source_target_pairs={{0,16},{8,24},{16,0},{24,8},{1,17},{9,25},{17,1},{25,9},{2,18},{10... | collective-permute-start | bytes 1179656 | tf_op jit(solution)/shard_map/ppermute | solution.py:56
  605.0 27.6 %collective-permute-start.14 = (bf16[2,192,1024]{2,1,0:T(8,128)(2,1)S(1)}, bf16[2,192,1024]{2,1,0:T(8,128)(2,1)S(1)}, u32[]{:S(2)}, u32[]{:S(2)}) collective-permute-start(bf16[2,192,1024]{2,1,0:T(8,128)(2,1)S(1)} %collective-permute-done.13), channel_id=1, source_target_pairs={{0,8},{8,0},{16,24},{24,16},{1,9},{9,1},{17,25},{25,17},{2,10},{10... | collective-permute-start | bytes 2359304 | tf_op jit(solution)/shard_map/ppermute | solution.py:56
  608.2 50.8 %collective-permute-start.7 = (bf16[256,1536]{1,0:T(8,128)(2,1)}, bf16[256,1536]{1,0:T(8,128)(2,1)}, u32[]{:S(2)}, u32[]{:S(2)}) collective-permute-start(bf16[256,1536]{1,0:T(8,128)(2,1)} %fusion.23), channel_id=1, source_target_pairs={{0,1},{1,0},{2,3},{3,2},{4,5},{5,4},{6,7},{7,6},{8,9},{9,8},{10,11... | collective-permute-start | bytes 2359304 | tf_op jit(solution)/shard_map/ppermute | solution.py:56
  649.4 22.1 %collective-permute-start.21 = (bf16[4,208,512]{2,1,0:T(8,128)(2,1)}, bf16[4,208,512]{2,1,0:T(8,128)(2,1)}, u32[]{:S(2)}, u32[]{:S(2)}) collective-permute-start(bf16[4,208,512]{2,1,0:T(8,128)(2,1)} %select_bitcast_fusion), channel_id=1, source_target_pairs={{0,1},{1,0},{2,3},{3,2},{4,5},{5,4},{6,7},{7,6},{8,9},{9,8},{10,11... | collective-permute-start | bytes 2555912 | tf_op jit(solution)/shard_map/ppermute | solution.py:56
  651.4 30.5 %collective-permute-start.19 = (bf16[2,256,1536]{2,1,0:T(8,128)(2,1)}, bf16[2,256,1536]{2,1,0:T(8,128)(2,1)}, u32[]{:S(2)}, u32[]{:S(2)}) collective-permute-start(bf16[2,256,1536]{2,1,0:T(8,128)(2,1)} %pad_maximum_fusion.16), channel_id=1, source_target_pairs={{0,8},{8,0},{16,24},{24,16},{1,9},{9,1},{17,25},{25,17},{2,10},{10... | collective-permute-start | bytes 4718600 | tf_op jit(solution)/shard_map/ppermute | solution.py:56
  657.5 38.1 %collective-permute-start.30 = (bf16[2,192,1216]{2,1,0:T(8,128)(2,1)}, bf16[2,192,1216]{2,1,0:T(8,128)(2,1)}, u32[]{:S(2)}, u32[]{:S(2)}) collective-permute-start(bf16[2,192,1216]{2,1,0:T(8,128)(2,1)} %pad_maximum_fusion.21), channel_id=1, source_target_pairs={{0,16},{8,24},{16,0},{24,8},{1,17},{9,25},{17,1},{25,9},{2,18},{10... | collective-permute-start | bytes 2801672 | tf_op jit(solution)/shard_map/ppermute | solution.py:56
  658.8 37.4 %collective-permute-start.29 = (bf16[2,192,1216]{2,1,0:T(8,128)(2,1)}, bf16[2,192,1216]{2,1,0:T(8,128)(2,1)}, u32[]{:S(2)}, u32[]{:S(2)}) collective-permute-start(bf16[2,192,1216]{2,1,0:T(8,128)(2,1)} %pad_maximum_fusion.21), channel_id=1, source_target_pairs={{0,8},{8,0},{16,24},{24,16},{1,9},{9,1},{17,25},{25,17},{2,10},{10... | collective-permute-start | bytes 2801672 | tf_op jit(solution)/shard_map/ppermute | solution.py:56
  659.0 22.3 %collective-permute-start.32 = (bf16[192,1216]{1,0:T(8,128)(2,1)}, bf16[192,1216]{1,0:T(8,128)(2,1)}, u32[]{:S(2)}, u32[]{:S(2)}) collective-permute-start(bf16[192,1216]{1,0:T(8,128)(2,1)} %get-tuple-element.107), channel_id=1, source_target_pairs={{0,1},{1,0},{2,3},{3,2},{4,5},{5,4},{6,7},{7,6},{8,9},{9,8},{10,11... | collective-permute-start | bytes 1400840 | tf_op jit(solution)/shard_map/ppermute | solution.py:56
  681.8 36.6 %collective-permute-start.33 = (bf16[192,1216]{1,0:T(8,128)(2,1)}, bf16[192,1216]{1,0:T(8,128)(2,1)S(1)}, u32[]{:S(2)}, u32[]{:S(2)}) collective-permute-start(bf16[192,1216]{1,0:T(8,128)(2,1)} %collective-permute-done.32), channel_id=1, source_target_pairs={{0,8},{8,0},{16,24},{24,16},{1,9},{9,1},{17,25},{25,17},{2,10},{10... | collective-permute-start | bytes 1400840 | tf_op jit(solution)/shard_map/ppermute | solution.py:56
  683.4 27.3 %collective-permute-start.20 = (bf16[256,1536]{1,0:T(8,128)(2,1)S(1)}, bf16[256,1536]{1,0:T(8,128)(2,1)S(1)}, u32[]{:S(2)}, u32[]{:S(2)}) collective-permute-start(bf16[256,1536]{1,0:T(8,128)(2,1)S(1)} %fusion.61), channel_id=1, source_target_pairs={{0,16},{8,24},{16,0},{24,8},{1,17},{9,25},{17,1},{25,9},{2,18},{10... | collective-permute-start | bytes 2359304 | tf_op jit(solution)/shard_map/ppermute | solution.py:56
  695.6 24.4 %collective-permute-start.35 = (bf16[192,1216]{1,0:T(8,128)(2,1)S(1)}, bf16[192,1216]{1,0:T(8,128)(2,1)S(1)}, u32[]{:S(2)}, u32[]{:S(2)}) collective-permute-start(bf16[192,1216]{1,0:T(8,128)(2,1)S(1)} %collective-permute-done.34), channel_id=1, source_target_pairs={{0,8},{8,0},{16,24},{24,16},{1,9},{9,1},{17,25},{25,17},{2,10},{10... | collective-permute-start | bytes 1400840 | tf_op jit(solution)/shard_map/ppermute | solution.py:56
  695.6 19.9 %collective-permute-start.31 = (bf16[2,192,1216]{2,1,0:T(8,128)(2,1)}, bf16[2,192,1216]{2,1,0:T(8,128)(2,1)S(1)}, u32[]{:S(2)}, u32[]{:S(2)}) collective-permute-start(bf16[2,192,1216]{2,1,0:T(8,128)(2,1)} %collective-permute-done.30), channel_id=1, source_target_pairs={{0,8},{8,0},{16,24},{24,16},{1,9},{9,1},{17,25},{25,17},{2,10},{10... | collective-permute-start | bytes 2801672 | tf_op jit(solution)/shard_map/ppermute | solution.py:56
  720.8 16.3 %collective-permute-start.26 = (bf16[208,896]{1,0:T(8,128)(2,1)}, bf16[208,896]{1,0:T(8,128)(2,1)S(1)}, u32[]{:S(2)}, u32[]{:S(2)}) collective-permute-start(bf16[208,896]{1,0:T(8,128)(2,1)} %bitcast.422), channel_id=1, source_target_pairs={{0,16},{8,24},{16,0},{24,8},{1,17},{9,25},{17,1},{25,9},{2,18},{10... | collective-permute-start | bytes 1118216 | tf_op jit(solution)/shard_map/ppermute | solution.py:56
  (80 other events, 702.5 us)
Sparse Core Ops, SparseCore 0:
  354.1 85.4 reduce-scatter.3
  459.0 104.7 reduce-scatter.7
  674.4 34.3 reduce-scatter.5

commit v3 on v2

v3 whole, which is shorter than its diff:
```python
import functools

import jax
import jax.numpy as jnp
from jax import lax
from jax.experimental import pallas as pl
from jax.experimental.pallas import tpu as pltpu
from jax.sharding import PartitionSpec as P

H = 12
KV = 2
HD = 128
EPSILON = 1e-06
THETA = 1000000.0
FLOOR = -1e30
LOW = jnp.bfloat16
F32 = jnp.float32


def inverse_rms(value):
    return lax.rsqrt(jnp.mean(value * value, axis=-1, keepdims=True) + EPSILON)


def turned(value):
    halfway = value.shape[-1] // 2
    return jnp.concatenate([-value[..., halfway:], value[..., :halfway]], axis=-1)


def turned_back(value):
    halfway = value.shape[-1] // 2
    return jnp.concatenate([value[..., halfway:], -value[..., :halfway]], axis=-1)


def norm_back(value, factor, gain, upstream):
    weighted = upstream * gain
    gain_term = jnp.sum(upstream * value * factor, axis=0)
    through = factor * weighted - value * factor**3 * jnp.mean(
        weighted * value, axis=-1, keepdims=True
    )
    return (through, gain_term)


def dot(left, right):
    return jnp.dot(left, right, preferred_element_type=F32)


def column_product(left, right):
    return lax.dot_general(left, right, (((0,), (0,)), ((), ())), preferred_element_type=F32)


def times_transpose(left, right):
    return lax.dot_general(left, right, (((1,), (1,)), ((), ())), preferred_element_type=F32)


def swap(value, axis, distance):
    return lax.ppermute(value, axis, [(i, i ^ distance) for i in range(lax.axis_size(axis))])


def lines():
    size = lax.axis_size("fsdp")
    return [list(range(first, size, 2)) for first in range(2)]


def line_gather(value):
    return lax.all_gather(value, "fsdp", axis=0, axis_index_groups=lines(), tiled=False)


def line_reduce(value):
    return lax.psum_scatter(
        value, "fsdp", scatter_dimension=0, axis_index_groups=lines(), tiled=False
    )


def by_pair(own, other):
    second = lax.axis_index("fsdp") % 2 == 1
    return (jnp.where(second, other, own), jnp.where(second, own, other))


def pick(flag, first, second):
    return (jnp.where(flag, second, first), jnp.where(flag, first, second))


def nought(value):
    return jnp.minimum(jnp.abs(value), 0.0).astype(LOW)


def seq_blocks(value):
    across = swap(value, "seq", 2)
    return [value, swap(value, "seq", 1), across, swap(across, "seq", 1)]


def seq_reduce(parts):
    arrived = swap(jnp.stack([parts[1], parts[3]]), "seq", 1)
    across = (parts[2].astype(F32) + arrived[1].astype(F32)).astype(LOW)
    here = parts[0].astype(F32) + arrived[0].astype(F32)
    return here + swap(across, "seq", 2).astype(F32)


def in_order(blocks):
    me = lax.axis_index("seq")
    bits = 1
    while bits < len(blocks):
        flip = (me & bits) != 0
        blocks = [jnp.where(flip, blocks[k ^ bits], blocks[k]) for k in range(len(blocks))]
        bits *= 2
    return blocks


def relative(value):
    size = lax.axis_size("seq")
    me = lax.axis_index("seq")
    cut = value.reshape(size, value.shape[0] // size, *value.shape[1:])
    return [lax.dynamic_index_in_dim(cut, me ^ k, 0, keepdims=False) for k in range(size)]


def seq_exchange(pieces):
    taken = [part[0] for part in relative(pieces)]
    return in_order([taken[0]] + [swap(taken[k], "seq", k) for k in range(1, len(taken))])


MESH = pl.DeviceIdType.MESH


def neighbours():
    me, owner = lax.axis_index("seq"), lax.axis_index("fsdp")
    sibling = me + 1 - 2 * (me % 2)
    across = me + 2 - 4 * (me // 2 % 2)
    partner = owner + 1 - 2 * (owner % 2)
    return (me, sibling, across), ({"seq": sibling}, {"seq": across}, {"fsdp": partner})


def greet(devices):
    barrier = pltpu.get_barrier_semaphore()
    for device in devices:
        pl.semaphore_signal(barrier, inc=1, device_id=device, device_id_type=MESH)
    pl.semaphore_wait(barrier, len(devices))


class Sender:
    def __init__(self, send_sems, recv_sems):
        self.sems = (send_sems, recv_sems)
        self.count, self.open = 0, []

    def send(self, source, target, device):
        number = self.count
        copy = pltpu.make_async_remote_copy(
            src_ref=source,
            dst_ref=target,
            send_sem=self.sems[0].at[number],
            recv_sem=self.sems[1].at[number],
            device_id=device,
            device_id_type=MESH,
        )
        copy.start()
        self.count += 1
        self.open.append(copy)
        return copy

    def release(self, *copies):
        for copy in copies:
            copy.wait_send()
            self.open = [other for other in self.open if other is not copy]

    def finish(self):
        self.release(*self.open)


def plane_gather(link, blocks, ids):
    core, over_x, over_y = ids
    rows = blocks.shape[1]
    halves = (pl.ds(0, rows // 2), pl.ds(rows // 2, rows // 2))
    to_x = [link.send(blocks.at[0, half], blocks.at[2, half], over_x) for half in halves]
    to_y = [link.send(blocks.at[0, half], blocks.at[4, half], over_y) for half in halves[::-1]]
    last = [link.send(blocks.at[0], blocks.at[1], core)]
    yield
    to_x[0].wait_recv()
    diagonal = [link.send(blocks.at[2, halves[0]], blocks.at[6, halves[0]], over_y)]
    last.append(link.send(blocks.at[2, halves[0]], blocks.at[3, halves[0]], core))
    to_y[0].wait_recv()
    diagonal.append(link.send(blocks.at[4, halves[1]], blocks.at[6, halves[1]], over_x))
    last.append(link.send(blocks.at[4, halves[1]], blocks.at[5, halves[1]], core))
    to_x[1].wait_recv()
    last.append(link.send(blocks.at[2, halves[1]], blocks.at[3, halves[1]], core))
    to_y[1].wait_recv()
    last.append(link.send(blocks.at[4, halves[0]], blocks.at[5, halves[0]], core))
    for copy, half in zip(diagonal, halves):
        copy.wait_recv()
        last.append(link.send(blocks.at[6, half], blocks.at[7, half], core))
    for copy in last:
        copy.wait_recv()
    yield


def opening_kernel(
    shape,
    tokens,
    cotangent,
    qkv,
    proj,
    ff_own,
    ff_down,
    cosines,
    sines,
    seg_col,
    seg_row,
    tokens_all,
    weight,
    vectors,
    proj_mine,
    ff_all,
    ff_rows,
    normed,
    queries,
    keys,
    values,
    merged,
    logsum,
    part,
    cots,
    qkv_all,
    proj_all,
    ff_line,
    kv,
    send_sems,
    recv_sems,
    hand_send,
    hand_recv,
    local_sem,
):
    owned, vector_size, per_dev, group = shape
    (me, sibling, across), ids = neighbours()
    core, over_x, over_y = ids
    far = across + 1 - 2 * (across % 2)
    line = qkv_all.shape[0]
    size = 2 * line
    owner = lax.axis_index("fsdp")
    at, pair = owner // 2, owner % 2
    below, above = ({"fsdp": (owner + size - 2) % size}, {"fsdp": (owner + 2) % size})
    rows, width = tokens.shape
    seq_count = tokens_all.shape[0]
    seq_len = seq_count * rows
    halves = (pl.ds(0, rows // 2), pl.ds(rows // 2, rows // 2))
    others = (sibling, across, far)
    greet((*ids, {"seq": far}, below, above))
    link = Sender(send_sems, recv_sems)

    own_copy = pltpu.make_async_copy(ff_own.at[pair], ff_all.at[at, pair], local_sem)
    own_copy.start()
    ff_line[at] = ff_down[...]
    tokens_all[me] = tokens[...]
    qkv_all[at, pair] = qkv[...]
    proj_all[at, pair] = proj[...]

    turned, handed = [], []

    def hand_on(k):
        z = (at + k) % line
        target, member = z // group, z % group
        copy = pltpu.make_async_remote_copy(
            src_ref=ff_line.at[z],
            dst_ref=ff_rows.at[me, member],
            send_sem=hand_send.at[k],
            recv_sem=hand_recv.at[me * group + member],
            device_id={"seq": target},
            device_id_type=MESH,
        )

        @pl.when(target != me)
        def _():
            copy.start()

        @pl.when(target == me)
        def _():
            ff_rows[me, member] = ff_line[z]

        handed.append((copy, target))

    def ring_steps():
        before = [None] * 3
        for k in range(line):
            z = (at + k) % line
            here = (ff_line.at[z], ff_all.at[z, pair], ff_all.at[z, 1 - pair])
            for place, target in enumerate(here):
                source = ff_own.at[pair] if k == 0 and place == 1 else target
                if k > 0:
                    before[place].wait_recv()
                elif place == 2:
                    turned[0].wait_recv()
                if k < line - 1:
                    before[place] = link.send(source, target, below)
                if place == 0:
                    hand_on(k)
                yield

    ring = ring_steps()

    def pump(count):
        for _ in range(count):
            next(ring, None)

    def along_line(array, k):
        here = array.at[(at + k) % line, pair]
        return link.send(here, here, below)

    def to_partner(array, k):
        here = array.at[(at + k) % line, pair]
        return link.send(here, here, over_y)

    onward = along_line(qkv_all, 0)
    last = [to_partner(qkv_all, 0)]
    to_x = [link.send(tokens_all.at[me, half], tokens_all.at[me, half], over_x) for half in halves]
    last.append(link.send(tokens_all.at[me], tokens_all.at[me], core))
    proj_onward = along_line(proj_all, 0)
    for k in range(1, line):
        onward.wait_recv()
        if k < line - 1:
            onward = along_line(qkv_all, k)
        last.append(to_partner(qkv_all, k))
        proj_onward.wait_recv()
        if k < line - 1:
            proj_onward = along_line(proj_all, k)
    turned.append(link.send(ff_own.at[1 - pair], ff_all.at[at, pair], over_y))
    pump(2)
    for copy, half in zip(to_x, halves):
        copy.wait_recv()
        last.append(link.send(tokens_all.at[across, half], tokens_all.at[across, half], core))
    for copy in last:
        copy.wait_recv()
    proj_over = [to_partner(proj_all, k) for k in range(line)]
    cots[0] = cotangent[...]

    for z in range(line):
        for y in range(2):
            owner_row = 2 * z + y
            weight[pl.ds(owner_row * owned, owned), :] = qkv_all[z, y, :owned, :]
            done = 0
            cols = qkv_all.shape[3]
            for start, count, target in (
                (0, owned, 0),
                (owned, owned, 1),
                (2 * owned, vector_size - 2 * owned, 2),
            ):
                while count > 0:
                    row, col = start // cols, start % cols
                    span = min(count, cols - col)
                    length = (owned, owned, vector_size - 2 * owned)[target]
                    to = owner_row * length + (length - count)
                    vectors[target : target + 1, to : to + span] = qkv_all[
                        z, y, owned + row : owned + row + 1, col : col + span
                    ].astype(F32)
                    start, count = start + span, count - span

    head_cols = per_dev * HD
    holds_values = me % 2 == 1
    kv_first = (H + KV * (me % 2) + me // 2) * HD
    bias = jnp.concatenate(
        [
            vectors[2:3, pl.ds(pl.multiple_of(me * head_cols, HD), head_cols)],
            vectors[2:3, pl.ds(pl.multiple_of(kv_first, HD), HD)],
        ],
        axis=1,
    )
    for block in range(seq_count):
        here = pl.ds(block * rows, rows)
        value = tokens_all[block].astype(F32)
        normal = (value * inverse_rms(value) * vectors[0:1, :width]).astype(LOW)
        normed[block] = normal
        projected = dot(normal, weight[...]) + bias
        cosine, sine = cosines[here, :], sines[here, :]

        def rotate(head):
            return head * cosine + pltpu.roll(head, HD // 2, 1) * sine

        for head in range(per_dev):
            queries[head, here, :] = rotate(projected[:, head * HD : (head + 1) * HD]).astype(LOW)
        plain = projected[:, head_cols:]
        kv[0, here, :] = jnp.where(holds_values, plain, rotate(plain)).astype(LOW)
    swapped = link.send(kv.at[0], kv.at[1], core)
    pump(3)
    swapped.wait_recv()
    keys[...] = jnp.where(holds_values, kv[1], kv[0])
    values[...] = jnp.where(holds_values, kv[0], kv[1])

    for copy in proj_over:
        copy.wait_recv()
    exchange = [
        link.send(proj_all.at[pl.ds(target * group, group)], proj_mine.at[me], {"seq": target})
        for target in others
    ]
    gather_cots = plane_gather(link, cots, ids)
    next(gather_cots)
    proj_mine[me] = proj_all[pl.ds(me * group, group)]

    for block in range(seq_count):
        here, last_key = pl.ds(block * rows, rows), (block + 1) * rows
        row_index = block * rows + lax.broadcasted_iota(jnp.int32, (rows, last_key), 0)
        key_index = lax.broadcasted_iota(jnp.int32, (rows, last_key), 1)
        allowed = (key_index <= row_index) & (seg_col[here, :] == seg_row[:, :last_key])
        for head in range(per_dev):
            scores = times_transpose(queries[head, here, :], keys[:last_key, :]) * HD ** (-0.5)
            scores = jnp.where(allowed, scores, FLOOR)
            highest = jnp.max(scores, axis=-1, keepdims=True)
            exponent = jnp.exp(scores - highest)
            total = jnp.sum(exponent, axis=-1, keepdims=True)
            mixture = dot((exponent / total).astype(LOW), values[:last_key, :])
            merged[here, head * HD : (head + 1) * HD] = mixture.astype(LOW)
            logsum[head, here, :] = highest + jnp.log(total)
        pump(1)
    for copy in exchange:
        copy.wait_recv()
    quarter = proj.shape[1]
    for block in range(seq_count):
        for k in range(seq_count):
            columns = proj_mine[k].reshape(-1, quarter)
            part[block, :, k * quarter : (k + 1) * quarter] = dot(
                merged[block * rows : (block + 1) * rows, :], columns
            ).astype(LOW)

    pump(6)
    next(gather_cots)
    pump(3 * line)
    own_copy.wait()
    for source in others:
        for member in range(group):
            pltpu.make_async_remote_copy(
                src_ref=ff_line.at[0],
                dst_ref=ff_rows.at[source, member],
                send_sem=hand_send.at[0],
                recv_sem=hand_recv.at[source * group + member],
                device_id=core,
                device_id_type=MESH,
            ).wait_recv()
    for copy, target in handed:

        @pl.when(target != me)
        def _():
            copy.wait_send()

    link.finish()


def opening(tokens, cotangent, qkv, proj, ff, tables, segments, sizes):
    owned, vector_size, per_dev, group, line = sizes
    rows, width = tokens.shape
    block = (rows, width)
    seq_len = 4 * rows
    cols = qkv.shape[1]
    heads = (seq_len, HD)
    vmem, hbm = (pl.BlockSpec(memory_space=pltpu.VMEM), pl.BlockSpec(memory_space=pl.ANY))

    def like(*shape, dtype=LOW):
        return jax.ShapeDtypeStruct(shape, dtype)

    outs = [
        (like(4, *block), vmem),
        (like(width, cols), vmem),
        (like(3, max(width, 2048), dtype=F32), vmem),
        (like(4, group, 2, *proj.shape), vmem),
        (like(line, *ff[0].shape), hbm),
        (like(4, group, *ff[1].shape), vmem),
        (like(4, *block), vmem),
        (like(per_dev, *heads), vmem),
        (like(*heads), vmem),
        (like(*heads), vmem),
        (like(seq_len, per_dev * HD), vmem),
        (like(per_dev, seq_len, 1, dtype=F32), vmem),
        (like(4, *block), vmem),
        (like(8, *block), vmem),
    ]
    copies = 10 * line + 40
    return pl.pallas_call(
        functools.partial(opening_kernel, (owned, vector_size, per_dev, group)),
        out_shape=[shape for shape, _ in outs],
        in_specs=[vmem] * 10,
        out_specs=[place for _, place in outs],
        scratch_shapes=[
            pltpu.VMEM((line, 2, *qkv.shape), LOW),
            pltpu.VMEM((line, 2, *proj.shape), LOW),
            pltpu.VMEM((line, *ff[1].shape), LOW),
            pltpu.VMEM((2, *heads), LOW),
            pltpu.SemaphoreType.DMA((copies,)),
            pltpu.SemaphoreType.DMA((copies,)),
            pltpu.SemaphoreType.DMA((line,)),
            pltpu.SemaphoreType.DMA((4 * group,)),
            pltpu.SemaphoreType.DMA,
        ],
        cost_estimate=pl.CostEstimate(
            flops=100_000_000_000, bytes_accessed=40_000_000, transcendentals=4_000_000
        ),
        compiler_params=pltpu.CompilerParams(
            collective_id=0, has_side_effects=True, vmem_limit_bytes=56 << 20
        ),
    )(tokens, cotangent, qkv, proj, *ff, *tables, *segments)


def middle_kernel(
    part, tokens, vectors, hidden, mids, arrived, summed, across_in, send_sems, recv_sems
):
    (me, sibling, across), ids = neighbours()
    far = across + 1 - 2 * (across % 2)
    width = tokens.shape[1]
    greet(ids)
    link = Sender(send_sems, recv_sems)
    first = link.send(part.at[far], arrived.at[0], ids[0])
    second = link.send(part.at[sibling], arrived.at[1], ids[0])
    first.wait_recv()
    summed[...] = (part[across].astype(F32) + arrived[0].astype(F32)).astype(LOW)
    third = link.send(summed, across_in, ids[1])
    second.wait_recv()
    hidden[...] = tokens[...].astype(F32) + (part[me].astype(F32) + arrived[1].astype(F32))
    third.wait_recv()
    total = hidden[...] + across_in[...].astype(F32)
    hidden[...] = total
    mids[0] = (total * inverse_rms(total) * vectors[1:2, :width]).astype(LOW)
    for _ in plane_gather(link, mids, ids):
        pass
    link.finish()


def middle(part, tokens, vectors):
    block = tokens.shape
    vmem = pl.BlockSpec(memory_space=pltpu.VMEM)
    return pl.pallas_call(
        middle_kernel,
        out_shape=[jax.ShapeDtypeStruct(block, F32), jax.ShapeDtypeStruct((8, *block), LOW)],
        in_specs=[vmem] * 3,
        out_specs=[vmem] * 2,
        scratch_shapes=[
            pltpu.VMEM((2, *block), LOW),
            pltpu.VMEM(block, LOW),
            pltpu.VMEM(block, LOW),
            pltpu.SemaphoreType.DMA((16,)),
            pltpu.SemaphoreType.DMA((16,)),
        ],
        compiler_params=pltpu.CompilerParams(
            collective_id=1, has_side_effects=True, vmem_limit_bytes=32 << 20
        ),
    )(part, tokens, vectors)


def cut_kernel(shape, *refs):
    follows, group, units = shape
    if follows:
        mids_in, cots_in, whole_in, out_before, mid_before, *refs = refs
    else:
        mids_in, cots_in, weight_in, rows_in, *refs = refs
    term, out, mid, mids, cots, weight, rows, down, act, grad, part, stage, *refs = refs
    before, load_sems, weight_sems, stage_sems, before_sems, send_sems, recv_sems = refs
    (me, sibling, across), ids = neighbours()
    far = across + 1 - 2 * (across % 2)
    others = (sibling, across, far)
    line, _, owned, cols = weight.shape
    count, block, width = mids.shape
    quarter = width // 4
    fold = quarter // owned
    greet((ids[0], ids[1], {"seq": far}))
    link = Sender(send_sems, recv_sems)

    def load(source, target, sem):
        copy = pltpu.make_async_copy(source, target, sem)
        copy.start()
        return copy

    if follows:
        sent = [
            link.send(whole_in.at[pl.ds(k * group, group), 2], rows.at[me], {"seq": k})
            for k in others
        ]
        loads = [load(whole_in.at[pl.ds(me * group, group), 2], rows.at[me], weight_sems.at[line])]
        loads += [
            load(whole_in.at[z, pl.ds(0, 2)], weight.at[z], weight_sems.at[z]) for z in range(line)
        ]
    else:
        sent = []
        loads = [load(rows_in, rows, weight_sems.at[line]), load(weight_in, weight, weight_sems.at[0])]
    for t in range(count):
        load(mids_in.at[t], mids.at[t], load_sems.at[0, t])
        load(cots_in.at[t], cots.at[t], load_sems.at[1, t])
    for copy in loads:
        copy.wait()
    for copy in sent:
        copy.wait_recv()
    for k in range(4):
        for member in range(group):
            for j in range(fold):
                first = k * quarter + j * owned
                down[first : first + owned, member * units : (member + 1) * units] = rows[
                    k, member, :, j * units : (j + 1) * units
                ]

    def tokens(t, carry):
        pltpu.make_async_copy(mids_in.at[t], mids.at[t], load_sems.at[0, t]).wait()
        pltpu.make_async_copy(cots_in.at[t], cots.at[t], load_sems.at[1, t]).wait()
        gate_up = dot(mids[t], weight[...].reshape(width, cols))
        grad_act = dot(cots[t], down[...])
        gate, upward = gate_up[:, : cols // 2], gate_up[:, cols // 2 :]
        sigmoid_gate = jax.nn.sigmoid(gate)
        silu = gate * sigmoid_gate
        act[t] = (silu * upward).astype(LOW)
        grad[t, :, : cols // 2] = (
            grad_act * upward * sigmoid_gate * (1.0 + gate * (1.0 - sigmoid_gate))
        ).astype(LOW)
        grad[t, :, cols // 2 :] = (grad_act * silu).astype(LOW)
        return carry

    lax.fori_loop(0, count, tokens, 0)

    all_act = act[...].reshape(count * block, cols // 2)
    for k in range(4):
        value = column_product(
            cots[:, :, k * quarter : (k + 1) * quarter].reshape(count * block, quarter), all_act
        ).astype(LOW)
        for member in range(group):
            for j in range(fold):
                part[k, member, :, j * units : (j + 1) * units] = value[
                    j * owned : (j + 1) * owned, member * units : (member + 1) * units
                ]
    sent = [
        link.send(part.at[k], term.at[pl.ds(me * group, group), 2], {"seq": k}) for k in others
    ]
    term[pl.ds(me * group, group), 2] = part[me]
    all_grad = grad[...].reshape(count * block, cols)
    for z in range(line):
        value = column_product(
            mids[:, :, 2 * owned * z : 2 * owned * (z + 1)].reshape(count * block, 2 * owned),
            all_grad,
        ).astype(LOW)
        for y in range(2):
            term[z, y] = value[y * owned : (y + 1) * owned, :]

    def ask(t, slot):
        for place, source in enumerate((out_before, mid_before)):
            load(source.at[t], before.at[slot, place], before_sems.at[slot, place])

    if follows:
        ask(0, 0)

    def back(t, carry):
        slot = t % 2

        def hand_over(t, place, target):
            return pltpu.make_async_copy(
                stage.at[t % 2, place], target.at[t], stage_sems.at[t % 2, place]
            )

        @pl.when(t >= 2)
        def _():
            hand_over(t - 2, 0, out).wait()
            hand_over(t - 2, 1, mid).wait()

        values = [
            times_transpose(act[t], down[...]),
            times_transpose(grad[t], weight[...].reshape(width, cols)),
        ]
        if follows:

            @pl.when(t + 1 < count)
            def _():
                ask(t + 1, (t + 1) % 2)

            for place, source in enumerate((out_before, mid_before)):
                pltpu.make_async_copy(
                    source.at[t], before.at[slot, place], before_sems.at[slot, place]
                ).wait()
                values[place] = values[place] + before[slot, place].astype(F32)
        for place, target in enumerate((out, mid)):
            stage[slot, place] = values[place].astype(LOW)
            hand_over(t, place, target).start()
        return carry

    lax.fori_loop(0, count, back, 0)
    for t in (count - 2, count - 1):
        for place, target in enumerate((out, mid)):
            pltpu.make_async_copy(
                stage.at[t % 2, place], target.at[t], stage_sems.at[t % 2, place]
            ).wait()
    for copy in sent:
        copy.wait_recv()
    link.finish()


def cut_call(follows, args, sizes):
    group, line, owned, units = sizes
    mids = args[0]
    count, block, width = mids.shape
    cols = 2 * group * units
    hbm, vmem = (pl.BlockSpec(memory_space=pl.ANY), pl.BlockSpec(memory_space=pltpu.VMEM))
    rows = (4, group, owned, cols)
    low_scratch = [
        mids.shape,
        mids.shape,
        (line, 2, owned, cols),
        rows,
        (width, cols // 2),
        (count, block, cols // 2),
        (count, block, cols),
        rows,
        (2, 2, block, width),
        (2, 2, block, width),
    ]
    return pl.pallas_call(
        functools.partial(cut_kernel, (follows, group, units)),
        out_shape=[
            jax.ShapeDtypeStruct((line, 3, owned, cols), LOW),
            jax.ShapeDtypeStruct(mids.shape, LOW),
            jax.ShapeDtypeStruct(mids.shape, LOW),
        ],
        in_specs=[hbm] * len(args),
        out_specs=[vmem, hbm, hbm],
        scratch_shapes=[pltpu.VMEM(shape, LOW) for shape in low_scratch]
        + [
            pltpu.SemaphoreType.DMA((2, count)),
            pltpu.SemaphoreType.DMA((line + 1,)),
            pltpu.SemaphoreType.DMA((2, 2)),
            pltpu.SemaphoreType.DMA((2, 2)),
            pltpu.SemaphoreType.DMA((6,)),
            pltpu.SemaphoreType.DMA((6,)),
        ],
        compiler_params=pltpu.CompilerParams(
            collective_id=4 if follows else 3, has_side_effects=True, vmem_limit_bytes=56 << 20
        ),
        cost_estimate=pl.CostEstimate(
            flops=50_000_000_000, bytes_accessed=40_000_000, transcendentals=2_000_000
        ),
    )(*args)


def spread_blocks(link, ids, pair, ff_sum, hidden_blocks, down_blocks, local_sems):
    core, over_x, over_y = ids
    kept, down = ff_sum.at[pair], ff_sum.at[2]
    local = [
        pltpu.make_async_copy(kept, hidden_blocks.at[0], local_sems.at[0]),
        pltpu.make_async_copy(down, down_blocks.at[0], local_sems.at[1]),
    ]
    for copy in local:
        copy.start()
    over = link.send(ff_sum.at[1 - pair], hidden_blocks.at[4], over_y)
    to_x = [
        link.send(kept, hidden_blocks.at[2], over_x),
        link.send(down, down_blocks.at[2], over_x),
    ]
    last = [
        link.send(kept, hidden_blocks.at[1], core),
        link.send(down, down_blocks.at[1], core),
    ]
    yield
    over.wait_recv()
    far = link.send(hidden_blocks.at[4], hidden_blocks.at[6], over_x)
    last.append(link.send(hidden_blocks.at[4], hidden_blocks.at[5], core))
    for copy, blocks in zip(to_x, (hidden_blocks, down_blocks)):
        copy.wait_recv()
        last.append(link.send(blocks.at[2], blocks.at[3], core))
    yield
    far.wait_recv()
    last.append(link.send(hidden_blocks.at[6], hidden_blocks.at[7], core))
    yield
    for copy in last:
        copy.wait_recv()
    for copy in local:
        copy.wait()
    yield


def closing_kernel(
    shape,
    mid_terms,
    hidden,
    upstream,
    tokens_all,
    normed,
    vectors,
    weight,
    proj_mine,
    queries,
    keys,
    values,
    merged,
    logsum,
    cosines,
    sines,
    seg_col,
    seg_row,
    ff_sum,
    tokens_grad,
    gain_terms,
    attn_sum,
    hidden_blocks,
    down_blocks,
    arrived,
    held,
    from_x,
    from_y,
    corner,
    upper,
    grad_heads,
    grad_queries,
    grad_keys,
    grad_values,
    kv,
    projected,
    proj_part,
    proj_in,
    proj_half,
    bias_row,
    qkv_part,
    qkv_in,
    late,
    late_x,
    send_sems,
    recv_sems,
    local_sems,
):
    owned, per_dev, group = shape
    (me, sibling, across), (core, over_x, over_y) = neighbours()
    far = across + 1 - 2 * (across % 2)
    others = (sibling, across, far)
    pair = lax.axis_index("fsdp") % 2
    rows, width = hidden.shape
    seq_count = tokens_all.shape[0]
    quarter = width // seq_count
    low, high = (pl.ds(0, rows // 2), pl.ds(rows // 2, rows // 2))
    gains = (vectors[0:1, :width], vectors[1:2, :width])
    greet((core, over_x, {"seq": far}, over_y))
    link = Sender(send_sems, recv_sems)

    halved = {k: link.send(mid_terms.at[k + 1], arrived.at[k // 2], core) for k in (6, 2, 4, 0)}

    def chip_sum(k):
        halved[k].wait_recv()
        return mid_terms[k].astype(F32) + arrived[k // 2].astype(F32)

    held[2] = chip_sum(6).astype(LOW)
    turn_y = link.send(held.at[2, low], corner.at[0], over_x)
    turn_x = link.send(held.at[2, high], corner.at[1], over_y)
    held[0] = chip_sum(2).astype(LOW)
    direct_x = link.send(held.at[0, low], from_x.at[low], over_x)
    held[1] = chip_sum(4).astype(LOW)
    direct_y = link.send(held.at[1, high], from_y.at[high], over_y)
    tokens_grad[...] = chip_sum(0)
    turn_x.wait_recv()
    held[0, high] = (held[0, high].astype(F32) + corner[1].astype(F32)).astype(LOW)
    second_x = link.send(held.at[0, high], from_x.at[high], over_x)
    turn_y.wait_recv()
    held[1, low] = (held[1, low].astype(F32) + corner[0].astype(F32)).astype(LOW)
    second_y = link.send(held.at[1, low], from_y.at[low], over_y)
    for copy in (direct_x, direct_y, second_x, second_y):
        copy.wait_recv()

    grad_mid = tokens_grad[...] + from_x[...].astype(F32) + from_y[...].astype(F32)
    through, term = norm_back(hidden[...], inverse_rms(hidden[...]), gains[1], grad_mid)
    gain_terms[1:2, :] = term[None]
    total = upstream[...].astype(F32) + through
    tokens_grad[...] = total
    upper[me] = total.astype(LOW)
    last = [link.send(upper.at[me], upper.at[me], core)]
    to_x = [link.send(upper.at[me, half], upper.at[me, half], over_x) for half in (low, high)]
    for copy, half in zip(to_x, (low, high)):
        copy.wait_recv()
        last.append(link.send(upper.at[across, half], upper.at[across, half], core))
    for copy in last:
        copy.wait_recv()

    head_rows = per_dev * HD
    for block in range(seq_count):
        grad_heads[block * rows : (block + 1) * rows, :] = sum(
            times_transpose(
                upper[block, :, k * quarter : (k + 1) * quarter],
                proj_mine[k].reshape(head_rows, quarter),
            )
            for k in range(seq_count)
        ).astype(LOW)
    for k in range(seq_count):
        term = sum(
            column_product(
                merged[block * rows : (block + 1) * rows, :],
                upper[block, :, k * quarter : (k + 1) * quarter],
            )
            for block in range(seq_count)
        ).astype(LOW)
        for member in range(group):
            for y in range(2):
                first = (2 * member + y) * owned
                proj_part[y, k, member] = term[first : first + owned, :]
    proj_over = link.send(proj_part.at[1 - pair], proj_in, over_y)
    spread = spread_blocks(
        link, (core, over_x, over_y), pair, ff_sum, hidden_blocks, down_blocks, local_sems
    )
    next(spread)

    grad_keys[...] = jnp.zeros_like(grad_keys)
    grad_values[...] = jnp.zeros_like(grad_values)
    scale = HD ** (-0.5)
    for block in range(seq_count):
        here, last_key = pl.ds(block * rows, rows), (block + 1) * rows
        row_index = block * rows + lax.broadcasted_iota(jnp.int32, (rows, last_key), 0)
        key_index = lax.broadcasted_iota(jnp.int32, (rows, last_key), 1)
        allowed = (key_index <= row_index) & (seg_col[here, :] == seg_row[:, :last_key])
        for head in range(per_dev):
            query = queries[head, here, :]
            upper_head = grad_heads[here, head * HD : (head + 1) * HD]
            scores = times_transpose(query, keys[:last_key, :]) * scale
            probs = jnp.where(allowed, jnp.exp(scores - logsum[head, here, :]), 0.0)
            grad_probs = times_transpose(upper_head, values[:last_key, :])
            inner = jnp.sum(probs * grad_probs, axis=-1, keepdims=True)
            grad_scores = (probs * (grad_probs - inner)).astype(LOW)
            grad_queries[head, here, :] = (dot(grad_scores, keys[:last_key, :]) * scale).astype(LOW)
            grad_keys[:last_key, :] += column_product(grad_scores, query)
            grad_values[:last_key, :] += column_product(probs.astype(LOW), upper_head)
    next(spread)
    holds_values = me % 2 == 1
    key_copy = (grad_keys[...] * scale).astype(LOW)
    value_copy = grad_values[...].astype(LOW)
    kv[0] = jnp.where(holds_values, key_copy, value_copy)
    swapped = link.send(kv.at[0], kv.at[1], core)
    grad_keys[...] = jnp.where(holds_values, value_copy, key_copy).astype(F32)
    proj_over.wait_recv()
    proj_half[...] = (proj_part[pair].astype(F32) + proj_in[...].astype(F32)).astype(LOW)
    cols = weight.shape[1]

    def proj_place(device):
        return (pl.ds(device * group, group), pl.ds(0, owned), pl.ds(cols, quarter))

    last = [
        link.send(proj_half.at[k], attn_sum.at[proj_place(me)], {"seq": k}) for k in others
    ]
    attn_sum[proj_place(me)] = proj_half[me]
    swapped.wait_recv()
    grad_kv = grad_keys[...] + kv[1].astype(F32)

    bias_row[...] = jnp.zeros_like(bias_row)
    bias_parts = 0.0
    gain_terms[0:1, :] = jnp.zeros((1, width), F32)
    for block in range(seq_count):
        here = pl.ds(block * rows, rows)
        cosine, sine = cosines[here, :], sines[here, :]

        def rotate_back(head):
            return head * cosine - pltpu.roll(head, HD // 2, 1) * sine

        for head in range(per_dev):
            projected[here, head * HD : (head + 1) * HD] = rotate_back(
                grad_queries[head, here, :].astype(F32)
            ).astype(LOW)
        plain = grad_kv[block * rows : (block + 1) * rows, :]
        projected[here, head_rows:] = jnp.where(holds_values, plain, rotate_back(plain)).astype(LOW)
        grad_block = projected[here, :]
        bias_parts += jnp.sum(grad_block.astype(F32), axis=0, keepdims=True)
        grad_in = times_transpose(grad_block, weight[...])
        value = tokens_all[block].astype(F32)
        gain_terms[0:1, :] += jnp.sum(
            grad_in * value * inverse_rms(value), axis=0, keepdims=True
        )
        arrived[block] = grad_in.astype(LOW)
    first = link.send(arrived.at[far], late.at[0], core)
    second = link.send(arrived.at[sibling], late.at[1], core)
    first.wait_recv()
    link.release(direct_x, second_x)
    held[0] = (arrived[across].astype(F32) + late[0].astype(F32)).astype(LOW)
    third = link.send(held.at[0], late_x, over_x)
    kv_first = (H + KV * (me % 2) + me // 2) * HD
    bias_row[0:1, pl.ds(pl.multiple_of(me * head_rows, HD), head_rows)] = bias_parts[:, :head_rows]
    bias_row[0:1, pl.ds(pl.multiple_of(kv_first, HD), HD)] = bias_parts[:, head_rows:]
    line = qkv_in.shape[0]
    owned_bias = bias_row.shape[1] // (2 * line)
    qkv_part[:, :, owned:, :] = jnp.zeros_like(qkv_part[:, :, owned:, :])
    for z in range(line):
        for y in range(2):
            owner, at = 2 * z + y, 0
            for source, row, length in (
                (gain_terms, 0, owned),
                (gain_terms, 1, owned),
                (bias_row, 0, owned_bias),
            ):
                done = 0
                while done < length:
                    span = min(length - done, cols - at % cols)
                    first_col = owner * length + done
                    qkv_part[
                        y, z, owned + at // cols : owned + at // cols + 1, at % cols : at % cols + span
                    ] = source[row : row + 1, first_col : first_col + span].astype(LOW)
                    done, at = done + span, at + span
    for z in range(line):
        term = sum(
            column_product(
                normed[block, :, 2 * owned * z : 2 * owned * (z + 1)],
                projected[block * rows : (block + 1) * rows, :],
            )
            for block in range(seq_count)
        ).astype(LOW)
        for y in range(2):
            qkv_part[y, z, :owned, :] = term[y * owned : (y + 1) * owned, :]
    qkv_over = link.send(qkv_part.at[1 - pair], qkv_in, over_y)
    next(spread)
    second.wait_recv()
    third.wait_recv()
    grad_in = arrived[me].astype(F32) + late[1].astype(F32) + late_x[...].astype(F32)
    value = tokens_all[me].astype(F32)
    through, _ = norm_back(value, inverse_rms(value), gains[0], grad_in)
    tokens_grad[...] += through
    qkv_over.wait_recv()
    attn_sum[:, :, :cols] = (qkv_part[pair].astype(F32) + qkv_in[...].astype(F32)).astype(LOW)
    attn_sum[:, owned:, cols:] = jnp.zeros_like(attn_sum[:, owned:, cols:])
    for copy in last:
        copy.wait_recv()
    next(spread)
    link.finish()


def closing(args, sizes):
    owned, vector_rows, bias_cols, per_dev, group, line = sizes
    hidden, weight, proj_mine = args[1], args[6], args[7]
    rows, width = hidden.shape
    block = (rows, width)
    cols = weight.shape[1]
    quarter = proj_mine.shape[-1]
    heads = (4 * rows, HD)
    rows_in = (4, group, owned, quarter)
    outs = [
        jax.ShapeDtypeStruct(block, F32),
        jax.ShapeDtypeStruct((2, width), F32),
        jax.ShapeDtypeStruct((line, owned + vector_rows, cols + quarter), LOW),
        jax.ShapeDtypeStruct((8, *args[-1].shape[1:]), LOW),
        jax.ShapeDtypeStruct((4, *args[-1].shape[1:]), LOW),
    ]
    low_scratch = [
        (4, *block),
        (3, *block),
        block,
        block,
        (2, rows // 2, width),
        (4, *block),
        (4 * rows, per_dev * HD),
        (per_dev, *heads),
    ]
    return pl.pallas_call(
        functools.partial(closing_kernel, (owned, per_dev, group)),
        out_shape=outs,
        in_specs=[pl.BlockSpec(memory_space=pltpu.VMEM)] * len(args),
        out_specs=[pl.BlockSpec(memory_space=pltpu.VMEM)] * (len(outs) - 2)
        + [pl.BlockSpec(memory_space=pl.ANY)] * 2,
        scratch_shapes=[pltpu.VMEM(shape, LOW) for shape in low_scratch]
        + [pltpu.VMEM(heads, F32)] * 2
        + [
            pltpu.VMEM(shape, LOW)
            for shape in (
                (2, *heads),
                (4 * rows, cols),
                (2, *rows_in),
                rows_in,
                rows_in,
            )
        ]
        + [pltpu.VMEM((1, bias_cols), F32)]
        + [
            pltpu.VMEM(shape, LOW)
            for shape in (
                (2, line, owned + vector_rows, cols),
                (line, owned + vector_rows, cols),
                (2, *block),
                block,
            )
        ]
        + [pltpu.SemaphoreType.DMA((48,))] * 2
        + [pltpu.SemaphoreType.DMA((2,))],
        compiler_params=pltpu.CompilerParams(
            collective_id=2, has_side_effects=True, vmem_limit_bytes=58 << 20
        ),
        cost_estimate=pl.CostEstimate(
            flops=100_000_000_000, bytes_accessed=40_000_000, transcendentals=4_000_000
        ),
    )(*args)


def columns_kernel(place, *refs):
    *pieces, out = refs
    row = 0
    for piece in pieces:
        count, rows, quarter = piece.shape
        for k in range(count):
            here = place[0] + k - 2 * ((place[0] % 2) * (k % 2)) - 4 * (
                (place[0] // 2 % 2) * (k // 2 % 2)
            )
            out[pl.ds(row, rows), pl.ds(k * quarter, quarter)] = piece[here].astype(F32)
        row += rows


def columns_call(place, pieces):
    rows = sum(piece.shape[1] for piece in pieces)
    width = pieces[0].shape[0] * pieces[0].shape[2]
    return pl.pallas_call(
        columns_kernel,
        out_shape=jax.ShapeDtypeStruct((rows, width), F32),
        in_specs=[pl.BlockSpec(memory_space=pltpu.SMEM)]
        + [pl.BlockSpec(memory_space=pltpu.VMEM)] * len(pieces),
        out_specs=pl.BlockSpec(memory_space=pltpu.VMEM),
        compiler_params=pltpu.CompilerParams(vmem_limit_bytes=40 << 20),
    )(place, *pieces)


def down_kernel(fold, place, *refs):
    *pieces, out = refs
    row = 0
    for piece in pieces:
        count, owned, width = piece.shape
        span = width // fold
        for k in range(count):
            here = place[0] + k - 2 * ((place[0] % 2) * (k % 2)) - 4 * (
                (place[0] // 2 % 2) * (k // 2 % 2)
            )
            whole = piece[here].astype(F32)
            for j in range(fold):
                whole_part = whole[:, j * span : (j + 1) * span]
                out[pl.ds(row, span), pl.ds((k * fold + j) * owned, owned)] = whole_part.T
        row += span


def down_call(place, pieces, fold):
    rows = sum(piece.shape[2] // fold for piece in pieces)
    width = pieces[0].shape[0] * pieces[0].shape[1] * fold
    return pl.pallas_call(
        functools.partial(down_kernel, fold),
        out_shape=jax.ShapeDtypeStruct((rows, width), F32),
        in_specs=[pl.BlockSpec(memory_space=pltpu.SMEM)]
        + [pl.BlockSpec(memory_space=pltpu.VMEM)] * len(pieces),
        out_specs=pl.BlockSpec(memory_space=pltpu.VMEM),
        compiler_params=pltpu.CompilerParams(vmem_limit_bytes=40 << 20),
    )(place, *pieces)


def hidden_kernel(cuts, group, place, *refs):
    *pieces, out = refs
    units = cuts[-1][1]
    count = pieces[0].shape[0] // 2
    for k in range(count):
        here = place[0] + k - 2 * ((place[0] % 2) * (k % 2)) - 4 * (
            (place[0] // 2 % 2) * (k // 2 % 2)
        )
        for pair in range(2):
            entry = (pair + place[1] - 2 * pair * place[1]) * count + here
            for part in range(2):
                for member in range(group):
                    first = (((part * count + k) * group + member) * 2 + pair) * units
                    for piece, (low, high) in zip(pieces, cuts):
                        span = high - low
                        at = (part * group + member) * span
                        out[:, first + low : first + high] = piece[entry][
                            :, at : at + span
                        ].astype(F32)


def hidden_call(place, pieces, cuts, group):
    rows = pieces[0].shape[1]
    units = cuts[-1][1]
    width = 2 * 8 * group * units
    step = 16
    return pl.pallas_call(
        functools.partial(hidden_kernel, cuts, group),
        grid=(rows // step,),
        out_shape=jax.ShapeDtypeStruct((rows, width), F32),
        in_specs=[pl.BlockSpec(memory_space=pltpu.SMEM)]
        + [pl.BlockSpec((8, step, piece.shape[2]), lambda i: (0, i, 0)) for piece in pieces],
        out_specs=pl.BlockSpec((step, width), lambda i: (i, 0)),
        compiler_params=pltpu.CompilerParams(vmem_limit_bytes=40 << 20),
    )(place, *pieces)


def local(
    tokens,
    segment_ids,
    attn_gain,
    qkv_weight,
    qkv_bias,
    proj_weight,
    mlp_gain,
    gate_up_weight,
    down_weight,
    cotangent,
):
    seq_count = lax.axis_size("seq")
    fsdp_count = lax.axis_size("fsdp")
    line = fsdp_count // 2
    place = lax.axis_index("seq")
    odd = lax.axis_index("fsdp") % 2 == 1
    tok_rows, width = tokens.shape[1:]
    seq_len = tok_rows * seq_count
    owned = qkv_weight.shape[0]
    owned_hidden = down_weight.shape[0]
    hidden = owned_hidden * fsdp_count
    quarter = width // seq_count
    per_dev = H // seq_count
    head_cols = per_dev * HD
    score_scale = HD ** (-0.5)
    group = line // seq_count
    cut_at = owned_hidden // 2 // 128 * 128
    cuts = [(0, cut_at), (cut_at, owned_hidden)]

    holds_values = place % 2 == 1
    kv_first = (H + KV * (place % 2) + place // 2) * HD
    qkv_own = jnp.concatenate(
        [
            lax.dynamic_slice_in_dim(qkv_weight, place * head_cols, head_cols, 1),
            lax.dynamic_slice_in_dim(qkv_weight, kv_first, HD, 1),
        ],
        axis=1,
    )
    cols = head_cols + HD
    vector = jnp.concatenate([attn_gain, mlp_gain, qkv_bias])
    vector_size = vector.shape[0]
    vector_rows = -(-vector_size // (16 * cols)) * 16
    vector = jnp.pad(vector, (0, vector_rows * cols - vector_size)).reshape(vector_rows, cols)
    proj_cols = lax.dynamic_slice_in_dim(proj_weight, place * quarter, quarter, 1)
    down_cols = lax.dynamic_slice_in_dim(down_weight, place * quarter, quarter, 1)
    fold = quarter // owned

    def folded(value):
        return jnp.concatenate(
            [value[..., j * owned : (j + 1) * owned, :] for j in range(fold)], axis=-1
        )

    def ff_columns(low, high, pair):
        return jnp.concatenate(
            [
                lax.dynamic_slice_in_dim(
                    gate_up_weight,
                    first + ((place * group + member) * 2 + pair) * owned_hidden + low,
                    high - low,
                    1,
                )
                for first in (0, hidden)
                for member in range(group)
            ],
            axis=1,
        )

    ff_sent = []
    for low, high in cuts:
        by_owner = [ff_columns(low, high, pair) for pair in range(2)]
        ff_sent.append((by_owner, folded(jnp.transpose(down_cols[low:high]))))
    segment_row = segment_ids[0]
    doc_starts = jnp.sum((segment_row[None, :] < segment_row[:, None]).astype(jnp.int32), axis=1)
    places = jnp.arange(seq_len, dtype=jnp.int32) - doc_starts
    inverse = THETA ** (-2.0 * jnp.arange(HD // 2, dtype=F32) / HD)
    angles = places.astype(F32)[:, None] * inverse[None, :]
    angles = jnp.concatenate([angles, angles], axis=-1)
    cosines = jnp.cos(angles)
    signs = jnp.where(jnp.arange(HD) < HD // 2, -1.0, 1.0).astype(F32)
    sines = jnp.sin(angles) * signs

    (
        tokens_all,
        qkv_mine,
        vectors,
        proj_mine,
        first_all,
        first_rows,
        normed_in,
        queries,
        head_keys,
        head_values,
        merged,
        logsum,
        attended,
        cots,
    ) = opening(
        tokens[0],
        cotangent[0],
        jnp.concatenate([qkv_own, vector], axis=0),
        lax.dynamic_slice_in_dim(proj_weight, place * quarter, quarter, 1),
        (jnp.stack(ff_sent[0][0]), ff_sent[0][1]),
        (cosines, sines),
        (segment_row[:, None], segment_row[None]),
        (owned, vector_size, per_dev, group, line),
    )
    (by_owner, second_down) = ff_sent[1]
    kept, given = pick(odd, *by_owner)
    second_sent = jnp.stack([*by_pair(kept, swap(given, "fsdp", 1)), second_down])
    second_all = line_gather(second_sent + nought(vectors[0, 0]))

    hidden_in, mids = middle(attended, tokens[0], vectors)

    def plane_reduce(total):
        parts = [total[k] for k in range(2 * seq_count)]
        away = seq_reduce(parts[seq_count:]).astype(LOW)
        return seq_reduce(parts[:seq_count]) + swap(away, "fsdp", 1).astype(F32)

    spans = [high - low for low, high in cuts]
    first_term, out_first, mid_first = cut_call(
        False, (mids, cots, first_all, first_rows), (group, line, owned, spans[0])
    )
    second_term, out, grad_mid = cut_call(
        True, (mids, cots, second_all, out_first, mid_first), (group, line, owned, spans[1])
    )

    sums = [line_reduce(term) for term in (first_term, second_term)]

    tokens_grad, gain_terms, attn_term, *first_blocks = closing(
        (
            grad_mid,
            hidden_in,
            cotangent[0],
            tokens_all,
            normed_in,
            vectors,
            qkv_mine,
            proj_mine,
            queries,
            head_keys,
            head_values,
            merged,
            logsum,
            cosines,
            sines,
            segment_row[:, None],
            segment_row[None],
            sums[0],
        ),
        (owned, vector_rows, qkv_weight.shape[1], per_dev, group, line),
    )
    block_out = (hidden_in + plane_reduce(out)).astype(LOW)

    places_here = jnp.stack([place, lax.axis_index("fsdp") % 2]).astype(jnp.int32)
    attn_sum = line_reduce(attn_term + nought(sums[1][0, 0, 0]))
    second_sum = sums[1] + nought(attn_sum[0, 0])
    kept, given = pick(odd, second_sum[0], second_sum[1])
    here = seq_blocks(jnp.stack([kept, second_sum[2]]))
    hidden_pieces = [
        first_blocks[0],
        jnp.stack([pair[0] for pair in here] + seq_blocks(swap(given, "fsdp", 1))),
    ]
    down_pieces = [first_blocks[1], jnp.stack([pair[1] for pair in here])]
    down_grad = down_call(places_here, down_pieces, fold)
    gate_up_grad = hidden_call(places_here, hidden_pieces, cuts, group)
    attn_sums = seq_blocks(attn_sum)
    proj_grad = columns_call(
        places_here, [jnp.stack([part[:owned, cols:] for part in attn_sums])]
    )
    qkv_sums = in_order([part[:, :cols] for part in attn_sums])
    qkv_grad = jnp.concatenate(
        [part[:owned, :head_cols] for part in qkv_sums]
        + [part[:owned, head_cols:] for part in qkv_sums[0::2]]
        + [part[:owned, head_cols:] for part in qkv_sums[1::2]],
        axis=-1,
    ).astype(F32)
    vector_sum = sum(part[owned:].astype(F32) for part in qkv_sums).reshape(-1)
    return (
        block_out[None],
        tokens_grad[None],
        vector_sum[:owned],
        qkv_grad,
        vector_sum[2 * owned : vector_size],
        proj_grad,
        vector_sum[owned : 2 * owned],
        gate_up_grad,
        down_grad,
    )


def solution(mesh):
    in_specs = (
        P("fsdp", "seq", None),
        P("fsdp", None),
        P("fsdp"),
        P("fsdp", None),
        P("fsdp"),
        P("fsdp", None),
        P("fsdp"),
        P("fsdp", None),
        P("fsdp", None),
        P("fsdp", "seq", None),
    )
    out_specs = (
        P("fsdp", "seq", None),
        P("fsdp", "seq", None),
        P("fsdp"),
        P("fsdp", None),
        P("fsdp"),
        P("fsdp", None),
        P("fsdp"),
        P("fsdp", None),
        P("fsdp", None),
    )
    return jax.shard_map(local, mesh=mesh, in_specs=in_specs, out_specs=out_specs, check_vma=False)
```

time: 758 us -> 601 us (0.79)
  matrix products: 149 us -> 0 us
  Pallas kernels: 311 us -> 440 us
  local copies, waits for them, and re-layouts: 79.4 us -> 25.4 us
  other arithmetic: 67.7 us -> 24 us
  waiting for transfers between devices: 105 us -> 75 us
  starting transfers between devices: 22.5 us -> 12.5 us
    pallas_call x1 -> x4, Pallas kernels: 52.2 us -> 298 us  [the longest x1 125 us: closing(): pl.pallas_call(functools.partial(closing_kernel, (owned, per_dev, group))...]
    dot_general x26 -> x0, matrix products: 149 us -> none  [the longest x6 55.7 us: times_transpose(): lax.dot_general(left, right, (((1,), (1,)), ((), ())), preferred_element_...]
    pallas_call x1, Pallas kernels: 243 us -> 126 us  [opening(): pl.pallas_call(functools.partial(opening_kernel, (owned, vector_size, per...]
    ppermute x36 -> x16, waiting for transfers between devices: 105 us -> 63.9 us  [swap(): lax.ppermute(value, axis, [(i, i ^ distance) for i in range(lax.axis_size...]
    slice x23 -> x9, local copies, waits for them, and re-layouts: 25.7 us -> 7.98 us  [the longest x1 2.12 us: plane_reduce(): parts = [total[k] for k in range(2 * seq_count)]]
    unnamed x163 -> x48, local copies, waits for them, and re-layouts: 23.4 us -> 9.92 us
    ppermute x36 -> x16, starting transfers between devices: 22.2 us -> 11.4 us  [swap(): lax.ppermute(value, axis, [(i, i ^ distance) for i in range(lax.axis_size...]
    another operation x22 -> x6, other arithmetic: 11 us -> 2.01 us  [the longest x2 1.06 us: local(): jnp.stack(ff_sent[0][0])]
  transfers between devices with their start and end apart: 39 -> 20, of which waited for: 12 -> 10; matrix products, arithmetic and copies ran while one was open for 29% -> 6% of each run, Pallas kernels for 9% -> 72%
where the time goes in v3:
time: 601 us; the launch traced here: 594 us
  Pallas kernels  440 us (73%)
  waiting for transfers between devices  75 us (12%)
  local copies, waits for them, and re-layouts  25.4 us (4%)
  other arithmetic  24 us (4%)
  between operations  16.6 us (3%)
  starting transfers between devices  12.5 us (2%)
    pallas_call x1, Pallas kernels, opening(): pl.pallas_call(functools.partial(opening_kernel, (owned, vector_size, per...  126 us
    pallas_call x1, Pallas kernels, closing(): pl.pallas_call(functools.partial(closing_kernel, (owned, per_dev, group))...  125 us
    pallas_call x2, Pallas kernels, cut_call(): pl.pallas_call(functools.partial(cut_kernel, (follows, group, units)), ou...  121 us
    ppermute x16, waiting for transfers between devices, swap(): lax.ppermute(value, axis, [(i, i ^ distance) for i in range(lax.axis_size...  63.9 us
    pallas_call x1, Pallas kernels, middle(): pl.pallas_call(middle_kernel, out_shape=[jax.ShapeDtypeStruct(block, F32)...  52.4 us
  transfers between devices with their start and end apart: 20, of which 10 were waited for; matrix products, arithmetic and copies ran while one was open for 6% of the time, Pallas kernels for 72%

profile of v3, /device:TPU:0, one launch (start us, length us, event | category | flops | bytes accessed | tf_op | source)
XLA Modules:
  0.0 593.6 jit_solution(1090234160537554303)
XLA Ops:
  7.3 1.8 constant_dynamic-slice_fusion.4
  10.1 3.0 collective-permute-start
  13.3 1.6 constant_dynamic-slice_fusion.9.proj
  19.2 1.7 constant_dynamic-slice_fusion.8
  22.9 2.9 sine_multiply_fusion
  26.5 125.9 %shard_map.169 = (bf16[4,256,1536]{2,1,0:T(8,128)(2,1)}, bf16[1536,512]{1,0:T(8,128)(2,1)}, f32[3,2048]{1,0:T(4,128)}, bf16[4,1,2,192,384]{4,3,2,1,0:T(8,128)(2,...) custom-call(bf16[256,1536]{1,0:T(8,128)(2,1)} %bitcast.67, ...), custom_call_target="tpu_custom_call" | custom-call | flops 99999997952 | bytes 40000000 | tf_op jit(solution)/shard_map/pallas_call | solution.py:471
  158.5 52.4 %shard_map.170 = (f32[256,1536]{1,0:T(8,128)S(1)}, bf16[8,256,1536]{2,1,0:T(8,128)(2,1)S(1)}) custom-call(bf16[4,256,1536]{2,1,0:T(8,128)(2,1)S(1)} %copy-done.2, bf16[256,1536]{1,0:T(8,128)(2,1)S(1)} %bitcast.68, f32[3,2048]{1,0:T(4,128)S(1)} %copy-done.8), custom_call_target="tpu_custom_call" | custom-call | tf_op jit(solution)/shard_map/pallas_call | solution.py:523
  212.0 2.7 copy-done.9
  214.7 43.4 %shard_map.171 = (bf16[4,3,192,1024]{3,2,1,0:T(8,128)(2,1)}, bf16[8,256,1536]{2,1,0:T(8,128)(2,1)}, bf16[8,256,1536]{2,1,0:T(8,128)(2,1)}) custom-call(bf16[8,256,1536]{2,1,0:T(8,128)(2,1)} %copy-done.9, bf16[8,256,1536]{2,1,0:T(8,128)(2,1)} %get-tuple-element.39.refs_1_, bf16[4,2,192,1024]{3,2,1,0:T(8,128)(2,1)} %get-tuple-element.40.refs_2_, ...), custom_call_target="tpu_custom_call" | custom-call | flops 49999998976 | bytes 40000000 | tf_op jit(solution)/shard_map/pallas_call | solution.py:701
  258.5 7.8 %all-gather.2.cloned.1.call-done.refs_2_ = bf16[4,3,192,1216]{3,2,1,0:T(8,128)(2,1)} async-done(((bf16[1,3,192,1216]{3,2,1,0:T(8,128)(2,1)}), bf16[4,3,192,1216]{3,2,1,0:T(8,128)(2,1)}) %all-gather.2.cloned.1.call-update) | async-done | bytes 5603344 | tf_op jit(solution)/shard_map/all_gather | solution.py:65
  266.3 77.7 %shard_map.172 = (bf16[4,3,192,1216]{3,2,1,0:T(8,128)(2,1)}, bf16[8,256,1536]{2,1,0:T(8,128)(2,1)}, bf16[8,256,1536]{2,1,0:T(8,128)(2,1)}) custom-call(bf16[8,256,1536]{2,1,0:T(8,128)(2,1)} %copy-done.9, bf16[8,256,1536]{2,1,0:T(8,128)(2,1)} %get-tuple-element.39.refs_1_, bf16[4,3,192,1216]{3,2,1,0:T(8,128)(2,1)} %all-gather.2.cloned.1.call-done.refs_2_, ...), custom_call_target="tpu_custom_call" | custom-call | flops 49999998976 | bytes 40000000 | tf_op jit(solution)/shard_map/pallas_call | solution.py:701
  344.5 2.1 fusion.13
  348.9 3.3 reduce-scatter.4.cloned.1.call-done
  352.1 124.8 %shard_map.173 = (f32[256,1536]{1,0:T(8,128)}, f32[2,1536]{1,0:T(2,128)}, bf16[4,208,896]{2,1,0:T(8,128)(2,1)}, bf16[8,192,1024]{2,1,0:T(8,128)(2,1)}, bf16[4,192,1024]{2,1,0:T(8,128)(2,1)}) custom-call(bf16[8,256,1536]{2,1,0:T(8,128)(2,1)} %get-tuple-element.45.mid_terms, f32[256,1536]{1,0:T(8,128)} %copy-done.4, bf16[256,1536]{1,0:T(8,128)(2,1)} %bitcast.84, ...), custom_call_target="tpu_custom_call" | custom-call | flops 99999997952 | bytes 40000000 | tf_op jit(solution)/shard_map/pallas_call | solution.py:1035
  478.7 2.6 broadcast_add_fusion
  481.4 2.9 fusion.4
  484.3 1.7 collective-permute-start.4
  486.3 18.4 %collective-permute-done.4 = bf16[256,1536]{1,0:T(8,128)(2,1)S(1)} collective-permute-done((bf16[256,1536]{1,0:T(8,128)(2,1)S(1)}, bf16[256,1536]{1,0:T(8,128)(2,1)S(1)}, u32[]{:S(2)}, u32[]{:S(2)}) %collective-permute-start.4) | collective-permute-done | bytes 786464 | tf_op jit(solution)/shard_map/ppermute | solution.py:56
  504.7 2.3 fusion
  507.0 1.7 collective-permute-start.5
  508.8 11.7 %collective-permute-done.2 = bf16[256,1536]{1,0:T(8,128)(2,1)} collective-permute-done((bf16[256,1536]{1,0:T(8,128)(2,1)}, bf16[256,1536]{1,0:T(8,128)(2,1)}, u32[]{:S(2)}, u32[]{:S(2)}) %collective-permute-start.2) | collective-permute-done | bytes 786464 | tf_op jit(solution)/shard_map/ppermute | solution.py:56
  520.5 4.2 collective-permute-done.5
  524.7 3.2 fusion.6
  527.9 1.6 collective-permute-start.6
  534.0 1.6 collective-permute-done.6
  535.7 9.7 %collective-permute-done.12 = bf16[192,1216]{1,0:T(8,128)(2,1)S(1)} collective-permute-done((bf16[192,1216]{1,0:T(8,128)(2,1)S(1)}, bf16[192,1216]{1,0:T(8,128)(2,1)S(1)}, u32[]{:S(2)}, u32[]{:S(2)}) %collective-permute-start.12) | collective-permute-done | bytes 466976 | tf_op jit(solution)/shard_map/ppermute | solution.py:56
  548.2 1.6 shard_map.174
  550.5 6.9 %collective-permute-done.10 = bf16[2,192,1216]{2,1,0:T(8,128)(2,1)S(1)} collective-permute-done((bf16[2,192,1216]{2,1,0:T(8,128)(2,1)S(1)}, bf16[2,192,1216]{2,1,0:T(8,128)(2,1)S(1)}, u32[]{:S(2)}, u32[]{:S(2)}) %collective-permute-start.10) | collective-permute-done | bytes 933920 | tf_op jit(solution)/shard_map/ppermute | solution.py:56
  557.7 9.8 %collective-permute-done.14 = bf16[192,1216]{1,0:T(8,128)(2,1)S(1)} collective-permute-done((bf16[192,1216]{1,0:T(8,128)(2,1)S(1)}, bf16[192,1216]{1,0:T(8,128)(2,1)S(1)}, u32[]{:S(2)}, u32[]{:S(2)}) %collective-permute-start.14) | collective-permute-done | bytes 466976 | tf_op jit(solution)/shard_map/ppermute | solution.py:56
  567.7 1.6 collective-permute-done.15
  569.4 8.4 %shard_map.175 = f32[192,17920]{1,0:T(8,128)} custom-call(s32[2]{0:T(128)S(1)} %pad_add_fusion.place, bf16[8,192,1024]{2,1,0:T(8,128)(2,1)S(1)} %copy-done.3, bf16[8,192,1216]{2,1,0:T(8,128)(2,1)S(1)} %bitcast_dynamic-update-slice_fusion.refs_1_), custom_call_target="tpu_custom_call" | custom-call | tf_op jit(solution)/shard_map/pallas_call | solution.py:1156
  579.2 5.9 shard_map.176
  (124 shorter events, 30.2 us)
Async XLA Ops:
  7.2 6.1 %copy-start = (bf16[192,2048]{1,0:T(8,128)(2,1)S(1)}, bf16[192,2048]{1,0:T(8,128)(2,1)}, u32[]{:S(2)}) copy-start(bf16[192,2048]{1,0:T(8,128)(2,1)} %param.13) | copy-start | bytes 2359300
  7.2 259.1 %all-gather.2.cloned.1.call-start = ((), (), s32[]{:S(2)}) async-start(), calls=%async_computation.3 | async-start | bytes 7372800 | tf_op jit(solution)/shard_map/all_gather | solution.py:65
  7.3 5.9 copy-start.14
  7.3 5.9 copy-start.15
  7.3 5.9 copy-start.16
  10.1 144.3 %collective-permute-start = (bf16[192,1216]{1,0:T(8,128)(2,1)}, bf16[192,1216]{1,0:T(8,128)(2,1)S(1)}, u32[]{:S(2)}, u32[]{:S(2)}) collective-permute-start(bf16[192,1216]{1,0:T(8,128)(2,1)} %broadcast_select_fusion.2), channel_id=1, source_target_pairs={{0,1},{1,0},{2,3},{3,2},{4,5},{5,4},{6,7},{7,6},{8,9},{9,8},{10,11... | collective-permute-start | bytes 1400840 | tf_op jit(solution)/shard_map/ppermute | solution.py:56
  13.1 3.1 copy-start.13
  154.9 2.4 copy-start.2
  155.0 2.4 copy-start.8
  156.3 195.8 %reduce-scatter.4.cloned.1.call-start = ((), (), s32[]{:S(2)}) async-start(), calls=%async_computation.4 | async-start | bytes 5898240 | tf_op jit(solution)/shard_map/reduce_scatter | solution.py:69
  212.0 2.7 copy-start.9
  258.2 218.7 %reduce-scatter.6.cloned.1.call-start = ((), (), s32[]{:S(2)}) async-start(), calls=%async_computation.5 | async-start | bytes 7372800 | tf_op jit(solution)/shard_map/reduce_scatter | solution.py:69
  344.0 183.9 %reduce-scatter.8.cloned.1.call-start = ((), (), s32[]{:S(2)}) async-start(), calls=%async_computation.6 | async-start | bytes 1863680 | tf_op jit(solution)/shard_map/reduce_scatter | solution.py:69
  346.8 134.6 %collective-permute-start.1 = (bf16[2,256,1536]{2,1,0:T(8,128)(2,1)S(1)}, bf16[2,256,1536]{2,1,0:T(8,128)(2,1)}, u32[]{:S(2)}, u32[]{:S(2)}) collective-permute-start(bf16[2,256,1536]{2,1,0:T(8,128)(2,1)S(1)} %pad_maximum_fusion.1), channel_id=1, source_target_pairs={{0,8},{8,0},{16,24},{24,16},{1,9},{9,1},{17,25},{25,17},{2,10},{10... | collective-permute-start | bytes 4718600 | tf_op jit(solution)/shard_map/ppermute | solution.py:56
  348.8 132.6 %collective-permute-start.3 = (bf16[2,256,1536]{2,1,0:T(8,128)(2,1)}, bf16[2,256,1536]{2,1,0:T(8,128)(2,1)S(1)}, u32[]{:S(2)}, u32[]{:S(2)}) collective-permute-start(bf16[2,256,1536]{2,1,0:T(8,128)(2,1)} %pad_maximum_fusion.2), channel_id=1, source_target_pairs={{0,8},{8,0},{16,24},{24,16},{1,9},{9,1},{17,25},{25,17},{2,10},{10... | collective-permute-start | bytes 4718600 | tf_op jit(solution)/shard_map/ppermute | solution.py:56
  484.3 20.4 %collective-permute-start.4 = (bf16[256,1536]{1,0:T(8,128)(2,1)S(1)}, bf16[256,1536]{1,0:T(8,128)(2,1)S(1)}, u32[]{:S(2)}, u32[]{:S(2)}) collective-permute-start(bf16[256,1536]{1,0:T(8,128)(2,1)S(1)} %get-tuple-element.72), channel_id=1, source_target_pairs={{0,16},{8,24},{16,0},{24,8},{1,17},{9,25},{17,1},{25,9},{2,18},{10... | collective-permute-start | bytes 2359304 | tf_op jit(solution)/shard_map/ppermute | solution.py:56
  486.0 38.7 %copy-start.5 = (f32[256,1536]{1,0:T(8,128)S(1)}, f32[256,1536]{1,0:T(8,128)}, u32[]{:S(2)}) copy-start(f32[256,1536]{1,0:T(8,128)} %copy-done.4) | copy-start | bytes 4718596
  486.0 34.5 %collective-permute-start.2 = (bf16[256,1536]{1,0:T(8,128)(2,1)}, bf16[256,1536]{1,0:T(8,128)(2,1)}, u32[]{:S(2)}, u32[]{:S(2)}) collective-permute-start(bf16[256,1536]{1,0:T(8,128)(2,1)} %get-tuple-element.71), channel_id=1, source_target_pairs={{0,16},{8,24},{16,0},{24,8},{1,17},{9,25},{17,1},{25,9},{2,18},{10... | collective-permute-start | bytes 2359304 | tf_op jit(solution)/shard_map/ppermute | solution.py:56
  507.0 17.6 %collective-permute-start.5 = (bf16[256,1536]{1,0:T(8,128)(2,1)}, bf16[256,1536]{1,0:T(8,128)(2,1)}, u32[]{:S(2)}, u32[]{:S(2)}) collective-permute-start(bf16[256,1536]{1,0:T(8,128)(2,1)} %fusion), channel_id=1, source_target_pairs={{0,1},{1,0},{2,3},{3,2},{4,5},{5,4},{6,7},{7,6},{8,9},{9,8},{10,11... | collective-permute-start | bytes 2359304 | tf_op jit(solution)/shard_map/ppermute | solution.py:56
  508.8 22.6 %copy-start.11 = (bf16[1,3,192,1216]{3,2,1,0:T(8,128)(2,1)S(1)}, bf16[1,3,192,1216]{3,2,1,0:T(8,128)(2,1)}, u32[]{:S(2)}) copy-start(bf16[1,3,192,1216]{3,2,1,0:T(8,128)(2,1)} %reduce-scatter.6.cloned.1.call-done) | copy-start | bytes 4202500
  527.9 7.8 %collective-permute-start.6 = (bf16[208,896]{1,0:T(8,128)(2,1)}, bf16[208,896]{1,0:T(8,128)(2,1)S(1)}, u32[]{:S(2)}, u32[]{:S(2)}) collective-permute-start(bf16[208,896]{1,0:T(8,128)(2,1)} %bitcast.73), channel_id=1, source_target_pairs={{0,16},{8,24},{16,0},{24,8},{1,17},{9,25},{17,1},{25,9},{2,18},{10... | collective-permute-start | bytes 1118216 | tf_op jit(solution)/shard_map/ppermute | solution.py:56
  529.5 6.2 %collective-permute-start.8 = (bf16[208,896]{1,0:T(8,128)(2,1)}, bf16[208,896]{1,0:T(8,128)(2,1)S(1)}, u32[]{:S(2)}, u32[]{:S(2)}) collective-permute-start(bf16[208,896]{1,0:T(8,128)(2,1)} %bitcast.74), channel_id=1, source_target_pairs={{0,8},{8,0},{16,24},{24,16},{1,9},{9,1},{17,25},{25,17},{2,10},{10... | collective-permute-start | bytes 1118216 | tf_op jit(solution)/shard_map/ppermute | solution.py:56
  531.7 13.7 %collective-permute-start.12 = (bf16[192,1216]{1,0:T(8,128)(2,1)S(1)}, bf16[192,1216]{1,0:T(8,128)(2,1)S(1)}, u32[]{:S(2)}, u32[]{:S(2)}) collective-permute-start(bf16[192,1216]{1,0:T(8,128)(2,1)S(1)} %get-tuple-element.81), channel_id=1, source_target_pairs={{0,1},{1,0},{2,3},{3,2},{4,5},{5,4},{6,7},{7,6},{8,9},{9,8},{10,11... | collective-permute-start | bytes 1400840 | tf_op jit(solution)/shard_map/ppermute | solution.py:56
  532.7 24.6 %collective-permute-start.10 = (bf16[2,192,1216]{2,1,0:T(8,128)(2,1)S(1)}, bf16[2,192,1216]{2,1,0:T(8,128)(2,1)S(1)}, u32[]{:S(2)}, u32[]{:S(2)}) collective-permute-start(bf16[2,192,1216]{2,1,0:T(8,128)(2,1)S(1)} %pad_maximum_fusion.3), channel_id=1, source_target_pairs={{0,16},{8,24},{16,0},{24,8},{1,17},{9,25},{17,1},{25,9},{2,18},{10... | collective-permute-start | bytes 2801672 | tf_op jit(solution)/shard_map/ppermute | solution.py:56
  534.0 23.5 %collective-permute-start.9 = (bf16[2,192,1216]{2,1,0:T(8,128)(2,1)S(1)}, bf16[2,192,1216]{2,1,0:T(8,128)(2,1)S(1)}, u32[]{:S(2)}, u32[]{:S(2)}) collective-permute-start(bf16[2,192,1216]{2,1,0:T(8,128)(2,1)S(1)} %pad_maximum_fusion.3), channel_id=1, source_target_pairs={{0,8},{8,0},{16,24},{24,16},{1,9},{9,1},{17,25},{25,17},{2,10},{10... | collective-permute-start | bytes 2801672 | tf_op jit(solution)/shard_map/ppermute | solution.py:56
  535.7 10.2 %collective-permute-start.7 = (bf16[208,896]{1,0:T(8,128)(2,1)S(1)}, bf16[208,896]{1,0:T(8,128)(2,1)S(1)}, u32[]{:S(2)}, u32[]{:S(2)}) collective-permute-start(bf16[208,896]{1,0:T(8,128)(2,1)S(1)} %collective-permute-done.6), channel_id=1, source_target_pairs={{0,8},{8,0},{16,24},{24,16},{1,9},{9,1},{17,25},{25,17},{2,10},{10... | collective-permute-start | bytes 1118216 | tf_op jit(solution)/shard_map/ppermute | solution.py:56
  545.4 22.2 %collective-permute-start.13 = (bf16[192,1216]{1,0:T(8,128)(2,1)S(1)}, bf16[192,1216]{1,0:T(8,128)(2,1)S(1)}, u32[]{:S(2)}, u32[]{:S(2)}) collective-permute-start(bf16[192,1216]{1,0:T(8,128)(2,1)S(1)} %collective-permute-done.12), channel_id=1, source_target_pairs={{0,8},{8,0},{16,24},{24,16},{1,9},{9,1},{17,25},{25,17},{2,10},{10... | collective-permute-start | bytes 1400840 | tf_op jit(solution)/shard_map/ppermute | solution.py:56
  545.4 22.1 %collective-permute-start.14 = (bf16[192,1216]{1,0:T(8,128)(2,1)S(1)}, bf16[192,1216]{1,0:T(8,128)(2,1)S(1)}, u32[]{:S(2)}, u32[]{:S(2)}) collective-permute-start(bf16[192,1216]{1,0:T(8,128)(2,1)S(1)} %collective-permute-done.12), channel_id=1, source_target_pairs={{0,16},{8,24},{16,0},{24,8},{1,17},{9,25},{17,1},{25,9},{2,18},{10... | collective-permute-start | bytes 1400840 | tf_op jit(solution)/shard_map/ppermute | solution.py:56
  557.4 10.1 %collective-permute-start.11 = (bf16[2,192,1216]{2,1,0:T(8,128)(2,1)S(1)}, bf16[2,192,1216]{2,1,0:T(8,128)(2,1)S(1)}, u32[]{:S(2)}, u32[]{:S(2)}) collective-permute-start(bf16[2,192,1216]{2,1,0:T(8,128)(2,1)S(1)} %collective-permute-done.10), channel_id=1, source_target_pairs={{0,8},{8,0},{16,24},{24,16},{1,9},{9,1},{17,25},{25,17},{2,10},{10... | collective-permute-start | bytes 2801672 | tf_op jit(solution)/shard_map/ppermute | solution.py:56
  567.5 1.9 collective-permute-start.15
  567.5 1.9 copy-start.3
  579.2 5.9 copy-start.10
  (5 other events, 6.4 us)
Sparse Core Ops, SparseCore 0:
  156.4 109.8 all-gather.1
  268.6 83.5 reduce-scatter.3
  354.5 104.8 reduce-scatter.5
  481.5 33.9 reduce-scatter.7

commit v4 on v3

--- a/solution.py
+++ b/solution.py
@@ -170,8 +170,9 @@
     rows = blocks.shape[1]
     halves = (pl.ds(0, rows // 2), pl.ds(rows // 2, rows // 2))
     to_x = [link.send(blocks.at[0, half], blocks.at[2, half], over_x) for half in halves]
+    last = [link.send(blocks.at[0], blocks.at[1], core)]
+    yield
     to_y = [link.send(blocks.at[0, half], blocks.at[4, half], over_y) for half in halves[::-1]]
-    last = [link.send(blocks.at[0], blocks.at[1], core)]
     yield
     to_x[0].wait_recv()
     diagonal = [link.send(blocks.at[2, halves[0]], blocks.at[6, halves[0]], over_y)]
@@ -199,6 +200,7 @@
     proj,
     ff_own,
     ff_down,
+    second,
     cosines,
     sines,
     seg_col,
@@ -209,6 +211,7 @@
     proj_mine,
     ff_all,
     ff_rows,
+    second_out,
     normed,
     queries,
     keys,
@@ -244,8 +247,10 @@
     greet((*ids, {"seq": far}, below, above))
     link = Sender(send_sems, recv_sems)
 
-    own_copy = pltpu.make_async_copy(ff_own.at[pair], ff_all.at[at, pair], local_sem)
+    own_copy = pltpu.make_async_copy(ff_own.at[pair], ff_all.at[at, pair], local_sem.at[0])
     own_copy.start()
+    second_copy = pltpu.make_async_copy(second, second_out, local_sem.at[1])
+    second_copy.start()
     ff_line[at] = ff_down[...]
     tokens_all[me] = tokens[...]
     qkv_all[at, pair] = qkv[...]
@@ -319,8 +324,9 @@
         proj_onward.wait_recv()
         if k < line - 1:
             proj_onward = along_line(proj_all, k)
+        if k == line - 2:
+            pump(2)
     turned.append(link.send(ff_own.at[1 - pair], ff_all.at[at, pair], over_y))
-    pump(2)
     for copy, half in zip(to_x, halves):
         copy.wait_recv()
         last.append(link.send(tokens_all.at[across, half], tokens_all.at[across, half], core))
@@ -328,6 +334,8 @@
         copy.wait_recv()
     proj_over = [to_partner(proj_all, k) for k in range(line)]
     cots[0] = cotangent[...]
+    gather_cots = plane_gather(link, cots, ids)
+    next(gather_cots)
 
     for z in range(line):
         for y in range(2):
@@ -387,7 +395,6 @@
         link.send(proj_all.at[pl.ds(target * group, group)], proj_mine.at[me], {"seq": target})
         for target in others
     ]
-    gather_cots = plane_gather(link, cots, ids)
     next(gather_cots)
     proj_mine[me] = proj_all[pl.ds(me * group, group)]
 
@@ -405,7 +412,7 @@
             mixture = dot((exponent / total).astype(LOW), values[:last_key, :])
             merged[here, head * HD : (head + 1) * HD] = mixture.astype(LOW)
             logsum[head, here, :] = highest + jnp.log(total)
-        pump(1)
+    pump(2)
     for copy in exchange:
         copy.wait_recv()
     quarter = proj.shape[1]
@@ -416,10 +423,11 @@
                 merged[block * rows : (block + 1) * rows, :], columns
             ).astype(LOW)
 
-    pump(6)
+    pump(1)
     next(gather_cots)
     pump(3 * line)
     own_copy.wait()
+    second_copy.wait()
     for source in others:
         for member in range(group):
             pltpu.make_async_remote_copy(
@@ -458,6 +466,7 @@
         (like(4, group, 2, *proj.shape), vmem),
         (like(line, *ff[0].shape), hbm),
         (like(4, group, *ff[1].shape), vmem),
+        (like(*ff[2].shape), hbm),
         (like(4, *block), vmem),
         (like(per_dev, *heads), vmem),
         (like(*heads), vmem),
@@ -471,7 +480,7 @@
     return pl.pallas_call(
         functools.partial(opening_kernel, (owned, vector_size, per_dev, group)),
         out_shape=[shape for shape, _ in outs],
-        in_specs=[vmem] * 10,
+        in_specs=[vmem] * 6 + [hbm] + [vmem] * 4,
         out_specs=[place for _, place in outs],
         scratch_shapes=[
             pltpu.VMEM((line, 2, *qkv.shape), LOW),
@@ -482,7 +491,7 @@
             pltpu.SemaphoreType.DMA((copies,)),
             pltpu.SemaphoreType.DMA((line,)),
             pltpu.SemaphoreType.DMA((4 * group,)),
-            pltpu.SemaphoreType.DMA,
+            pltpu.SemaphoreType.DMA((2,)),
         ],
         cost_estimate=pl.CostEstimate(
             flops=100_000_000_000, bytes_accessed=40_000_000, transcendentals=4_000_000
@@ -544,8 +553,8 @@
         mids_in, cots_in, whole_in, out_before, mid_before, *refs = refs
     else:
         mids_in, cots_in, weight_in, rows_in, *refs = refs
-    term, out, mid, mids, cots, weight, rows, down, act, grad, part, stage, *refs = refs
-    before, load_sems, weight_sems, stage_sems, before_sems, send_sems, recv_sems = refs
+    term, out, mid, mids, cots, weight, rows, down, act, grad, stage, *refs = refs
+    before, ahead, load_sems, weight_sems, stage_sems, before_sems, send_sems, recv_sems = refs
     (me, sibling, across), ids = neighbours()
     far = across + 1 - 2 * (across % 2)
     others = (sibling, across, far)
@@ -578,6 +587,15 @@
         load(cots_in.at[t], cots.at[t], load_sems.at[1, t])
     for copy in loads:
         copy.wait()
+
+    def forward(t, carry):
+        pltpu.make_async_copy(mids_in.at[t], mids.at[t], load_sems.at[0, t]).wait()
+        ahead[t] = dot(mids[t], weight[...].reshape(width, cols))
+        return carry
+
+    early = ahead.shape[0]
+    if follows:
+        lax.fori_loop(0, early, forward, 0)
     for copy in sent:
         copy.wait_recv()
     for k in range(4):
@@ -588,10 +606,13 @@
                     k, member, :, j * units : (j + 1) * units
                 ]
 
-    def tokens(t, carry):
-        pltpu.make_async_copy(mids_in.at[t], mids.at[t], load_sems.at[0, t]).wait()
+    def tokens(first, t, carry):
+        if first == 0 and follows:
+            gate_up = ahead[t]
+        else:
+            pltpu.make_async_copy(mids_in.at[t], mids.at[t], load_sems.at[0, t]).wait()
+            gate_up = dot(mids[t], weight[...].reshape(width, cols))
         pltpu.make_async_copy(cots_in.at[t], cots.at[t], load_sems.at[1, t]).wait()
-        gate_up = dot(mids[t], weight[...].reshape(width, cols))
         grad_act = dot(cots[t], down[...])
         gate, upward = gate_up[:, : cols // 2], gate_up[:, cols // 2 :]
         sigmoid_gate = jax.nn.sigmoid(gate)
@@ -603,7 +624,11 @@
         grad[t, :, cols // 2 :] = (grad_act * silu).astype(LOW)
         return carry
 
-    lax.fori_loop(0, count, tokens, 0)
+    if follows:
+        lax.fori_loop(0, early, functools.partial(tokens, 0), 0)
+        lax.fori_loop(early, count, functools.partial(tokens, early), 0)
+    else:
+        lax.fori_loop(0, count, functools.partial(tokens, 0), 0)
 
     all_act = act[...].reshape(count * block, cols // 2)
     for k in range(4):
@@ -612,13 +637,13 @@
         ).astype(LOW)
         for member in range(group):
             for j in range(fold):
-                part[k, member, :, j * units : (j + 1) * units] = value[
+                rows[k, member, :, j * units : (j + 1) * units] = value[
                     j * owned : (j + 1) * owned, member * units : (member + 1) * units
                 ]
     sent = [
-        link.send(part.at[k], term.at[pl.ds(me * group, group), 2], {"seq": k}) for k in others
+        link.send(rows.at[k], term.at[pl.ds(me * group, group), 2], {"seq": k}) for k in others
     ]
-    term[pl.ds(me * group, group), 2] = part[me]
+    term[pl.ds(me * group, group), 2] = rows[me]
     all_grad = grad[...].reshape(count * block, cols)
     for z in range(line):
         value = column_product(
@@ -694,7 +719,6 @@
         (width, cols // 2),
         (count, block, cols // 2),
         (count, block, cols),
-        rows,
         (2, 2, block, width),
         (2, 2, block, width),
     ]
@@ -709,6 +733,7 @@
         out_specs=[vmem, hbm, hbm],
         scratch_shapes=[pltpu.VMEM(shape, LOW) for shape in low_scratch]
         + [
+            pltpu.VMEM((count // 2 if follows else 1, block, cols), F32),
             pltpu.SemaphoreType.DMA((2, count)),
             pltpu.SemaphoreType.DMA((line + 1,)),
             pltpu.SemaphoreType.DMA((2, 2)),
@@ -759,6 +784,88 @@
     for copy in local:
         copy.wait()
     yield
+
+
+def output_kernel(
+    terms_in,
+    hidden,
+    ff_sum,
+    block_out,
+    hidden_blocks,
+    down_blocks,
+    terms,
+    arrived,
+    held,
+    from_x,
+    from_y,
+    corner,
+    send_sems,
+    recv_sems,
+    load_sems,
+    local_sems,
+):
+    _, ids = neighbours()
+    core, over_x, over_y = ids
+    pair = lax.axis_index("fsdp") % 2
+    greet(ids)
+    link = Sender(send_sems, recv_sems)
+    order = (7, 6, 5, 4, 3, 2, 1, 0)
+    loads = {k: pltpu.make_async_copy(terms_in.at[k], terms.at[k], load_sems.at[k]) for k in order}
+    for k in order:
+        loads[k].start()
+    spread = spread_blocks(link, ids, pair, ff_sum, hidden_blocks, down_blocks, local_sems)
+    next(spread)
+    halved = {}
+    for k in (6, 4, 2, 0):
+        loads[k + 1].wait()
+        halved[k] = link.send(terms.at[k + 1], arrived.at[k // 2], core)
+
+    def chip_sum(k):
+        loads[k].wait()
+        halved[k].wait_recv()
+        return terms[k].astype(F32) + arrived[k // 2].astype(F32)
+
+    held[0] = chip_sum(6).astype(LOW)
+    turn = link.send(held.at[0], corner, over_y)
+    held[1] = chip_sum(4).astype(LOW)
+    direct = link.send(held.at[1], from_y, over_y)
+    total = chip_sum(2)
+    turn.wait_recv()
+    held[2] = (total + corner[...].astype(F32)).astype(LOW)
+    last = link.send(held.at[2], from_x, over_x)
+    next(spread)
+    total = hidden[...] + chip_sum(0)
+    direct.wait_recv()
+    last.wait_recv()
+    total = total + from_x[...].astype(F32) + from_y[...].astype(F32)
+    block_out[...] = total.astype(LOW)
+    next(spread)
+    next(spread)
+    link.finish()
+
+
+def spread(ff_sum, terms, hidden):
+    hbm, vmem = (pl.BlockSpec(memory_space=pl.ANY), pl.BlockSpec(memory_space=pltpu.VMEM))
+    shapes = [jax.ShapeDtypeStruct((count, *ff_sum.shape[1:]), LOW) for count in (8, 4)]
+    sems = [pltpu.SemaphoreType.DMA((18,))] * 2
+    block = hidden.shape
+    return pl.pallas_call(
+        output_kernel,
+        out_shape=[jax.ShapeDtypeStruct(block, LOW), *shapes],
+        in_specs=[hbm, vmem, vmem],
+        out_specs=[vmem, hbm, hbm],
+        scratch_shapes=[
+            pltpu.VMEM(shape, LOW)
+            for shape in (terms.shape, (4, *block), (3, *block), block, block, block)
+        ]
+        + [*sems, pltpu.SemaphoreType.DMA((8,)), pltpu.SemaphoreType.DMA((2,))],
+        compiler_params=pltpu.CompilerParams(
+            collective_id=5, has_side_effects=True, vmem_limit_bytes=32 << 20
+        ),
+        cost_estimate=pl.CostEstimate(
+            flops=50_000_000_000, bytes_accessed=20_000_000, transcendentals=0
+        ),
+    )(terms, hidden, ff_sum)
 
 
 def closing_kernel(
@@ -1236,6 +1343,10 @@
     for low, high in cuts:
         by_owner = [ff_columns(low, high, pair) for pair in range(2)]
         ff_sent.append((by_owner, folded(jnp.transpose(down_cols[low:high]))))
+    (by_owner, second_down) = ff_sent[1]
+    kept, given = pick(odd, *by_owner)
+    second_sent = jnp.stack([*by_pair(kept, swap(given, "fsdp", 1)), second_down])
+
     segment_row = segment_ids[0]
     doc_starts = jnp.sum((segment_row[None, :] < segment_row[:, None]).astype(jnp.int32), axis=1)
     places = jnp.arange(seq_len, dtype=jnp.int32) - doc_starts
@@ -1253,6 +1364,7 @@
         proj_mine,
         first_all,
         first_rows,
+        second_sent,
         normed_in,
         queries,
         head_keys,
@@ -1266,22 +1378,13 @@
         cotangent[0],
         jnp.concatenate([qkv_own, vector], axis=0),
         lax.dynamic_slice_in_dim(proj_weight, place * quarter, quarter, 1),
-        (jnp.stack(ff_sent[0][0]), ff_sent[0][1]),
+        (jnp.stack(ff_sent[0][0]), ff_sent[0][1], second_sent),
         (cosines, sines),
         (segment_row[:, None], segment_row[None]),
         (owned, vector_size, per_dev, group, line),
     )
-    (by_owner, second_down) = ff_sent[1]
-    kept, given = pick(odd, *by_owner)
-    second_sent = jnp.stack([*by_pair(kept, swap(given, "fsdp", 1)), second_down])
-    second_all = line_gather(second_sent + nought(vectors[0, 0]))
-
+    second_all = line_gather(second_sent)
     hidden_in, mids = middle(attended, tokens[0], vectors)
-
-    def plane_reduce(total):
-        parts = [total[k] for k in range(2 * seq_count)]
-        away = seq_reduce(parts[seq_count:]).astype(LOW)
-        return seq_reduce(parts[:seq_count]) + swap(away, "fsdp", 1).astype(F32)
 
     spans = [high - low for low, high in cuts]
     first_term, out_first, mid_first = cut_call(
@@ -1316,21 +1419,15 @@
         ),
         (owned, vector_rows, qkv_weight.shape[1], per_dev, group, line),
     )
-    block_out = (hidden_in + plane_reduce(out)).astype(LOW)
-
     places_here = jnp.stack([place, lax.axis_index("fsdp") % 2]).astype(jnp.int32)
-    attn_sum = line_reduce(attn_term + nought(sums[1][0, 0, 0]))
-    second_sum = sums[1] + nought(attn_sum[0, 0])
-    kept, given = pick(odd, second_sum[0], second_sum[1])
-    here = seq_blocks(jnp.stack([kept, second_sum[2]]))
-    hidden_pieces = [
-        first_blocks[0],
-        jnp.stack([pair[0] for pair in here] + seq_blocks(swap(given, "fsdp", 1))),
-    ]
-    down_pieces = [first_blocks[1], jnp.stack([pair[1] for pair in here])]
+    attn_term = attn_term + nought(sums[1][0, 0, 0])
+    attn_sum = line_reduce(attn_term)
+    block_out, *second_blocks = spread(sums[1], out, hidden_in + nought(attn_term[0, 0, 0]))
+    hidden_pieces = [first_blocks[0], second_blocks[0]]
+    down_pieces = [first_blocks[1], second_blocks[1]]
     down_grad = down_call(places_here, down_pieces, fold)
     gate_up_grad = hidden_call(places_here, hidden_pieces, cuts, group)
-    attn_sums = seq_blocks(attn_sum)
+    attn_sums = seq_blocks(attn_sum + nought(block_out[0, 0]))
     proj_grad = columns_call(
         places_here, [jnp.stack([part[:owned, cols:] for part in attn_sums])]
     )

time: 601 us -> 584 us (0.972)
  waiting for transfers between devices: 75 us -> 14.1 us
  Pallas kernels: 440 us -> 491 us
  other arithmetic: 24 us -> 16.4 us
  starting transfers between devices: 12.5 us -> 5.88 us
    ppermute x16 -> x4, waiting for transfers between devices: 63.9 us -> 0.6 us  [swap(): lax.ppermute(value, axis, [(i, i ^ distance) for i in range(lax.axis_size...]
    pallas_call x0 -> x1, Pallas kernels: none -> 61.9 us  [spread(): pl.pallas_call(output_kernel, out_shape=[jax.ShapeDtypeStruct(block, LOW)...]
    pallas_call x1, Pallas kernels: 126 us -> 115 us  [opening(): pl.pallas_call(functools.partial(opening_kernel, (owned, vector_size, per...]
    unnamed x48 -> x56, local copies, waits for them, and re-layouts: 9.92 us -> 17.7 us
    ppermute x16 -> x4, starting transfers between devices: 11.4 us -> 5.32 us  [swap(): lax.ppermute(value, axis, [(i, i ^ distance) for i in range(lax.axis_size...]
  transfers between devices with their start and end apart: 20 -> 8, of which waited for: 10 -> 3; matrix products, arithmetic and copies ran while one was open for 6% -> 3% of each run, Pallas kernels for 72% -> 65%
where the time goes in v4:
time: 584 us; the launch traced here: 575 us
  Pallas kernels  491 us (84%)
  local copies, waits for them, and re-layouts  30.3 us (5%)
  between operations  16.5 us (3%)
  other arithmetic  16.4 us (3%)
  waiting for transfers between devices  14.1 us (2%)
  starting transfers between devices  5.88 us (1%)
    pallas_call x1, Pallas kernels, closing(): pl.pallas_call(functools.partial(closing_kernel, (owned, per_dev, group))...  125 us
    pallas_call x2, Pallas kernels, cut_call(): pl.pallas_call(functools.partial(cut_kernel, (follows, group, units)), ou...  122 us
    pallas_call x1, Pallas kernels, opening(): pl.pallas_call(functools.partial(opening_kernel, (owned, vector_size, per...  115 us
    pallas_call x1, Pallas kernels, spread(): pl.pallas_call(output_kernel, out_shape=[jax.ShapeDtypeStruct(block, LOW)...  61.9 us
    pallas_call x1, Pallas kernels, middle(): pl.pallas_call(middle_kernel, out_shape=[jax.ShapeDtypeStruct(block, F32)...  51.2 us
    unnamed x56, local copies, waits for them, and re-layouts  17.7 us
  transfers between devices with their start and end apart: 8, of which 3 were waited for; matrix products, arithmetic and copies ran while one was open for 3% of the time, Pallas kernels for 65%

profile of v4, /device:TPU:0, one launch (start us, length us, event | category | flops | bytes accessed | tf_op | source)
XLA Modules:
  0.0 574.6 jit_solution(6903892412300110102)
XLA Ops:
  7.3 1.8 constant_dynamic-slice_fusion.4
  10.1 3.0 collective-permute-start
  13.1 1.1 constant_dynamic-slice_fusion
  15.2 1.6 constant_dynamic-slice_fusion.9.proj
  18.6 1.7 constant_dynamic-slice_fusion.8
  23.0 2.9 sine_multiply_fusion
  25.9 1.5 select_bitcast_fusion.1
  27.4 1.3 pad_maximum_fusion.second
  28.7 115.1 %shard_map.169 = (bf16[4,256,1536]{2,1,0:T(8,128)(2,1)}, bf16[1536,512]{1,0:T(8,128)(2,1)}, f32[3,2048]{1,0:T(4,128)}, bf16[4,1,2,192,384]{4,3,2,1,0:T(8,128)(2,...) custom-call(bf16[256,1536]{1,0:T(8,128)(2,1)} %bitcast.41, ...), custom_call_target="tpu_custom_call" | custom-call | flops 99999997952 | bytes 40000000 | tf_op jit(solution)/shard_map/pallas_call | solution.py:480
  144.9 1.9 copy-done.4
  147.5 51.2 %shard_map.170 = (f32[256,1536]{1,0:T(8,128)S(1)}, bf16[8,256,1536]{2,1,0:T(8,128)(2,1)S(1)}) custom-call(bf16[4,256,1536]{2,1,0:T(8,128)(2,1)S(1)} %copy-done.4, bf16[256,1536]{1,0:T(8,128)(2,1)S(1)} %bitcast.42, f32[3,2048]{1,0:T(4,128)S(1)} %copy-done.12), custom_call_target="tpu_custom_call" | custom-call | tf_op jit(solution)/shard_map/pallas_call | solution.py:532
  198.8 1.1 copy-done.6
  199.9 2.7 copy-done.13
  202.6 45.8 %shard_map.171 = (bf16[4,3,192,1024]{3,2,1,0:T(8,128)(2,1)}, bf16[8,256,1536]{2,1,0:T(8,128)(2,1)}, bf16[8,256,1536]{2,1,0:T(8,128)(2,1)}) custom-call(bf16[8,256,1536]{2,1,0:T(8,128)(2,1)} %copy-done.13, bf16[8,256,1536]{2,1,0:T(8,128)(2,1)} %get-tuple-element.42.refs_1_, bf16[4,2,192,1024]{3,2,1,0:T(8,128)(2,1)} %get-tuple-element.44.refs_2_, ...), custom_call_target="tpu_custom_call" | custom-call | flops 49999998976 | bytes 40000000 | tf_op jit(solution)/shard_map/pallas_call | solution.py:725
  248.5 4.5 all-gather.3.cloned.1.call-done
  253.0 76.7 %shard_map.172 = (bf16[4,3,192,1216]{3,2,1,0:T(8,128)(2,1)}, bf16[8,256,1536]{2,1,0:T(8,128)(2,1)}, bf16[8,256,1536]{2,1,0:T(8,128)(2,1)}) custom-call(bf16[8,256,1536]{2,1,0:T(8,128)(2,1)} %copy-done.13, bf16[8,256,1536]{2,1,0:T(8,128)(2,1)} %get-tuple-element.42.refs_1_, bf16[4,3,192,1216]{3,2,1,0:T(8,128)(2,1)} %bitcast.52, ...), custom_call_target="tpu_custom_call" | custom-call | flops 49999998976 | bytes 40000000 | tf_op jit(solution)/shard_map/pallas_call | solution.py:725
  329.9 8.9 %reduce-scatter.4.cloned.1.call-done = bf16[1,3,192,1024]{3,2,1,0:T(8,128)(2,1)} async-done(((bf16[4,3,192,1024]{3,2,1,0:T(8,128)(2,1)}), bf16[1,3,192,1024]{3,2,1,0:T(8,128)(2,1)}) %reduce-scatter.4.cloned.1.call-update) | async-done | bytes 1179664 | tf_op jit(solution)/shard_map/reduce_scatter | solution.py:69
  338.8 124.7 %shard_map.173 = (f32[256,1536]{1,0:T(8,128)}, f32[2,1536]{1,0:T(2,128)}, bf16[4,208,896]{2,1,0:T(8,128)(2,1)}, bf16[8,192,1024]{2,1,0:T(8,128)(2,1)}, bf16[4,192,1024]{2,1,0:T(8,128)(2,1)}) custom-call(bf16[8,256,1536]{2,1,0:T(8,128)(2,1)} %get-tuple-element.50.mid_terms, f32[256,1536]{1,0:T(8,128)} %copy-done.6, bf16[256,1536]{1,0:T(8,128)(2,1)} %bitcast.55, ...), custom_call_target="tpu_custom_call" | custom-call | flops 99999997952 | bytes 40000000 | tf_op jit(solution)/shard_map/pallas_call | solution.py:1142
  463.6 1.2 slice.132
  465.5 1.6 broadcast_add_fusion.1
  469.1 1.2 copy-done.14
  470.3 2.8 copy-done.15
  473.1 61.9 %shard_map.174 = (bf16[256,1536]{1,0:T(8,128)(2,1)S(1)}, bf16[8,192,1216]{2,1,0:T(8,128)(2,1)S(1)}, bf16[4,192,1216]{2,1,0:T(8,128)(2,1)S(1)}) custom-call(bf16[8,256,1536]{2,1,0:T(8,128)(2,1)S(1)} %copy-done.15, f32[256,1536]{1,0:T(8,128)S(1)} %broadcast_add_fusion.hidden, bf16[3,192,1216]{2,1,0:T(8,128)(2,1)S(1)} %bitcast.44), custom_call_target="tpu_custom_call" | custom-call | flops 49999998976 | bytes 20000000 | tf_op jit(solution)/shard_map/pallas_call | solution.py:852
  535.1 1.9 copy-done.2
  539.1 1.8 add_bitcast_fusion
  540.8 1.8 collective-permute-start.1
  542.7 5.9 %shard_map.177 = f32[1120,1536]{1,0:T(8,128)} custom-call(s32[2]{0:T(128)S(1)} %pad_add_fusion.place, bf16[4,192,1024]{2,1,0:T(8,128)(2,1)S(1)} %copy-done.8, bf16[4,192,1216]{2,1,0:T(8,128)(2,1)S(1)} %get-tuple-element.68.refs_1_), custom_call_target="tpu_custom_call" | custom-call | tf_op jit(solution)/shard_map/pallas_call | solution.py:1227
  548.6 8.4 %shard_map.176 = f32[192,17920]{1,0:T(8,128)} custom-call(s32[2]{0:T(128)S(1)} %pad_add_fusion.place, bf16[8,192,1024]{2,1,0:T(8,128)(2,1)S(1)} %copy-done.5, bf16[8,192,1216]{2,1,0:T(8,128)(2,1)S(1)} %copy-done.3), custom_call_target="tpu_custom_call" | custom-call | tf_op jit(solution)/shard_map/pallas_call | solution.py:1263
  560.1 1.1 broadcast_select_fusion.9
  562.6 1.6 shard_map.175
  564.4 1.3 convert_element_type.41
  566.6 1.1 copy.43
  (98 shorter events, 16.9 us)
Async XLA Ops:
  7.2 7.4 %copy-start = (bf16[192,2048]{1,0:T(8,128)(2,1)S(1)}, bf16[192,2048]{1,0:T(8,128)(2,1)}, u32[]{:S(2)}) copy-start(bf16[192,2048]{1,0:T(8,128)(2,1)} %param.13) | copy-start | bytes 2359300
  7.2 245.8 %all-gather.3.cloned.1.call-start = ((), (), s32[]{:S(2)}) async-start(), calls=%async_computation.6 | async-start | bytes 7372800 | tf_op jit(solution)/shard_map/all_gather | solution.py:65
  10.1 15.8 %collective-permute-start = (bf16[192,1216]{1,0:T(8,128)(2,1)}, bf16[192,1216]{1,0:T(8,128)(2,1)}, u32[]{:S(2)}, u32[]{:S(2)}) collective-permute-start(bf16[192,1216]{1,0:T(8,128)(2,1)} %broadcast_select_fusion.1), channel_id=1, source_target_pairs={{0,1},{1,0},{2,3},{3,2},{4,5},{5,4},{6,7},{7,6},{8,9},{9,8},{10,11... | collective-permute-start | bytes 1400840 | tf_op jit(solution)/shard_map/ppermute | solution.py:56
  13.1 1.2 dynamic-slice-start
  14.2 0.7 copy-start.19
  14.2 0.7 copy-start.20
  14.2 0.7 copy-start.21
  14.5 2.3 copy-start.18
  143.7 1.1 copy-start.11
  143.8 195.1 %reduce-scatter.4.cloned.1.call-start = ((), (), s32[]{:S(2)}) async-start(), calls=%async_computation.3 | async-start | bytes 5898240 | tf_op jit(solution)/shard_map/reduce_scatter | solution.py:69
  144.9 1.9 copy-start.4
  146.8 0.8 copy-start.12
  198.7 1.1 copy-start.6
  199.9 2.7 copy-start.13
  248.4 215.2 %reduce-scatter.6.cloned.1.call-start = ((), (), s32[]{:S(2)}) async-start(), calls=%async_computation.4 | async-start | bytes 7372800 | tf_op jit(solution)/shard_map/reduce_scatter | solution.py:69
  329.7 209.3 %reduce-scatter.8.cloned.1.call-start = ((), (), s32[]{:S(2)}) async-start(), calls=%async_computation.5 | async-start | bytes 1863680 | tf_op jit(solution)/shard_map/reduce_scatter | solution.py:69
  465.5 3.5 copy-start.7
  467.1 1.1 copy-start.16
  469.0 1.4 copy-start.14
  470.3 2.8 copy-start.15
  473.1 69.6 %copy-start.8 = (bf16[4,192,1024]{2,1,0:T(8,128)(2,1)S(1)}, bf16[4,192,1024]{2,1,0:T(8,128)(2,1)}, u32[]{:S(2)}) copy-start(bf16[4,192,1024]{2,1,0:T(8,128)(2,1)} %get-tuple-element.67.refs_0_) | copy-start | bytes 4718596
  535.0 1.9 copy-start.2
  537.0 0.9 copy-start.9
  540.8 17.3 %collective-permute-start.1 = (bf16[208,896]{1,0:T(8,128)(2,1)}, bf16[208,896]{1,0:T(8,128)(2,1)}, u32[]{:S(2)}, u32[]{:S(2)}) collective-permute-start(bf16[208,896]{1,0:T(8,128)(2,1)} %add_bitcast_fusion), channel_id=1, source_target_pairs={{0,16},{8,24},{16,0},{24,8},{1,17},{9,25},{17,1},{25,9},{2,18},{10... | collective-permute-start | bytes 1118216 | tf_op jit(solution)/shard_map/ppermute | solution.py:56
  542.7 5.9 %copy-start.3 = (bf16[8,192,1216]{2,1,0:T(8,128)(2,1)S(1)}, bf16[8,192,1216]{2,1,0:T(8,128)(2,1)}, u32[]{:S(2)}) copy-start(bf16[8,192,1216]{2,1,0:T(8,128)(2,1)} %copy-done.2) | copy-start | bytes 11206660
  542.7 5.9 %copy-start.5 = (bf16[8,192,1024]{2,1,0:T(8,128)(2,1)S(1)}, bf16[8,192,1024]{2,1,0:T(8,128)(2,1)}, u32[]{:S(2)}) copy-start(bf16[8,192,1024]{2,1,0:T(8,128)(2,1)} %get-tuple-element.65.refs_0_) | copy-start | bytes 9437188
  557.0 2.4 collective-permute-start.3
  558.1 2.0 collective-permute-start.2
  564.3 1.5 copy-start.10
  564.4 2.2 copy-start.17
  565.8 2.0 copy-start.1
Sparse Core Ops, SparseCore 0:
  143.9 109.0 all-gather.2
  255.3 83.5 reduce-scatter.3
  341.2 104.8 reduce-scatter.5
  468.4 33.9 reduce-scatter.7

commit v5 on v4

--- a/solution.py
+++ b/solution.py
@@ -200,24 +200,30 @@
     proj,
     ff_own,
     ff_down,
-    second,
+    second_own,
+    second_down,
+    inverse,
+    seg_col,
+    seg_row,
     cosines,
     sines,
-    seg_col,
-    seg_row,
-    tokens_all,
+    tokens_out,
     weight,
     vectors,
     proj_mine,
     ff_all,
     ff_rows,
     second_out,
-    normed,
+    normed_out,
     queries,
     keys,
     values,
     merged,
     logsum,
+    part_out,
+    cots_out,
+    tokens_all,
+    normed,
     part,
     cots,
     qkv_all,
@@ -249,8 +255,15 @@
 
     own_copy = pltpu.make_async_copy(ff_own.at[pair], ff_all.at[at, pair], local_sem.at[0])
     own_copy.start()
-    second_copy = pltpu.make_async_copy(second, second_out, local_sem.at[1])
-    second_copy.start()
+    leaving = [own_copy]
+
+    def leave(source, target):
+        copy = pltpu.make_async_copy(source, target, local_sem.at[len(leaving)])
+        copy.start()
+        leaving.append(copy)
+
+    leave(second_own.at[pair], second_out.at[pair])
+    leave(second_down, second_out.at[2])
     ff_line[at] = ff_down[...]
     tokens_all[me] = tokens[...]
     qkv_all[at, pair] = qkv[...]
@@ -316,6 +329,15 @@
     to_x = [link.send(tokens_all.at[me, half], tokens_all.at[me, half], over_x) for half in halves]
     last.append(link.send(tokens_all.at[me], tokens_all.at[me], core))
     proj_onward = along_line(proj_all, 0)
+
+    lanes = lax.broadcasted_iota(jnp.int32, (rows, HD), 1)
+    for block in range(seq_count):
+        here = pl.ds(block * rows, rows)
+        before = jnp.sum((seg_row[...] < seg_col[here, :]).astype(F32), axis=1, keepdims=True)
+        index = (block * rows + lax.broadcasted_iota(jnp.int32, (rows, 1), 0)).astype(F32)
+        angles = (index - before) * inverse[...]
+        cosines[here, :] = jnp.cos(angles)
+        sines[here, :] = jnp.where(lanes < HD // 2, -jnp.sin(angles), jnp.sin(angles))
     for k in range(1, line):
         onward.wait_recv()
         if k < line - 1:
@@ -333,6 +355,8 @@
     for copy in last:
         copy.wait_recv()
     proj_over = [to_partner(proj_all, k) for k in range(line)]
+    second_over = link.send(second_own.at[1 - pair], second_out.at[pair], over_y)
+    leave(tokens_all, tokens_out)
     cots[0] = cotangent[...]
     gather_cots = plane_gather(link, cots, ids)
     next(gather_cots)
@@ -384,6 +408,7 @@
         plain = projected[:, head_cols:]
         kv[0, here, :] = jnp.where(holds_values, plain, rotate(plain)).astype(LOW)
     swapped = link.send(kv.at[0], kv.at[1], core)
+    leave(normed, normed_out)
     pump(3)
     swapped.wait_recv()
     keys[...] = jnp.where(holds_values, kv[1], kv[0])
@@ -423,11 +448,14 @@
                 merged[block * rows : (block + 1) * rows, :], columns
             ).astype(LOW)
 
+    leave(part, part_out)
     pump(1)
     next(gather_cots)
+    leave(cots, cots_out)
     pump(3 * line)
-    own_copy.wait()
-    second_copy.wait()
+    for copy in leaving:
+        copy.wait()
+    second_over.wait_recv()
     for source in others:
         for member in range(group):
             pltpu.make_async_remote_copy(
@@ -447,7 +475,7 @@
     link.finish()
 
 
-def opening(tokens, cotangent, qkv, proj, ff, tables, segments, sizes):
+def opening(tokens, cotangent, qkv, proj, ff, inverse, segments, sizes):
     owned, vector_size, per_dev, group, line = sizes
     rows, width = tokens.shape
     block = (rows, width)
@@ -460,29 +488,35 @@
         return jax.ShapeDtypeStruct(shape, dtype)
 
     outs = [
-        (like(4, *block), vmem),
+        (like(*heads, dtype=F32), vmem),
+        (like(*heads, dtype=F32), vmem),
+        (like(4, *block), hbm),
         (like(width, cols), vmem),
         (like(3, max(width, 2048), dtype=F32), vmem),
         (like(4, group, 2, *proj.shape), vmem),
         (like(line, *ff[0].shape), hbm),
         (like(4, group, *ff[1].shape), vmem),
-        (like(*ff[2].shape), hbm),
-        (like(4, *block), vmem),
+        (like(3, *ff[2].shape[1:]), hbm),
+        (like(4, *block), hbm),
         (like(per_dev, *heads), vmem),
         (like(*heads), vmem),
         (like(*heads), vmem),
         (like(seq_len, per_dev * HD), vmem),
         (like(per_dev, seq_len, 1, dtype=F32), vmem),
-        (like(4, *block), vmem),
-        (like(8, *block), vmem),
+        (like(4, *block), hbm),
+        (like(8, *block), hbm),
     ]
     copies = 10 * line + 40
     return pl.pallas_call(
         functools.partial(opening_kernel, (owned, vector_size, per_dev, group)),
         out_shape=[shape for shape, _ in outs],
-        in_specs=[vmem] * 6 + [hbm] + [vmem] * 4,
+        in_specs=[vmem] * 6 + [hbm] * 2 + [vmem] * 3,
         out_specs=[place for _, place in outs],
         scratch_shapes=[
+            pltpu.VMEM((4, *block), LOW),
+            pltpu.VMEM((4, *block), LOW),
+            pltpu.VMEM((4, *block), LOW),
+            pltpu.VMEM((8, *block), LOW),
             pltpu.VMEM((line, 2, *qkv.shape), LOW),
             pltpu.VMEM((line, 2, *proj.shape), LOW),
             pltpu.VMEM((line, *ff[1].shape), LOW),
@@ -491,15 +525,15 @@
             pltpu.SemaphoreType.DMA((copies,)),
             pltpu.SemaphoreType.DMA((line,)),
             pltpu.SemaphoreType.DMA((4 * group,)),
-            pltpu.SemaphoreType.DMA((2,)),
+            pltpu.SemaphoreType.DMA((8,)),
         ],
         cost_estimate=pl.CostEstimate(
             flops=100_000_000_000, bytes_accessed=40_000_000, transcendentals=4_000_000
         ),
         compiler_params=pltpu.CompilerParams(
-            collective_id=0, has_side_effects=True, vmem_limit_bytes=56 << 20
+            collective_id=0, has_side_effects=True, vmem_limit_bytes=58 << 20
         ),
-    )(tokens, cotangent, qkv, proj, *ff, *tables, *segments)
+    )(tokens, cotangent, qkv, proj, *ff, inverse, *segments)
 
 
 def middle_kernel(
@@ -542,7 +576,7 @@
             pltpu.SemaphoreType.DMA((16,)),
         ],
         compiler_params=pltpu.CompilerParams(
-            collective_id=1, has_side_effects=True, vmem_limit_bytes=32 << 20
+            collective_id=1, has_side_effects=True, vmem_limit_bytes=58 << 20
         ),
     )(part, tokens, vectors)
 
@@ -742,7 +776,7 @@
             pltpu.SemaphoreType.DMA((6,)),
         ],
         compiler_params=pltpu.CompilerParams(
-            collective_id=4 if follows else 3, has_side_effects=True, vmem_limit_bytes=56 << 20
+            collective_id=4 if follows else 3, has_side_effects=True, vmem_limit_bytes=58 << 20
         ),
         cost_estimate=pl.CostEstimate(
             flops=50_000_000_000, bytes_accessed=40_000_000, transcendentals=2_000_000
@@ -759,7 +793,6 @@
     ]
     for copy in local:
         copy.start()
-    over = link.send(ff_sum.at[1 - pair], hidden_blocks.at[4], over_y)
     to_x = [
         link.send(kept, hidden_blocks.at[2], over_x),
         link.send(down, down_blocks.at[2], over_x),
@@ -768,6 +801,8 @@
         link.send(kept, hidden_blocks.at[1], core),
         link.send(down, down_blocks.at[1], core),
     ]
+    yield
+    over = link.send(ff_sum.at[1 - pair], hidden_blocks.at[4], over_y)
     yield
     over.wait_recv()
     far = link.send(hidden_blocks.at[4], hidden_blocks.at[6], over_x)
@@ -790,6 +825,7 @@
     terms_in,
     hidden,
     ff_sum,
+    _,
     block_out,
     hidden_blocks,
     down_blocks,
@@ -814,11 +850,11 @@
     for k in order:
         loads[k].start()
     spread = spread_blocks(link, ids, pair, ff_sum, hidden_blocks, down_blocks, local_sems)
-    next(spread)
     halved = {}
     for k in (6, 4, 2, 0):
         loads[k + 1].wait()
         halved[k] = link.send(terms.at[k + 1], arrived.at[k // 2], core)
+    next(spread)
 
     def chip_sum(k):
         loads[k].wait()
@@ -827,6 +863,7 @@
 
     held[0] = chip_sum(6).astype(LOW)
     turn = link.send(held.at[0], corner, over_y)
+    next(spread)
     held[1] = chip_sum(4).astype(LOW)
     direct = link.send(held.at[1], from_y, over_y)
     total = chip_sum(2)
@@ -844,7 +881,7 @@
     link.finish()
 
 
-def spread(ff_sum, terms, hidden):
+def spread(ff_sum, terms, hidden, earlier):
     hbm, vmem = (pl.BlockSpec(memory_space=pl.ANY), pl.BlockSpec(memory_space=pltpu.VMEM))
     shapes = [jax.ShapeDtypeStruct((count, *ff_sum.shape[1:]), LOW) for count in (8, 4)]
     sems = [pltpu.SemaphoreType.DMA((18,))] * 2
@@ -852,7 +889,7 @@
     return pl.pallas_call(
         output_kernel,
         out_shape=[jax.ShapeDtypeStruct(block, LOW), *shapes],
-        in_specs=[hbm, vmem, vmem],
+        in_specs=[hbm, vmem, vmem, hbm],
         out_specs=[vmem, hbm, hbm],
         scratch_shapes=[
             pltpu.VMEM(shape, LOW)
@@ -860,21 +897,21 @@
         ]
         + [*sems, pltpu.SemaphoreType.DMA((8,)), pltpu.SemaphoreType.DMA((2,))],
         compiler_params=pltpu.CompilerParams(
-            collective_id=5, has_side_effects=True, vmem_limit_bytes=32 << 20
+            collective_id=5, has_side_effects=True, vmem_limit_bytes=58 << 20
         ),
         cost_estimate=pl.CostEstimate(
             flops=50_000_000_000, bytes_accessed=20_000_000, transcendentals=0
         ),
-    )(terms, hidden, ff_sum)
+    )(terms, hidden, ff_sum, earlier)
 
 
 def closing_kernel(
     shape,
-    mid_terms,
+    terms_in,
     hidden,
     upstream,
-    tokens_all,
-    normed,
+    tokens_in,
+    normed_in,
     vectors,
     weight,
     proj_mine,
@@ -893,6 +930,9 @@
     attn_sum,
     hidden_blocks,
     down_blocks,
+    mid_terms,
+    tokens_all,
+    normed,
     arrived,
     held,
     from_x,
@@ -916,6 +956,7 @@
     send_sems,
     recv_sems,
     local_sems,
+    load_sems,
 ):
     owned, per_dev, group = shape
     (me, sibling, across), (core, over_x, over_y) = neighbours()
@@ -930,9 +971,23 @@
     greet((core, over_x, {"seq": far}, over_y))
     link = Sender(send_sems, recv_sems)
 
-    halved = {k: link.send(mid_terms.at[k + 1], arrived.at[k // 2], core) for k in (6, 2, 4, 0)}
+    loads = {}
+    for k in (7, 3, 5, 1, 6, 2, 4, 0):
+        loads[k] = pltpu.make_async_copy(terms_in.at[k], mid_terms.at[k], load_sems.at[k])
+        loads[k].start()
+    kept_loads = [
+        pltpu.make_async_copy(source, target, load_sems.at[8 + number])
+        for number, (source, target) in enumerate(((tokens_in, tokens_all), (normed_in, normed)))
+    ]
+    for copy in kept_loads:
+        copy.start()
+    halved = {}
+    for k in (6, 2, 4, 0):
+        loads[k + 1].wait()
+        halved[k] = link.send(mid_terms.at[k + 1], arrived.at[k // 2], core)
 
     def chip_sum(k):
+        loads[k].wait()
         halved[k].wait_recv()
         return mid_terms[k].astype(F32) + arrived[k // 2].astype(F32)
 
@@ -993,6 +1048,7 @@
         link, (core, over_x, over_y), pair, ff_sum, hidden_blocks, down_blocks, local_sems
     )
     next(spread)
+    next(spread)
 
     grad_keys[...] = jnp.zeros_like(grad_keys)
     grad_values[...] = jnp.zeros_like(grad_values)
@@ -1014,6 +1070,8 @@
             grad_keys[:last_key, :] += column_product(grad_scores, query)
             grad_values[:last_key, :] += column_product(probs.astype(LOW), upper_head)
     next(spread)
+    for copy in kept_loads:
+        copy.wait()
     holds_values = me % 2 == 1
     key_copy = (grad_keys[...] * scale).astype(LOW)
     value_copy = grad_values[...].astype(LOW)
@@ -1130,6 +1188,9 @@
         jax.ShapeDtypeStruct((4, *args[-1].shape[1:]), LOW),
     ]
     low_scratch = [
+        (8, *block),
+        (4, *block),
+        (4, *block),
         (4, *block),
         (3, *block),
         block,
@@ -1142,7 +1203,10 @@
     return pl.pallas_call(
         functools.partial(closing_kernel, (owned, per_dev, group)),
         out_shape=outs,
-        in_specs=[pl.BlockSpec(memory_space=pltpu.VMEM)] * len(args),
+        in_specs=[
+            pl.BlockSpec(memory_space=pl.ANY if k in (0, 3, 4) else pltpu.VMEM)
+            for k in range(len(args))
+        ],
         out_specs=[pl.BlockSpec(memory_space=pltpu.VMEM)] * (len(outs) - 2)
         + [pl.BlockSpec(memory_space=pl.ANY)] * 2,
         scratch_shapes=[pltpu.VMEM(shape, LOW) for shape in low_scratch]
@@ -1168,7 +1232,7 @@
             )
         ]
         + [pltpu.SemaphoreType.DMA((48,))] * 2
-        + [pltpu.SemaphoreType.DMA((2,))],
+        + [pltpu.SemaphoreType.DMA((2,)), pltpu.SemaphoreType.DMA((10,))],
         compiler_params=pltpu.CompilerParams(
             collective_id=2, has_side_effects=True, vmem_limit_bytes=58 << 20
         ),
@@ -1343,21 +1407,13 @@
     for low, high in cuts:
         by_owner = [ff_columns(low, high, pair) for pair in range(2)]
         ff_sent.append((by_owner, folded(jnp.transpose(down_cols[low:high]))))
-    (by_owner, second_down) = ff_sent[1]
-    kept, given = pick(odd, *by_owner)
-    second_sent = jnp.stack([*by_pair(kept, swap(given, "fsdp", 1)), second_down])
-
     segment_row = segment_ids[0]
-    doc_starts = jnp.sum((segment_row[None, :] < segment_row[:, None]).astype(jnp.int32), axis=1)
-    places = jnp.arange(seq_len, dtype=jnp.int32) - doc_starts
     inverse = THETA ** (-2.0 * jnp.arange(HD // 2, dtype=F32) / HD)
-    angles = places.astype(F32)[:, None] * inverse[None, :]
-    angles = jnp.concatenate([angles, angles], axis=-1)
-    cosines = jnp.cos(angles)
-    signs = jnp.where(jnp.arange(HD) < HD // 2, -1.0, 1.0).astype(F32)
-    sines = jnp.sin(angles) * signs
+    inverse = jnp.concatenate([inverse, inverse])[None]
 
     (
+        cosines,
+        sines,
         tokens_all,
         qkv_mine,
         vectors,
@@ -1378,8 +1434,8 @@
         cotangent[0],
         jnp.concatenate([qkv_own, vector], axis=0),
         lax.dynamic_slice_in_dim(proj_weight, place * quarter, quarter, 1),
-        (jnp.stack(ff_sent[0][0]), ff_sent[0][1], second_sent),
-        (cosines, sines),
+        [part for by_owner, rows in ff_sent for part in (jnp.stack(by_owner), rows)],
+        inverse,
         (segment_row[:, None], segment_row[None]),
         (owned, vector_size, per_dev, group, line),
     )
@@ -1422,7 +1478,7 @@
     places_here = jnp.stack([place, lax.axis_index("fsdp") % 2]).astype(jnp.int32)
     attn_term = attn_term + nought(sums[1][0, 0, 0])
     attn_sum = line_reduce(attn_term)
-    block_out, *second_blocks = spread(sums[1], out, hidden_in + nought(attn_term[0, 0, 0]))
+    block_out, *second_blocks = spread(sums[1], out, hidden_in, attn_term)
     hidden_pieces = [first_blocks[0], second_blocks[0]]
     down_pieces = [first_blocks[1], second_blocks[1]]
     down_grad = down_call(places_here, down_pieces, fold)

time: 584 us -> 560 us (0.959)
  local copies, waits for them, and re-layouts: 30.3 us -> 17.1 us
    unnamed x56 -> x30, local copies, waits for them, and re-layouts: 17.7 us -> 5.24 us
    pallas_call x1, Pallas kernels: 51.2 us -> 57.6 us  [middle(): pl.pallas_call(middle_kernel, out_shape=[jax.ShapeDtypeStruct(block, F32)...]
  transfers between devices with their start and end apart: 8 -> 7, of which waited for: 3 -> 4; matrix products, arithmetic and copies ran while one was open for 3% -> 0% of each run, Pallas kernels for 65% -> 68%
where the time goes in v5:
time: 560 us; the launch traced here: 553 us
  Pallas kernels  489 us (87%)
  waiting for transfers between devices  17.8 us (3%)
  local copies, waits for them, and re-layouts  17.1 us (3%)
  between operations  15.7 us (3%)
  other arithmetic  11.4 us (2%)
    pallas_call x1, Pallas kernels, closing(): pl.pallas_call(functools.partial(closing_kernel, (owned, per_dev, group))...  122 us
    pallas_call x2, Pallas kernels, cut_call(): pl.pallas_call(functools.partial(cut_kernel, (follows, group, units)), ou...  122 us
    pallas_call x1, Pallas kernels, opening(): pl.pallas_call(functools.partial(opening_kernel, (owned, vector_size, per...  112 us
    pallas_call x1, Pallas kernels, spread(): pl.pallas_call(output_kernel, out_shape=[jax.ShapeDtypeStruct(block, LOW)...  59.3 us
    pallas_call x1, Pallas kernels, middle(): pl.pallas_call(middle_kernel, out_shape=[jax.ShapeDtypeStruct(block, F32)...  57.6 us
  transfers between devices with their start and end apart: 7, of which 4 were waited for; matrix products, arithmetic and copies ran while one was open for 0% of the time, Pallas kernels for 68%

profile of v5, /device:TPU:0, one launch (start us, length us, event | category | flops | bytes accessed | tf_op | source)
XLA Modules:
  0.0 553.4 jit_solution(14408710934500955910)
XLA Ops:
  7.3 1.0 copy-done
  9.2 1.0 constant_dynamic-slice_fusion
  10.2 1.1 dynamic-slice.1
  11.8 1.6 constant_dynamic-slice_fusion.9.proj
  13.4 1.0 copy.24.seg_col
  15.0 1.7 constant_dynamic-slice_fusion.4
  17.0 1.0 pad_maximum_fusion.second_own
  18.0 1.6 constant_dynamic-slice_fusion.8
  19.8 1.0 pad_maximum_fusion.1.ff_own
  20.8 0.9 pad_maximum_fusion.3.second_down
  21.7 0.8 pad_maximum_fusion.4.ff_down
  23.2 111.9 %shard_map.169 = (f32[1024,128]{1,0:T(8,128)}, f32[1024,128]{1,0:T(8,128)}, bf16[4,256,1536]{2,1,0:T(8,128)(2,1)}, bf16[1536,512]{1,0:T(8,128)(2,1)}, f32[3,2048...) custom-call(bf16[256,1536]{1,0:T(8,128)(2,1)} %bitcast.41, ...), custom_call_target="tpu_custom_call" | custom-call | flops 99999997952 | bytes 40000000 | tf_op jit(solution)/shard_map/pallas_call | solution.py:510
  135.4 57.6 %shard_map.170 = (f32[256,1536]{1,0:T(8,128)}, bf16[8,256,1536]{2,1,0:T(8,128)(2,1)}) custom-call(bf16[4,256,1536]{2,1,0:T(8,128)(2,1)} %get-tuple-element.41.part, bf16[256,1536]{1,0:T(8,128)(2,1)} %bitcast.42, f32[3,2048]{1,0:T(4,128)} %get-tuple-element.42.vectors), custom_call_target="tpu_custom_call" | custom-call | tf_op jit(solution)/shard_map/pallas_call | solution.py:566
  193.0 45.5 %shard_map.171 = (bf16[4,3,192,1024]{3,2,1,0:T(8,128)(2,1)}, bf16[8,256,1536]{2,1,0:T(8,128)(2,1)}, bf16[8,256,1536]{2,1,0:T(8,128)(2,1)}) custom-call(bf16[8,256,1536]{2,1,0:T(8,128)(2,1)} %get-tuple-element.43.refs_0_, bf16[8,256,1536]{2,1,0:T(8,128)(2,1)} %get-tuple-element.44.refs_1_, bf16[4,2,192,1024]{3,2,1,0:T(8,128)(2,1)} %get-tuple-element.46.refs_2_, ...), custom_call_target="tpu_custom_call" | custom-call | flops 49999998976 | bytes 40000000 | tf_op jit(solution)/shard_map/pallas_call | solution.py:759
  238.5 7.0 %all-gather.3.cloned.1.call-done = bf16[12,192,1216]{2,1,0:T(8,128)(2,1)} async-done(((bf16[3,192,1216]{2,1,0:T(8,128)(2,1)}), bf16[12,192,1216]{2,1,0:T(8,128)(2,1)}) %all-gather.3.cloned.1.call-update) | async-done | bytes 5603344 | tf_op jit(solution)/shard_map/all_gather | solution.py:65
  245.6 76.6 %shard_map.172 = (bf16[4,3,192,1216]{3,2,1,0:T(8,128)(2,1)}, bf16[8,256,1536]{2,1,0:T(8,128)(2,1)}, bf16[8,256,1536]{2,1,0:T(8,128)(2,1)}) custom-call(bf16[8,256,1536]{2,1,0:T(8,128)(2,1)} %get-tuple-element.43.refs_0_, bf16[8,256,1536]{2,1,0:T(8,128)(2,1)} %get-tuple-element.44.refs_1_, bf16[4,3,192,1216]{3,2,1,0:T(8,128)(2,1)} %bitcast.46, ...), custom_call_target="tpu_custom_call" | custom-call | flops 49999998976 | bytes 40000000 | tf_op jit(solution)/shard_map/pallas_call | solution.py:759
  322.4 9.1 %reduce-scatter.6.cloned.1.call-done = bf16[1,3,192,1024]{3,2,1,0:T(8,128)(2,1)} async-done(((bf16[4,3,192,1024]{3,2,1,0:T(8,128)(2,1)}), bf16[1,3,192,1024]{3,2,1,0:T(8,128)(2,1)}) %reduce-scatter.6.cloned.1.call-update) | async-done | bytes 1179664 | tf_op jit(solution)/shard_map/reduce_scatter | solution.py:69
  331.5 122.5 %shard_map.173 = (f32[256,1536]{1,0:T(8,128)}, f32[2,1536]{1,0:T(2,128)}, bf16[4,208,896]{2,1,0:T(8,128)(2,1)}, bf16[8,192,1024]{2,1,0:T(8,128)(2,1)}, bf16[4,192,1024]{2,1,0:T(8,128)(2,1)}) custom-call(bf16[8,256,1536]{2,1,0:T(8,128)(2,1)} %get-tuple-element.53.terms_in, f32[256,1536]{1,0:T(8,128)} %get-tuple-element.51.hidden, bf16[256,1536]{1,0:T(8,128)(2,1)} %bitcast.51, ...), custom_call_target="tpu_custom_call" | custom-call | flops 99999997952 | bytes 40000000 | tf_op jit(solution)/shard_map/pallas_call | solution.py:1203
  453.9 1.2 slice.128
  455.8 2.6 broadcast_add_fusion._
  458.5 59.3 %shard_map.174 = (bf16[256,1536]{1,0:T(8,128)(2,1)}, bf16[8,192,1216]{2,1,0:T(8,128)(2,1)}, bf16[4,192,1216]{2,1,0:T(8,128)(2,1)}) custom-call(bf16[8,256,1536]{2,1,0:T(8,128)(2,1)} %get-tuple-element.50.terms_in, f32[256,1536]{1,0:T(8,128)} %get-tuple-element.51.hidden, bf16[3,192,1216]{2,1,0:T(8,128)(2,1)} %bitcast.48, ...), custom_call_target="tpu_custom_call" | custom-call | flops 49999998976 | bytes 20000000 | tf_op jit(solution)/shard_map/pallas_call | solution.py:889
  517.8 1.2 slice.100
  519.7 1.0 add_bitcast_fusion
  520.7 1.1 collective-permute-start
  521.9 1.5 copy-done.4
  523.4 5.9 %shard_map.177 = f32[1120,1536]{1,0:T(8,128)} custom-call(s32[2]{0:T(128)S(1)} %pad_add_fusion.place, bf16[4,192,1024]{2,1,0:T(8,128)(2,1)S(1)} %copy-done.5, bf16[4,192,1216]{2,1,0:T(8,128)(2,1)S(1)} %copy-done.4), custom_call_target="tpu_custom_call" | custom-call | tf_op jit(solution)/shard_map/pallas_call | solution.py:1291
  529.4 8.4 %shard_map.176 = f32[192,17920]{1,0:T(8,128)} custom-call(s32[2]{0:T(128)S(1)} %pad_add_fusion.place, bf16[8,192,1024]{2,1,0:T(8,128)(2,1)S(1)} %copy-done.3, bf16[8,192,1216]{2,1,0:T(8,128)(2,1)S(1)} %copy-done.2), custom_call_target="tpu_custom_call" | custom-call | tf_op jit(solution)/shard_map/pallas_call | solution.py:1327
  538.4 1.1 collective-permute-done.2
  541.5 1.6 shard_map.175
  543.3 1.3 convert_element_type.21
  544.6 0.9 copy.39
  545.5 1.1 copy.40
  (62 shorter events, 6.5 us)
Async XLA Ops:
  7.2 1.1 copy-start
  7.2 6.2 %copy-start.8 = (s32[1,1024]{1,0:T(1,128)S(1)}, s32[1,1024]{1,0:T(1,128)}, u32[]{:S(2)}) copy-start(s32[1,1024]{1,0:T(1,128)} %seg_row.3) | copy-start | bytes 12292
  7.2 238.4 %all-gather.3.cloned.1.call-start = ((), (), s32[]{:S(2)}) async-start(), calls=%async_computation.6 | async-start | bytes 7372800 | tf_op jit(solution)/shard_map/all_gather | solution.py:65
  135.1 196.3 %reduce-scatter.6.cloned.1.call-start = ((), (), s32[]{:S(2)}) async-start(), calls=%async_computation.4 | async-start | bytes 5898240 | tf_op jit(solution)/shard_map/reduce_scatter | solution.py:69
  238.5 215.4 %reduce-scatter.4.cloned.1.call-start = ((), (), s32[]{:S(2)}) async-start(), calls=%async_computation.3 | async-start | bytes 7372800 | tf_op jit(solution)/shard_map/reduce_scatter | solution.py:69
  322.2 197.5 %reduce-scatter.8.cloned.1.call-start = ((), (), s32[]{:S(2)}) async-start(), calls=%async_computation.5 | async-start | bytes 1863680 | tf_op jit(solution)/shard_map/reduce_scatter | solution.py:69
  458.5 63.4 %copy-start.5 = (bf16[4,192,1024]{2,1,0:T(8,128)(2,1)S(1)}, bf16[4,192,1024]{2,1,0:T(8,128)(2,1)}, u32[]{:S(2)}) copy-start(bf16[4,192,1024]{2,1,0:T(8,128)(2,1)} %get-tuple-element.71.refs_0_) | copy-start | bytes 4718596
  520.7 17.2 %collective-permute-start = (bf16[208,896]{1,0:T(8,128)(2,1)S(1)}, bf16[208,896]{1,0:T(8,128)(2,1)S(1)}, u32[]{:S(2)}, u32[]{:S(2)}) collective-permute-start(bf16[208,896]{1,0:T(8,128)(2,1)S(1)} %add_bitcast_fusion), channel_id=1, source_target_pairs={{0,16},{8,24},{16,0},{24,8},{1,17},{9,25},{17,1},{25,9},{2,18},{10... | collective-permute-start | bytes 1118216 | tf_op jit(solution)/shard_map/ppermute | solution.py:56
  521.9 1.5 copy-start.4
  523.4 5.9 %copy-start.2 = (bf16[8,192,1216]{2,1,0:T(8,128)(2,1)S(1)}, bf16[8,192,1216]{2,1,0:T(8,128)(2,1)}, u32[]{:S(2)}) copy-start(bf16[8,192,1216]{2,1,0:T(8,128)(2,1)} %get-tuple-element.70.refs_1_) | copy-start | bytes 11206660
  523.4 5.9 %copy-start.3 = (bf16[8,192,1024]{2,1,0:T(8,128)(2,1)S(1)}, bf16[8,192,1024]{2,1,0:T(8,128)(2,1)}, u32[]{:S(2)}) copy-start(bf16[8,192,1024]{2,1,0:T(8,128)(2,1)} %get-tuple-element.69.refs_0_) | copy-start | bytes 9437188
  537.8 1.7 collective-permute-start.2
  537.9 2.0 collective-permute-start.1
  541.4 3.3 copy-start.7
  541.5 4.1 copy-start.6
  543.3 3.4 copy-start.1
Sparse Core Ops, SparseCore 0:
  135.3 110.2 all-gather.2
  247.9 83.5 reduce-scatter.5
  333.8 104.8 reduce-scatter.3
  458.6 33.9 reduce-scatter.7

commit v6 on v5

--- a/solution.py
+++ b/solution.py
@@ -584,11 +584,16 @@
 def cut_kernel(shape, *refs):
     follows, group, units = shape
     if follows:
-        mids_in, cots_in, whole_in, out_before, mid_before, *refs = refs
+        mids_in, cots_in, whole_in, out_before, mid_before, hidden_in, *refs = refs
     else:
         mids_in, cots_in, weight_in, rows_in, *refs = refs
-    term, out, mid, mids, cots, weight, rows, down, act, grad, stage, *refs = refs
-    before, ahead, load_sems, weight_sems, stage_sems, before_sems, send_sems, recv_sems = refs
+    term, out, mid, *refs = refs
+    if follows:
+        ahead, *refs = refs
+    mids, cots, weight, rows, down, act, grad, stage, before, *refs = refs
+    if follows:
+        odd, arrived, held, from_y, corner, total, slots, ahead_sems, *refs = refs
+    load_sems, weight_sems, stage_sems, before_sems, send_sems, recv_sems = refs
     (me, sibling, across), ids = neighbours()
     far = across + 1 - 2 * (across % 2)
     others = (sibling, across, far)
@@ -596,7 +601,8 @@
     count, block, width = mids.shape
     quarter = width // 4
     fold = quarter // owned
-    greet((ids[0], ids[1], {"seq": far}))
+    core, over_x, over_y = ids
+    greet((core, over_x, {"seq": far}, over_y))
     link = Sender(send_sems, recv_sems)
 
     def load(source, target, sem):
@@ -619,17 +625,33 @@
     for t in range(count):
         load(mids_in.at[t], mids.at[t], load_sems.at[0, t])
         load(cots_in.at[t], cots.at[t], load_sems.at[1, t])
+    if follows:
+        loads.append(load(hidden_in, total, ahead_sems.at[2]))
     for copy in loads:
         copy.wait()
 
+    def put(t):
+        return pltpu.make_async_copy(slots.at[t % 2], ahead.at[t], ahead_sems.at[t % 2])
+
+    def take(t):
+        return pltpu.make_async_copy(ahead.at[t], slots.at[t % 2], ahead_sems.at[t % 2])
+
     def forward(t, carry):
         pltpu.make_async_copy(mids_in.at[t], mids.at[t], load_sems.at[0, t]).wait()
-        ahead[t] = dot(mids[t], weight[...].reshape(width, cols))
+
+        @pl.when(t >= 2)
+        def _():
+            put(t - 2).wait()
+
+        slots[t % 2] = dot(mids[t], weight[...].reshape(width, cols))
+        put(t).start()
         return carry
 
-    early = ahead.shape[0]
     if follows:
-        lax.fori_loop(0, early, forward, 0)
+        lax.fori_loop(0, count, forward, 0)
+        for t in (count - 2, count - 1):
+            put(t).wait()
+        take(0).start()
     for copy in sent:
         copy.wait_recv()
     for k in range(4):
@@ -640,9 +662,15 @@
                     k, member, :, j * units : (j + 1) * units
                 ]
 
-    def tokens(first, t, carry):
-        if first == 0 and follows:
-            gate_up = ahead[t]
+    def tokens(t, carry):
+        if follows:
+
+            @pl.when(t + 1 < count)
+            def _():
+                take(t + 1).start()
+
+            take(t).wait()
+            gate_up = slots[t % 2]
         else:
             pltpu.make_async_copy(mids_in.at[t], mids.at[t], load_sems.at[0, t]).wait()
             gate_up = dot(mids[t], weight[...].reshape(width, cols))
@@ -658,11 +686,10 @@
         grad[t, :, cols // 2 :] = (grad_act * silu).astype(LOW)
         return carry
 
-    if follows:
-        lax.fori_loop(0, early, functools.partial(tokens, 0), 0)
-        lax.fori_loop(early, count, functools.partial(tokens, early), 0)
-    else:
-        lax.fori_loop(0, count, functools.partial(tokens, 0), 0)
+    lax.fori_loop(0, count, tokens, 0)
+
+    def ask(source, t, slot):
+        return load(source.at[t], before.at[slot], before_sems.at[slot])
 
     all_act = act[...].reshape(count * block, cols // 2)
     for k in range(4):
@@ -678,6 +705,35 @@
         link.send(rows.at[k], term.at[pl.ds(me * group, group), 2], {"seq": k}) for k in others
     ]
     term[pl.ds(me * group, group), 2] = rows[me]
+    if follows:
+        order = (7, 5, 6, 3, 4, 1, 2, 0)
+        asked = ask(out_before, order[0], 0)
+        halved = {}
+        for number, t in enumerate(order):
+            ready = asked
+            if number + 1 < count:
+                asked = ask(out_before, order[number + 1], (number + 1) % 2)
+            value = times_transpose(act[t], down[...])
+            ready.wait()
+            value = value + before[number % 2].astype(F32)
+            if t % 2 == 1:
+                slot = t // 2 % 2
+                if t < 4:
+                    link.release(halved[t + 3])
+                odd[slot] = value.astype(LOW)
+                halved[t - 1] = link.send(odd.at[slot], arrived.at[t // 2], core)
+                continue
+            halved[t].wait_recv()
+            value = value + arrived[t // 2].astype(F32)
+            if t == 0:
+                total[...] += value
+            else:
+                held[t // 2 - 1] = value.astype(LOW)
+            if t == 6:
+                turn = link.send(held.at[2], corner, over_y)
+            if t == 4:
+                direct = link.send(held.at[1], from_y, over_y)
+
     all_grad = grad[...].reshape(count * block, cols)
     for z in range(line):
         value = column_product(
@@ -686,55 +742,54 @@
         ).astype(LOW)
         for y in range(2):
             term[z, y] = value[y * owned : (y + 1) * owned, :]
-
-    def ask(t, slot):
-        for place, source in enumerate((out_before, mid_before)):
-            load(source.at[t], before.at[slot, place], before_sems.at[slot, place])
-
+        if follows and z == line - 2:
+            turn.wait_recv()
+            held[0] = (held[0].astype(F32) + corner[...].astype(F32)).astype(LOW)
+            last = link.send(held.at[0], out, over_x)
+
+    targets = {0: mid} if follows else {0: mid, 1: out}
     if follows:
-        ask(0, 0)
+        ask(mid_before, 0, 0)
+
+    def hand_over(t, place):
+        return pltpu.make_async_copy(
+            stage.at[t % 2, place], targets[place].at[t], stage_sems.at[t % 2, place]
+        )
 
     def back(t, carry):
-        slot = t % 2
-
-        def hand_over(t, place, target):
-            return pltpu.make_async_copy(
-                stage.at[t % 2, place], target.at[t], stage_sems.at[t % 2, place]
-            )
-
         @pl.when(t >= 2)
         def _():
-            hand_over(t - 2, 0, out).wait()
-            hand_over(t - 2, 1, mid).wait()
-
-        values = [
-            times_transpose(act[t], down[...]),
-            times_transpose(grad[t], weight[...].reshape(width, cols)),
-        ]
+            for place in targets:
+                hand_over(t - 2, place).wait()
+
+        values = {0: times_transpose(grad[t], weight[...].reshape(width, cols))}
         if follows:
 
             @pl.when(t + 1 < count)
             def _():
-                ask(t + 1, (t + 1) % 2)
-
-            for place, source in enumerate((out_before, mid_before)):
-                pltpu.make_async_copy(
-                    source.at[t], before.at[slot, place], before_sems.at[slot, place]
-                ).wait()
-                values[place] = values[place] + before[slot, place].astype(F32)
-        for place, target in enumerate((out, mid)):
-            stage[slot, place] = values[place].astype(LOW)
-            hand_over(t, place, target).start()
+                ask(mid_before, t + 1, (t + 1) % 2)
+
+            pltpu.make_async_copy(
+                mid_before.at[t], before.at[t % 2], before_sems.at[t % 2]
+            ).wait()
+            values[0] = values[0] + before[t % 2].astype(F32)
+        else:
+            values[1] = times_transpose(act[t], down[...])
+        for place in targets:
+            stage[t % 2, place] = values[place].astype(LOW)
+            hand_over(t, place).start()
         return carry
 
     lax.fori_loop(0, count, back, 0)
     for t in (count - 2, count - 1):
-        for place, target in enumerate((out, mid)):
-            pltpu.make_async_copy(
-                stage.at[t % 2, place], target.at[t], stage_sems.at[t % 2, place]
-            ).wait()
+        for place in targets:
+            hand_over(t, place).wait()
     for copy in sent:
         copy.wait_recv()
+    if follows:
+        direct.wait_recv()
+        last.wait_recv()
+        out[...] = (total[...] + out[...].astype(F32) + from_y[...].astype(F32)).astype(LOW)
     link.finish()
 
 
@@ -745,6 +800,7 @@
     cols = 2 * group * units
     hbm, vmem = (pl.BlockSpec(memory_space=pl.ANY), pl.BlockSpec(memory_space=pltpu.VMEM))
     rows = (4, group, owned, cols)
+    like_mids = jax.ShapeDtypeStruct(mids.shape, LOW)
     low_scratch = [
         mids.shape,
         mids.shape,
@@ -753,30 +809,42 @@
         (width, cols // 2),
         (count, block, cols // 2),
         (count, block, cols),
-        (2, 2, block, width),
-        (2, 2, block, width),
+        (2, 1 if follows else 2, block, width),
+        (2, block, width),
     ]
+    ahead, late_scratch = [], []
+    if follows:
+        for size in (2, 4, 3):
+            low_scratch.append((size, block, width))
+        low_scratch += [(block, width)] * 2
+        ahead = [jax.ShapeDtypeStruct((count, block, cols), F32)]
+        late_scratch = [
+            pltpu.VMEM((block, width), F32),
+            pltpu.VMEM((2, block, cols), F32),
+            pltpu.SemaphoreType.DMA((3,)),
+        ]
     return pl.pallas_call(
         functools.partial(cut_kernel, (follows, group, units)),
         out_shape=[
             jax.ShapeDtypeStruct((line, 3, owned, cols), LOW),
-            jax.ShapeDtypeStruct(mids.shape, LOW),
-            jax.ShapeDtypeStruct(mids.shape, LOW),
+            jax.ShapeDtypeStruct((block, width), LOW) if follows else like_mids,
+            like_mids,
+            *ahead,
         ],
         in_specs=[hbm] * len(args),
-        out_specs=[vmem, hbm, hbm],
+        out_specs=[vmem, vmem if follows else hbm, hbm] + [hbm] * len(ahead),
         scratch_shapes=[pltpu.VMEM(shape, LOW) for shape in low_scratch]
+        + late_scratch
         + [
-            pltpu.VMEM((count // 2 if follows else 1, block, cols), F32),
             pltpu.SemaphoreType.DMA((2, count)),
             pltpu.SemaphoreType.DMA((line + 1,)),
             pltpu.SemaphoreType.DMA((2, 2)),
-            pltpu.SemaphoreType.DMA((2, 2)),
-            pltpu.SemaphoreType.DMA((6,)),
-            pltpu.SemaphoreType.DMA((6,)),
+            pltpu.SemaphoreType.DMA((2,)),
+            pltpu.SemaphoreType.DMA((16,)),
+            pltpu.SemaphoreType.DMA((16,)),
         ],
         compiler_params=pltpu.CompilerParams(
-            collective_id=4 if follows else 3, has_side_effects=True, vmem_limit_bytes=58 << 20
+            collective_id=4 if follows else 3, has_side_effects=True, vmem_limit_bytes=61 << 20
         ),
         cost_estimate=pl.CostEstimate(
             flops=50_000_000_000, bytes_accessed=40_000_000, transcendentals=2_000_000
@@ -821,88 +889,33 @@
     yield
 
 
-def output_kernel(
-    terms_in,
-    hidden,
-    ff_sum,
-    _,
-    block_out,
-    hidden_blocks,
-    down_blocks,
-    terms,
-    arrived,
-    held,
-    from_x,
-    from_y,
-    corner,
-    send_sems,
-    recv_sems,
-    load_sems,
-    local_sems,
-):
+def spread_kernel(ff_sum, _, hidden_blocks, down_blocks, send_sems, recv_sems, local_sems):
     _, ids = neighbours()
-    core, over_x, over_y = ids
-    pair = lax.axis_index("fsdp") % 2
     greet(ids)
     link = Sender(send_sems, recv_sems)
-    order = (7, 6, 5, 4, 3, 2, 1, 0)
-    loads = {k: pltpu.make_async_copy(terms_in.at[k], terms.at[k], load_sems.at[k]) for k in order}
-    for k in order:
-        loads[k].start()
-    spread = spread_blocks(link, ids, pair, ff_sum, hidden_blocks, down_blocks, local_sems)
-    halved = {}
-    for k in (6, 4, 2, 0):
-        loads[k + 1].wait()
-        halved[k] = link.send(terms.at[k + 1], arrived.at[k // 2], core)
-    next(spread)
-
-    def chip_sum(k):
-        loads[k].wait()
-        halved[k].wait_recv()
-        return terms[k].astype(F32) + arrived[k // 2].astype(F32)
-
-    held[0] = chip_sum(6).astype(LOW)
-    turn = link.send(held.at[0], corner, over_y)
-    next(spread)
-    held[1] = chip_sum(4).astype(LOW)
-    direct = link.send(held.at[1], from_y, over_y)
-    total = chip_sum(2)
-    turn.wait_recv()
-    held[2] = (total + corner[...].astype(F32)).astype(LOW)
-    last = link.send(held.at[2], from_x, over_x)
-    next(spread)
-    total = hidden[...] + chip_sum(0)
-    direct.wait_recv()
-    last.wait_recv()
-    total = total + from_x[...].astype(F32) + from_y[...].astype(F32)
-    block_out[...] = total.astype(LOW)
-    next(spread)
-    next(spread)
+    pair = lax.axis_index("fsdp") % 2
+    for _ in spread_blocks(link, ids, pair, ff_sum, hidden_blocks, down_blocks, local_sems):
+        pass
     link.finish()
 
 
-def spread(ff_sum, terms, hidden, earlier):
+def spread(ff_sum, earlier):
     hbm, vmem = (pl.BlockSpec(memory_space=pl.ANY), pl.BlockSpec(memory_space=pltpu.VMEM))
-    shapes = [jax.ShapeDtypeStruct((count, *ff_sum.shape[1:]), LOW) for count in (8, 4)]
-    sems = [pltpu.SemaphoreType.DMA((18,))] * 2
-    block = hidden.shape
     return pl.pallas_call(
-        output_kernel,
-        out_shape=[jax.ShapeDtypeStruct(block, LOW), *shapes],
-        in_specs=[hbm, vmem, vmem, hbm],
-        out_specs=[vmem, hbm, hbm],
-        scratch_shapes=[
-            pltpu.VMEM(shape, LOW)
-            for shape in (terms.shape, (4, *block), (3, *block), block, block, block)
-        ]
-        + [*sems, pltpu.SemaphoreType.DMA((8,)), pltpu.SemaphoreType.DMA((2,))],
+        spread_kernel,
+        out_shape=[
+            jax.ShapeDtypeStruct((count, *ff_sum.shape[1:]), LOW) for count in (8, 4)
+        ],
+        in_specs=[vmem, hbm],
+        out_specs=[hbm] * 2,
+        scratch_shapes=[pltpu.SemaphoreType.DMA((12,))] * 2 + [pltpu.SemaphoreType.DMA((2,))],
         compiler_params=pltpu.CompilerParams(
             collective_id=5, has_side_effects=True, vmem_limit_bytes=58 << 20
         ),
         cost_estimate=pl.CostEstimate(
             flops=50_000_000_000, bytes_accessed=20_000_000, transcendentals=0
         ),
-    )(terms, hidden, ff_sum, earlier)
+    )(ff_sum, earlier)
 
 
 def closing_kernel(
@@ -1446,8 +1459,8 @@
     first_term, out_first, mid_first = cut_call(
         False, (mids, cots, first_all, first_rows), (group, line, owned, spans[0])
     )
-    second_term, out, grad_mid = cut_call(
-        True, (mids, cots, second_all, out_first, mid_first), (group, line, owned, spans[1])
+    second_term, block_out, grad_mid, _ = cut_call(
+        True, (mids, cots, second_all, out_first, mid_first, hidden_in), (group, line, owned, spans[1])
     )
 
     sums = [line_reduce(term) for term in (first_term, second_term)]
@@ -1476,14 +1489,15 @@
         (owned, vector_rows, qkv_weight.shape[1], per_dev, group, line),
     )
     places_here = jnp.stack([place, lax.axis_index("fsdp") % 2]).astype(jnp.int32)
-    attn_term = attn_term + nought(sums[1][0, 0, 0])
+    corner = attn_term[:1, :16, :HD] + nought(sums[1][0, 0, 0])
+    attn_term = lax.dynamic_update_slice(attn_term, corner, (0, 0, 0))
     attn_sum = line_reduce(attn_term)
-    block_out, *second_blocks = spread(sums[1], out, hidden_in, attn_term)
+    second_blocks = spread(sums[1], attn_term)
     hidden_pieces = [first_blocks[0], second_blocks[0]]
     down_pieces = [first_blocks[1], second_blocks[1]]
     down_grad = down_call(places_here, down_pieces, fold)
     gate_up_grad = hidden_call(places_here, hidden_pieces, cuts, group)
-    attn_sums = seq_blocks(attn_sum + nought(block_out[0, 0]))
+    attn_sums = seq_blocks(attn_sum + nought(second_blocks[0][0, 0, 0]))
     proj_grad = columns_call(
         places_here, [jnp.stack([part[:owned, cols:] for part in attn_sums])]
     )

time: 560 us -> 540 us (0.964)
  Pallas kernels: 489 us -> 477 us
  waiting for transfers between devices: 17.8 us -> 8.03 us
    pallas_call x1, Pallas kernels: 59.3 us -> 38.4 us  [spread(): pl.pallas_call(spread_kernel, out_shape=[jax.ShapeDtypeStruct((count, *ff...]
    pallas_call x2, Pallas kernels: 122 us -> 132 us  [cut_call(): pl.pallas_call(functools.partial(cut_kernel, (follows, group, units)), ou...]
    reduce_scatter x3, waiting for transfers between devices: 9.1 us -> 0.06 us  [line_reduce(): lax.psum_scatter(value, 'fsdp', scatter_dimension=0, axis_index_groups=li...]
  transfers between devices with their start and end apart: 7 -> 7, of which waited for: 4 -> 3; matrix products, arithmetic and copies ran while one was open for 0% -> 0% of each run, Pallas kernels for 68% -> 68%
where the time goes in v6:
time: 540 us; the launch traced here: 533 us
  Pallas kernels  477 us (88%)
  local copies, waits for them, and re-layouts  18.6 us (3%)
  between operations  15.9 us (3%)
  other arithmetic  10.9 us (2%)
  waiting for transfers between devices  8.03 us (1%)
    pallas_call x2, Pallas kernels, cut_call(): pl.pallas_call(functools.partial(cut_kernel, (follows, group, units)), ou...  132 us
    pallas_call x1, Pallas kernels, closing(): pl.pallas_call(functools.partial(closing_kernel, (owned, per_dev, group))...  122 us
    pallas_call x1, Pallas kernels, opening(): pl.pallas_call(functools.partial(opening_kernel, (owned, vector_size, per...  112 us
    pallas_call x1, Pallas kernels, middle(): pl.pallas_call(middle_kernel, out_shape=[jax.ShapeDtypeStruct(block, F32)...  57.5 us
    pallas_call x1, Pallas kernels, spread(): pl.pallas_call(spread_kernel, out_shape=[jax.ShapeDtypeStruct((count, *ff...  38.4 us
  transfers between devices with their start and end apart: 7, of which 3 were waited for; matrix products, arithmetic and copies ran while one was open for 0% of the time, Pallas kernels for 68%

profile of v6, /device:TPU:0, one launch (start us, length us, event | category | flops | bytes accessed | tf_op | source)
XLA Modules:
  0.0 533.1 jit_solution(6731351712997393593)
XLA Ops:
  7.3 1.0 copy-done
  9.2 1.0 constant_dynamic-slice_fusion
  10.2 1.1 dynamic-slice.1
  11.8 1.6 constant_dynamic-slice_fusion.9.proj
  13.4 1.0 copy.24.seg_col
  15.0 1.7 constant_dynamic-slice_fusion.4
  17.0 1.0 pad_maximum_fusion.second_own
  18.1 1.6 constant_dynamic-slice_fusion.8
  19.8 1.0 pad_maximum_fusion.1.ff_own
  20.8 0.9 pad_maximum_fusion.3.second_down
  21.7 0.8 pad_maximum_fusion.4.ff_down
  23.2 111.9 %shard_map.169 = (f32[1024,128]{1,0:T(8,128)}, f32[1024,128]{1,0:T(8,128)}, bf16[4,256,1536]{2,1,0:T(8,128)(2,1)}, bf16[1536,512]{1,0:T(8,128)(2,1)}, f32[3,2048...) custom-call(bf16[256,1536]{1,0:T(8,128)(2,1)} %bitcast.41, ...), custom_call_target="tpu_custom_call" | custom-call | flops 99999997952 | bytes 40000000 | tf_op jit(solution)/shard_map/pallas_call | solution.py:510
  135.4 57.5 %shard_map.170 = (f32[256,1536]{1,0:T(8,128)}, bf16[8,256,1536]{2,1,0:T(8,128)(2,1)}) custom-call(bf16[4,256,1536]{2,1,0:T(8,128)(2,1)} %get-tuple-element.40.part, bf16[256,1536]{1,0:T(8,128)(2,1)} %bitcast.42, f32[3,2048]{1,0:T(4,128)} %get-tuple-element.41.vectors), custom_call_target="tpu_custom_call" | custom-call | tf_op jit(solution)/shard_map/pallas_call | solution.py:566
  193.0 45.5 %shard_map.171 = (bf16[4,3,192,1024]{3,2,1,0:T(8,128)(2,1)}, bf16[8,256,1536]{2,1,0:T(8,128)(2,1)}, bf16[8,256,1536]{2,1,0:T(8,128)(2,1)}) custom-call(bf16[8,256,1536]{2,1,0:T(8,128)(2,1)} %get-tuple-element.42.refs_0_, bf16[8,256,1536]{2,1,0:T(8,128)(2,1)} %get-tuple-element.43.refs_1_, bf16[4,2,192,1024]{3,2,1,0:T(8,128)(2,1)} %get-tuple-element.45.refs_2_, ...), custom_call_target="tpu_custom_call" | custom-call | flops 49999998976 | bytes 40000000 | tf_op jit(solution)/shard_map/pallas_call | solution.py:826
  238.5 7.0 %all-gather.3.cloned.1.call-done = bf16[12,192,1216]{2,1,0:T(8,128)(2,1)} async-done(((bf16[3,192,1216]{2,1,0:T(8,128)(2,1)}), bf16[12,192,1216]{2,1,0:T(8,128)(2,1)}) %all-gather.3.cloned.1.call-update) | async-done | bytes 5603344 | tf_op jit(solution)/shard_map/all_gather | solution.py:65
  245.6 86.3 %shard_map.172 = (bf16[4,3,192,1216]{3,2,1,0:T(8,128)(2,1)}, bf16[256,1536]{1,0:T(8,128)(2,1)}, bf16[8,256,1536]{2,1,0:T(8,128)(2,1)}, f32[8,256,1216]{2,1,0:T(8,128)}) custom-call(bf16[8,256,1536]{2,1,0:T(8,128)(2,1)} %get-tuple-element.42.refs_0_, bf16[8,256,1536]{2,1,0:T(8,128)(2,1)} %get-tuple-element.43.refs_1_, bf16[4,3,192,1216]{3,2,1,0:T(8,128)(2,1)} %bitcast.46, ...), custom_call_target="tpu_custom_call" | custom-call | flops 49999998976 | bytes 40000000 | tf_op jit(solution)/shard_map/pallas_call | solution.py:826
  332.2 121.7 %shard_map.173 = (f32[256,1536]{1,0:T(8,128)}, f32[2,1536]{1,0:T(2,128)}, bf16[4,208,896]{2,1,0:T(8,128)(2,1)}, bf16[8,192,1024]{2,1,0:T(8,128)(2,1)}, bf16[4,192,1024]{2,1,0:T(8,128)(2,1)}) custom-call(bf16[8,256,1536]{2,1,0:T(8,128)(2,1)} %get-tuple-element.51.terms_in, f32[256,1536]{1,0:T(8,128)} %get-tuple-element.49.refs_5_.hidden, ...), custom_call_target="tpu_custom_call" | custom-call | flops 99999997952 | bytes 40000000 | tf_op jit(solution)/shard_map/pallas_call | solution.py:1216
  453.9 1.2 slice.132
  455.8 1.2 add_dynamic-update-slice_fusion._
  457.0 38.4 %shard_map.174 = (bf16[8,192,1216]{2,1,0:T(8,128)(2,1)}, bf16[4,192,1216]{2,1,0:T(8,128)(2,1)}) custom-call(bf16[3,192,1216]{2,1,0:T(8,128)(2,1)} %bitcast.48, bf16[4,208,896]{2,1,0:T(8,128)(2,1)} %add_dynamic-update-slice_fusion._), custom_call_target="tpu_custom_call" | custom-call | flops 49999998976 | bytes 20000000 | tf_op jit(solution)/shard_map/pallas_call | solution.py:904
  495.5 1.2 slice.104
  497.3 1.0 add_bitcast_fusion
  498.4 1.2 collective-permute-start
  499.6 2.1 copy-done.2
  501.7 8.4 %shard_map.176 = f32[192,17920]{1,0:T(8,128)} custom-call(s32[2]{0:T(128)S(1)} %pad_add_fusion.place, bf16[8,192,1024]{2,1,0:T(8,128)(2,1)S(1)} %copy-done.3, bf16[8,192,1216]{2,1,0:T(8,128)(2,1)S(1)} %copy-done.2), custom_call_target="tpu_custom_call" | custom-call | tf_op jit(solution)/shard_map/pallas_call | solution.py:1340
  510.1 5.9 %shard_map.177 = f32[1120,1536]{1,0:T(8,128)} custom-call(s32[2]{0:T(128)S(1)} %pad_add_fusion.place, bf16[4,192,1024]{2,1,0:T(8,128)(2,1)S(1)} %copy-done.5, bf16[4,192,1216]{2,1,0:T(8,128)(2,1)S(1)} %copy-done.4), custom_call_target="tpu_custom_call" | custom-call | tf_op jit(solution)/shard_map/pallas_call | solution.py:1304
  516.7 0.9 slice_bitcast_fusion.1
  518.5 1.0 broadcast_select_fusion.7
  520.9 1.6 shard_map.175
  522.8 1.3 convert_element_type.21
  524.1 0.9 copy.40
  525.0 1.1 copy.41
  (62 shorter events, 6.9 us)
Async XLA Ops:
  7.2 1.1 copy-start
  7.2 6.2 %copy-start.8 = (s32[1,1024]{1,0:T(1,128)S(1)}, s32[1,1024]{1,0:T(1,128)}, u32[]{:S(2)}) copy-start(s32[1,1024]{1,0:T(1,128)} %seg_row.3) | copy-start | bytes 12292
  7.2 238.4 %all-gather.3.cloned.1.call-start = ((), (), s32[]{:S(2)}) async-start(), calls=%async_computation.6 | async-start | bytes 7372800 | tf_op jit(solution)/shard_map/all_gather | solution.py:65
  135.1 197.0 %reduce-scatter.4.cloned.1.call-start = ((), (), s32[]{:S(2)}) async-start(), calls=%async_computation.3 | async-start | bytes 5898240 | tf_op jit(solution)/shard_map/reduce_scatter | solution.py:69
  238.5 215.4 %reduce-scatter.6.cloned.1.call-start = ((), (), s32[]{:S(2)}) async-start(), calls=%async_computation.4 | async-start | bytes 7372800 | tf_op jit(solution)/shard_map/reduce_scatter | solution.py:69
  331.9 165.4 %reduce-scatter.8.cloned.1.call-start = ((), (), s32[]{:S(2)}) async-start(), calls=%async_computation.5 | async-start | bytes 1863680 | tf_op jit(solution)/shard_map/reduce_scatter | solution.py:69
  457.0 42.6 %copy-start.3 = (bf16[8,192,1024]{2,1,0:T(8,128)(2,1)S(1)}, bf16[8,192,1024]{2,1,0:T(8,128)(2,1)}, u32[]{:S(2)}) copy-start(bf16[8,192,1024]{2,1,0:T(8,128)(2,1)} %get-tuple-element.68.refs_0_) | copy-start | bytes 9437188
  498.4 17.8 %collective-permute-start = (bf16[208,896]{1,0:T(8,128)(2,1)S(1)}, bf16[208,896]{1,0:T(8,128)(2,1)}, u32[]{:S(2)}, u32[]{:S(2)}) collective-permute-start(bf16[208,896]{1,0:T(8,128)(2,1)S(1)} %add_bitcast_fusion), channel_id=1, source_target_pairs={{0,16},{8,24},{16,0},{24,8},{1,17},{9,25},{17,1},{25,9},{2,18},{10... | collective-permute-start | bytes 1118216 | tf_op jit(solution)/shard_map/ppermute | solution.py:56
  499.6 2.1 copy-start.2
  501.7 8.4 %copy-start.4 = (bf16[4,192,1216]{2,1,0:T(8,128)(2,1)S(1)}, bf16[4,192,1216]{2,1,0:T(8,128)(2,1)}, u32[]{:S(2)}) copy-start(bf16[4,192,1216]{2,1,0:T(8,128)(2,1)} %get-tuple-element.70.refs_1_) | copy-start | bytes 5603332
  501.7 8.4 %copy-start.5 = (bf16[4,192,1024]{2,1,0:T(8,128)(2,1)S(1)}, bf16[4,192,1024]{2,1,0:T(8,128)(2,1)}, u32[]{:S(2)}) copy-start(bf16[4,192,1024]{2,1,0:T(8,128)(2,1)} %get-tuple-element.69.refs_0_) | copy-start | bytes 4718596
  516.1 1.7 collective-permute-start.2
  516.2 2.3 collective-permute-start.1
  520.8 3.3 copy-start.7
  520.9 4.1 copy-start.6
  522.7 3.4 copy-start.1
Sparse Core Ops, SparseCore 0:
  135.3 110.2 all-gather.2
  247.9 83.5 reduce-scatter.3
  333.8 104.8 reduce-scatter.5
  457.2 33.9 reduce-scatter.7

commit v7 on v6

--- a/solution.py
+++ b/solution.py
@@ -918,8 +918,21 @@
     )(ff_sum, earlier)
 
 
-def closing_kernel(
+def closing_kernel(shape, late, *refs):
+    count = 18
+    given, places, sems = list(refs[:count]), refs[-len(late) - 1 : -1], refs[-1]
+    late_loads = []
+    for number, place in zip(late, places):
+        late_loads.append(
+            pltpu.make_async_copy(given[number], place, sems.at[len(late_loads)])
+        )
+        given[number] = place
+    closing_body(shape, late_loads, *given, *refs[count : -len(late) - 1])
+
+
+def closing_body(
     shape,
+    late_loads,
     terms_in,
     hidden,
     upstream,
@@ -992,7 +1005,7 @@
         pltpu.make_async_copy(source, target, load_sems.at[8 + number])
         for number, (source, target) in enumerate(((tokens_in, tokens_all), (normed_in, normed)))
     ]
-    for copy in kept_loads:
+    for copy in (*kept_loads, *late_loads):
         copy.start()
     halved = {}
     for k in (6, 2, 4, 0):
@@ -1029,14 +1042,15 @@
     upper[me] = total.astype(LOW)
     last = [link.send(upper.at[me], upper.at[me], core)]
     to_x = [link.send(upper.at[me, half], upper.at[me, half], over_x) for half in (low, high)]
-    for copy, half in zip(to_x, (low, high)):
-        copy.wait_recv()
-        last.append(link.send(upper.at[across, half], upper.at[across, half], core))
-    for copy in last:
-        copy.wait_recv()
-
-    head_rows = per_dev * HD
-    for block in range(seq_count):
+    last[0].wait_recv()
+    for copy in late_loads:
+        copy.wait()
+    head_rows, cols = per_dev * HD, weight.shape[1]
+    scale = HD ** (-0.5)
+    grad_keys[...] = jnp.zeros_like(grad_keys)
+    grad_values[...] = jnp.zeros_like(grad_values)
+
+    def attend_back(block):
         grad_heads[block * rows : (block + 1) * rows, :] = sum(
             times_transpose(
                 upper[block, :, k * quarter : (k + 1) * quarter],
@@ -1044,29 +1058,6 @@
             )
             for k in range(seq_count)
         ).astype(LOW)
-    for k in range(seq_count):
-        term = sum(
-            column_product(
-                merged[block * rows : (block + 1) * rows, :],
-                upper[block, :, k * quarter : (k + 1) * quarter],
-            )
-            for block in range(seq_count)
-        ).astype(LOW)
-        for member in range(group):
-            for y in range(2):
-                first = (2 * member + y) * owned
-                proj_part[y, k, member] = term[first : first + owned, :]
-    proj_over = link.send(proj_part.at[1 - pair], proj_in, over_y)
-    spread = spread_blocks(
-        link, (core, over_x, over_y), pair, ff_sum, hidden_blocks, down_blocks, local_sems
-    )
-    next(spread)
-    next(spread)
-
-    grad_keys[...] = jnp.zeros_like(grad_keys)
-    grad_values[...] = jnp.zeros_like(grad_values)
-    scale = HD ** (-0.5)
-    for block in range(seq_count):
         here, last_key = pl.ds(block * rows, rows), (block + 1) * rows
         row_index = block * rows + lax.broadcasted_iota(jnp.int32, (rows, last_key), 0)
         key_index = lax.broadcasted_iota(jnp.int32, (rows, last_key), 1)
@@ -1082,6 +1073,36 @@
             grad_queries[head, here, :] = (dot(grad_scores, keys[:last_key, :]) * scale).astype(LOW)
             grad_keys[:last_key, :] += column_product(grad_scores, query)
             grad_values[:last_key, :] += column_product(probs.astype(LOW), upper_head)
+
+    here_first = [block // 2 == me // 2 for block in range(seq_count)]
+    for block in range(seq_count):
+        pl.when(here_first[block])(functools.partial(attend_back, block))
+    for copy, half in zip(to_x, (low, high)):
+        copy.wait_recv()
+        last.append(link.send(upper.at[across, half], upper.at[across, half], core))
+    for copy in last[1:]:
+        copy.wait_recv()
+    spread = spread_blocks(
+        link, (core, over_x, over_y), pair, ff_sum, hidden_blocks, down_blocks, local_sems
+    )
+    next(spread)
+    next(spread)
+    for block in range(seq_count):
+        pl.when(jnp.logical_not(here_first[block]))(functools.partial(attend_back, block))
+
+    for k in range(seq_count):
+        term = sum(
+            column_product(
+                merged[block * rows : (block + 1) * rows, :],
+                upper[block, :, k * quarter : (k + 1) * quarter],
+            )
+            for block in range(seq_count)
+        ).astype(LOW)
+        for member in range(group):
+            for y in range(2):
+                first = (2 * member + y) * owned
+                proj_part[y, k, member] = term[first : first + owned, :]
+    proj_over = link.send(proj_part.at[1 - pair], proj_in, over_y)
     next(spread)
     for copy in kept_loads:
         copy.wait()
@@ -1091,17 +1112,6 @@
     kv[0] = jnp.where(holds_values, key_copy, value_copy)
     swapped = link.send(kv.at[0], kv.at[1], core)
     grad_keys[...] = jnp.where(holds_values, value_copy, key_copy).astype(F32)
-    proj_over.wait_recv()
-    proj_half[...] = (proj_part[pair].astype(F32) + proj_in[...].astype(F32)).astype(LOW)
-    cols = weight.shape[1]
-
-    def proj_place(device):
-        return (pl.ds(device * group, group), pl.ds(0, owned), pl.ds(cols, quarter))
-
-    last = [
-        link.send(proj_half.at[k], attn_sum.at[proj_place(me)], {"seq": k}) for k in others
-    ]
-    attn_sum[proj_place(me)] = proj_half[me]
     swapped.wait_recv()
     grad_kv = grad_keys[...] + kv[1].astype(F32)
 
@@ -1135,6 +1145,16 @@
     link.release(direct_x, second_x)
     held[0] = (arrived[across].astype(F32) + late[0].astype(F32)).astype(LOW)
     third = link.send(held.at[0], late_x, over_x)
+    proj_over.wait_recv()
+    proj_half[...] = (proj_part[pair].astype(F32) + proj_in[...].astype(F32)).astype(LOW)
+
+    def proj_place(device):
+        return (pl.ds(device * group, group), pl.ds(0, owned), pl.ds(cols, quarter))
+
+    last = [
+        link.send(proj_half.at[k], attn_sum.at[proj_place(me)], {"seq": k}) for k in others
+    ]
+    attn_sum[proj_place(me)] = proj_half[me]
     kv_first = (H + KV * (me % 2) + me // 2) * HD
     bias_row[0:1, pl.ds(pl.multiple_of(me * head_rows, HD), head_rows)] = bias_parts[:, :head_rows]
     bias_row[0:1, pl.ds(pl.multiple_of(kv_first, HD), HD)] = bias_parts[:, head_rows:]
@@ -1213,11 +1233,12 @@
         (4 * rows, per_dev * HD),
         (per_dev, *heads),
     ]
+    late = (6, 7, 8, 9, 10, 11, 12, 13, 14, 15, 17)
     return pl.pallas_call(
-        functools.partial(closing_kernel, (owned, per_dev, group)),
+        functools.partial(closing_kernel, (owned, per_dev, group), late),
         out_shape=outs,
         in_specs=[
-            pl.BlockSpec(memory_space=pl.ANY if k in (0, 3, 4) else pltpu.VMEM)
+            pl.BlockSpec(memory_space=pl.ANY if k in (0, 3, 4, *late) else pltpu.VMEM)
             for k in range(len(args))
         ],
         out_specs=[pl.BlockSpec(memory_space=pltpu.VMEM)] * (len(outs) - 2)
@@ -1245,7 +1266,9 @@
             )
         ]
         + [pltpu.SemaphoreType.DMA((48,))] * 2
-        + [pltpu.SemaphoreType.DMA((2,)), pltpu.SemaphoreType.DMA((10,))],
+        + [pltpu.SemaphoreType.DMA((2,)), pltpu.SemaphoreType.DMA((10,))]
+        + [pltpu.VMEM(args[k].shape, args[k].dtype) for k in late]
+        + [pltpu.SemaphoreType.DMA((len(late),))],
         compiler_params=pltpu.CompilerParams(
             collective_id=2, has_side_effects=True, vmem_limit_bytes=58 << 20
         ),
@@ -1281,7 +1304,7 @@
     )(place, *pieces)
 
 
-def down_kernel(fold, place, *refs):
+def down_kernel(fold, place, _, *refs):
     *pieces, out = refs
     row = 0
     for piece in pieces:
@@ -1298,17 +1321,17 @@
         row += span
 
 
-def down_call(place, pieces, fold):
+def down_call(place, earlier, pieces, fold):
     rows = sum(piece.shape[2] // fold for piece in pieces)
     width = pieces[0].shape[0] * pieces[0].shape[1] * fold
     return pl.pallas_call(
         functools.partial(down_kernel, fold),
         out_shape=jax.ShapeDtypeStruct((rows, width), F32),
-        in_specs=[pl.BlockSpec(memory_space=pltpu.SMEM)]
+        in_specs=[pl.BlockSpec(memory_space=pltpu.SMEM), pl.BlockSpec(memory_space=pl.ANY)]
         + [pl.BlockSpec(memory_space=pltpu.VMEM)] * len(pieces),
         out_specs=pl.BlockSpec(memory_space=pltpu.VMEM),
         compiler_params=pltpu.CompilerParams(vmem_limit_bytes=40 << 20),
-    )(place, *pieces)
+    )(place, earlier, *pieces)
 
 
 def hidden_kernel(cuts, group, place, *refs):
@@ -1495,9 +1518,9 @@
     second_blocks = spread(sums[1], attn_term)
     hidden_pieces = [first_blocks[0], second_blocks[0]]
     down_pieces = [first_blocks[1], second_blocks[1]]
-    down_grad = down_call(places_here, down_pieces, fold)
     gate_up_grad = hidden_call(places_here, hidden_pieces, cuts, group)
     attn_sums = seq_blocks(attn_sum + nought(second_blocks[0][0, 0, 0]))
+    down_grad = down_call(places_here, attn_sums[2], down_pieces, fold)
     proj_grad = columns_call(
         places_here, [jnp.stack([part[:owned, cols:] for part in attn_sums])]
     )

time: 540 us -> 528 us (0.978)
  Pallas kernels: 477 us -> 466 us
    pallas_call x1, Pallas kernels: 122 us -> 109 us  [closing(): pl.pallas_call(functools.partial(closing_kernel, (owned, per_dev, group),...]
  transfers between devices with their start and end apart: 7 -> 7, of which waited for: 3 -> 1; matrix products, arithmetic and copies ran while one was open for 0% -> 0% of each run, Pallas kernels for 68% -> 68%
where the time goes in v7:
time: 528 us; the launch traced here: 521 us
  Pallas kernels  466 us (88%)
  local copies, waits for them, and re-layouts  18.6 us (4%)
  between operations  15.7 us (3%)
  other arithmetic  11.7 us (2%)
  waiting for transfers between devices  7.2 us (1%)
    pallas_call x2, Pallas kernels, cut_call(): pl.pallas_call(functools.partial(cut_kernel, (follows, group, units)), ou...  132 us
    pallas_call x1, Pallas kernels, opening(): pl.pallas_call(functools.partial(opening_kernel, (owned, vector_size, per...  112 us
    pallas_call x1, Pallas kernels, closing(): pl.pallas_call(functools.partial(closing_kernel, (owned, per_dev, group),...  109 us
    pallas_call x1, Pallas kernels, middle(): pl.pallas_call(middle_kernel, out_shape=[jax.ShapeDtypeStruct(block, F32)...  57.5 us
    pallas_call x1, Pallas kernels, spread(): pl.pallas_call(spread_kernel, out_shape=[jax.ShapeDtypeStruct((count, *ff...  39.2 us
  transfers between devices with their start and end apart: 7, of which 1 were waited for; matrix products, arithmetic and copies ran while one was open for 0% of the time, Pallas kernels for 68%

profile of v7, /device:TPU:0, one launch (start us, length us, event | category | flops | bytes accessed | tf_op | source)
XLA Modules:
  0.0 520.8 jit_solution(2377001708783076774)
XLA Ops:
  7.3 1.0 copy-done
  9.2 1.0 constant_dynamic-slice_fusion
  10.2 1.1 dynamic-slice.1
  11.8 1.6 constant_dynamic-slice_fusion.9.proj
  13.4 1.0 copy.24.seg_col.refs_15_
  15.0 1.7 constant_dynamic-slice_fusion.4
  17.0 1.0 pad_maximum_fusion.second_own
  18.1 1.6 constant_dynamic-slice_fusion.8
  19.8 1.0 pad_maximum_fusion.1.ff_own
  20.8 0.9 pad_maximum_fusion.3.second_down
  21.7 0.8 pad_maximum_fusion.4.ff_down
  23.2 111.9 %shard_map.169 = (f32[1024,128]{1,0:T(8,128)}, f32[1024,128]{1,0:T(8,128)}, bf16[4,256,1536]{2,1,0:T(8,128)(2,1)}, bf16[1536,512]{1,0:T(8,128)(2,1)}, f32[3,2048...) custom-call(bf16[256,1536]{1,0:T(8,128)(2,1)} %bitcast.41, ...), custom_call_target="tpu_custom_call" | custom-call | flops 99999997952 | bytes 40000000 | tf_op jit(solution)/shard_map/pallas_call | solution.py:510
  135.4 57.5 %shard_map.170 = (f32[256,1536]{1,0:T(8,128)}, bf16[8,256,1536]{2,1,0:T(8,128)(2,1)}) custom-call(bf16[4,256,1536]{2,1,0:T(8,128)(2,1)} %get-tuple-element.40.part, bf16[256,1536]{1,0:T(8,128)(2,1)} %bitcast.42, f32[3,2048]{1,0:T(4,128)} %get-tuple-element.41.vectors.refs_5_), custom_call_target="tpu_custom_call" | custom-call | tf_op jit(solution)/shard_map/pallas_call | solution.py:566
  192.9 45.5 %shard_map.171 = (bf16[4,3,192,1024]{3,2,1,0:T(8,128)(2,1)}, bf16[8,256,1536]{2,1,0:T(8,128)(2,1)}, bf16[8,256,1536]{2,1,0:T(8,128)(2,1)}) custom-call(bf16[8,256,1536]{2,1,0:T(8,128)(2,1)} %get-tuple-element.42.refs_0_, bf16[8,256,1536]{2,1,0:T(8,128)(2,1)} %get-tuple-element.43.refs_1_, bf16[4,2,192,1024]{3,2,1,0:T(8,128)(2,1)} %get-tuple-element.45.refs_2_, ...), custom_call_target="tpu_custom_call" | custom-call | flops 49999998976 | bytes 40000000 | tf_op jit(solution)/shard_map/pallas_call | solution.py:826
  238.5 7.1 %all-gather.3.cloned.1.call-done = bf16[12,192,1216]{2,1,0:T(8,128)(2,1)} async-done(((bf16[3,192,1216]{2,1,0:T(8,128)(2,1)}), bf16[12,192,1216]{2,1,0:T(8,128)(2,1)}) %all-gather.3.cloned.1.call-update) | async-done | bytes 5603344 | tf_op jit(solution)/shard_map/all_gather | solution.py:65
  245.6 86.3 %shard_map.172 = (bf16[4,3,192,1216]{3,2,1,0:T(8,128)(2,1)}, bf16[256,1536]{1,0:T(8,128)(2,1)}, bf16[8,256,1536]{2,1,0:T(8,128)(2,1)}, f32[8,256,1216]{2,1,0:T(8,128)}) custom-call(bf16[8,256,1536]{2,1,0:T(8,128)(2,1)} %get-tuple-element.42.refs_0_, bf16[8,256,1536]{2,1,0:T(8,128)(2,1)} %get-tuple-element.43.refs_1_, bf16[4,3,192,1216]{3,2,1,0:T(8,128)(2,1)} %bitcast.46, ...), custom_call_target="tpu_custom_call" | custom-call | flops 49999998976 | bytes 40000000 | tf_op jit(solution)/shard_map/pallas_call | solution.py:826
  332.0 109.3 %shard_map.173 = (f32[256,1536]{1,0:T(8,128)}, f32[2,1536]{1,0:T(2,128)}, bf16[4,208,896]{2,1,0:T(8,128)(2,1)}, bf16[8,192,1024]{2,1,0:T(8,128)(2,1)}, bf16[4,192,1024]{2,1,0:T(8,128)(2,1)}) custom-call(bf16[8,256,1536]{2,1,0:T(8,128)(2,1)} %get-tuple-element.51.refs_0_, f32[256,1536]{1,0:T(8,128)} %get-tuple-element.49.refs_5_.refs_1_, ...), custom_call_target="tpu_custom_call" | custom-call | flops 99999997952 | bytes 40000000 | tf_op jit(solution)/shard_map/pallas_call | solution.py:1237
  441.3 1.2 slice.132
  443.2 1.2 add_dynamic-update-slice_fusion._
  444.4 39.2 %shard_map.174 = (bf16[8,192,1216]{2,1,0:T(8,128)(2,1)}, bf16[4,192,1216]{2,1,0:T(8,128)(2,1)}) custom-call(bf16[3,192,1216]{2,1,0:T(8,128)(2,1)} %bitcast.48, bf16[4,208,896]{2,1,0:T(8,128)(2,1)} %add_dynamic-update-slice_fusion._), custom_call_target="tpu_custom_call" | custom-call | flops 49999998976 | bytes 20000000 | tf_op jit(solution)/shard_map/pallas_call | solution.py:904
  483.6 1.2 slice.104
  485.5 1.8 add_bitcast_fusion
  487.2 1.1 collective-permute-start
  488.4 2.1 copy-done.2
  490.5 8.4 %shard_map.176 = f32[192,17920]{1,0:T(8,128)} custom-call(s32[2]{0:T(128)S(1)} %pad_add_fusion.place, bf16[8,192,1024]{2,1,0:T(8,128)(2,1)S(1)} %copy-done.3, bf16[8,192,1216]{2,1,0:T(8,128)(2,1)S(1)} %copy-done.2), custom_call_target="tpu_custom_call" | custom-call | tf_op jit(solution)/shard_map/pallas_call | solution.py:1363
  499.0 0.9 slice_bitcast_fusion.3
  500.4 5.9 %shard_map.177 = f32[1120,1536]{1,0:T(8,128)} custom-call(s32[2]{0:T(128)S(1)} %pad_add_fusion.place, bf16[208,896]{1,0:T(8,128)(2,1)S(1)} %collective-permute-done._, bf16[4,192,1024]{2,1,0:T(8,128)(2,1)S(1)} %copy-done.5, bf16[4,192,1216]{2,1,0:T(8,128)(2,1)S(1)} %copy-done.4), custom_call_target="tpu_custom_call" | custom-call | tf_op jit(solution)/shard_map/pallas_call | solution.py:1327
  506.4 1.0 broadcast_select_fusion.7
  508.8 1.6 shard_map.175
  510.7 1.3 convert_element_type.21
  512.0 0.9 copy.40
  512.9 1.1 copy.41
  (62 shorter events, 5.8 us)
Async XLA Ops:
  7.2 1.1 copy-start
  7.2 6.2 %copy-start.8 = (s32[1,1024]{1,0:T(1,128)S(1)}, s32[1,1024]{1,0:T(1,128)}, u32[]{:S(2)}) copy-start(s32[1,1024]{1,0:T(1,128)} %refs_16_.1) | copy-start | bytes 12292
  7.2 238.4 %all-gather.3.cloned.1.call-start = ((), (), s32[]{:S(2)}) async-start(), calls=%async_computation.6 | async-start | bytes 7372800 | tf_op jit(solution)/shard_map/all_gather | solution.py:65
  135.1 196.8 %reduce-scatter.4.cloned.1.call-start = ((), (), s32[]{:S(2)}) async-start(), calls=%async_computation.3 | async-start | bytes 5898240 | tf_op jit(solution)/shard_map/reduce_scatter | solution.py:69
  238.5 202.9 %reduce-scatter.6.cloned.1.call-start = ((), (), s32[]{:S(2)}) async-start(), calls=%async_computation.4 | async-start | bytes 7372800 | tf_op jit(solution)/shard_map/reduce_scatter | solution.py:69
  331.9 153.6 %reduce-scatter.8.cloned.1.call-start = ((), (), s32[]{:S(2)}) async-start(), calls=%async_computation.5 | async-start | bytes 1863680 | tf_op jit(solution)/shard_map/reduce_scatter | solution.py:69
  444.4 44.0 %copy-start.3 = (bf16[8,192,1024]{2,1,0:T(8,128)(2,1)S(1)}, bf16[8,192,1024]{2,1,0:T(8,128)(2,1)}, u32[]{:S(2)}) copy-start(bf16[8,192,1024]{2,1,0:T(8,128)(2,1)} %get-tuple-element.68.refs_0_) | copy-start | bytes 9437188
  487.2 12.7 %collective-permute-start = (bf16[208,896]{1,0:T(8,128)(2,1)}, bf16[208,896]{1,0:T(8,128)(2,1)S(1)}, u32[]{:S(2)}, u32[]{:S(2)}) collective-permute-start(bf16[208,896]{1,0:T(8,128)(2,1)} %add_bitcast_fusion), channel_id=1, source_target_pairs={{0,16},{8,24},{16,0},{24,8},{1,17},{9,25},{17,1},{25,9},{2,18},{10... | collective-permute-start | bytes 1118216 | tf_op jit(solution)/shard_map/ppermute | solution.py:56
  488.4 2.1 copy-start.2
  490.5 9.9 %copy-start.4 = (bf16[4,192,1216]{2,1,0:T(8,128)(2,1)S(1)}, bf16[4,192,1216]{2,1,0:T(8,128)(2,1)}, u32[]{:S(2)}) copy-start(bf16[4,192,1216]{2,1,0:T(8,128)(2,1)} %get-tuple-element.70.refs_1_) | copy-start | bytes 5603332
  490.5 9.9 %copy-start.5 = (bf16[4,192,1024]{2,1,0:T(8,128)(2,1)S(1)}, bf16[4,192,1024]{2,1,0:T(8,128)(2,1)}, u32[]{:S(2)}) copy-start(bf16[4,192,1024]{2,1,0:T(8,128)(2,1)} %get-tuple-element.69.refs_0_) | copy-start | bytes 4718596
  498.9 7.5 %collective-permute-start.2 = (bf16[208,896]{1,0:T(8,128)(2,1)}, bf16[208,896]{1,0:T(8,128)(2,1)S(1)}, u32[]{:S(2)}, u32[]{:S(2)}) collective-permute-start(bf16[208,896]{1,0:T(8,128)(2,1)} %add_bitcast_fusion), channel_id=1, source_target_pairs={{0,8},{8,0},{16,24},{24,16},{1,9},{9,1},{17,25},{25,17},{2,10},{10... | collective-permute-start | bytes 1118216 | tf_op jit(solution)/shard_map/ppermute | solution.py:56
  499.9 6.5 %collective-permute-start.1 = (bf16[208,896]{1,0:T(8,128)(2,1)S(1)}, bf16[208,896]{1,0:T(8,128)(2,1)S(1)}, u32[]{:S(2)}, u32[]{:S(2)}) collective-permute-start(bf16[208,896]{1,0:T(8,128)(2,1)S(1)} %collective-permute-done._), channel_id=1, source_target_pairs={{0,8},{8,0},{16,24},{24,16},{1,9},{9,1},{17,25},{25,17},{2,10},{10... | collective-permute-start | bytes 1118216 | tf_op jit(solution)/shard_map/ppermute | solution.py:56
  508.7 3.3 copy-start.7
  508.8 4.1 copy-start.6
  510.7 3.4 copy-start.1
Sparse Core Ops, SparseCore 0:
  135.3 110.2 all-gather.2
  247.9 83.5 reduce-scatter.3
  333.8 104.8 reduce-scatter.5
  444.5 34.8 reduce-scatter.7
